TPU v7x, 32 devices: a whole 2x2x4 slice. The times are simulated.
32 devices in a mesh: dp: 16 (over z, x, core), tensor: 2 (over y).
Axes of the slice: x: 2, y: 2, z: 4, core: 2. Of those that a mesh axis runs over, the one named last changes fastest.
Arguments:
- features: bfloat16 [65536, 512], P('dp', 'tensor'), may hold values from -6 to 6
- tangents: bfloat16 [3, 65536, 512], P(None, 'dp', 'tensor'), may hold values from -6 to 6
- weight_in: bfloat16 [2, 512, 512], P(None, None, 'tensor'), may hold values from -0.25 to 0.25
- bias_in: float32 [2, 512], P(None, 'tensor'), may hold values from -3 to 3
- weight_out: bfloat16 [2, 512, 512], P(None, 'tensor'), may hold values from -0.25 to 0.25
- bias_out: float32 [2, 512], P(None, 'tensor'), may hold values from -3 to 3
- true_counts: int32 [256], P('dp'), may hold values from 33 to 256, as said below
- cotangent_values: bfloat16 [65536, 512], P('dp', 'tensor'), may hold values from -6 to 6
- cotangent_tangents: bfloat16 [3, 65536, 512], P(None, 'dp', 'tensor'), may hold values from -6 to 6
Outputs:
- values_out: bfloat16 [65536, 512], P('dp', 'tensor')
- tangents_out: bfloat16 [3, 65536, 512], P(None, 'dp', 'tensor')
- values_grad: bfloat16 [65536, 512], P('dp', 'tensor')
- tangents_grad: bfloat16 [3, 65536, 512], P(None, 'dp', 'tensor')
- weight_in_grad: float32 [2, 512, 512], P(None, None, 'tensor')
- bias_in_grad: float32 [2, 512], P(None, 'tensor')
- weight_out_grad: float32 [2, 512, 512], P(None, 'tensor')
- bias_out_grad: float32 [2, 512], P(None, 'tensor')
Inputs may be any that keep to these rules, and one draw needn't show every extreme that they name: `true_counts`: each source has between 33 and 256 live rows; some source is full in every draw.
All inputs are finite; a program needn't handle non-finite values.
Results may differ from a plain program's by a relative error of at most 0.0065.
Values may be sent and summed in bfloat16 or wider, within the bound.
No kernel may reach another device: no remote copies, remote signals or barrier semaphores. Data moves between devices by JAX's collectives and lax.ppermute only.
A program may use at most 448 MiB of HBM per device.

v0:
```python
import math

import jax
import jax.numpy as jnp
from jax import lax
from jax.sharding import PartitionSpec as P

log_two = math.log(2.0)


def shifted(value):
    return jax.nn.softplus(value) - log_two


def lift(gathered, weight, bias):
    pre_act = jnp.einsum("srd,dh->srh", gathered, weight, preferred_element_type=jnp.float32)
    return pre_act.at[0].add(bias)


def activate(pre_act):
    slopes = jax.nn.sigmoid(pre_act[0])
    activated = jnp.concatenate([shifted(pre_act[0])[None], slopes[None] * pre_act[1:]], 0)
    return (activated.astype(jnp.bfloat16), slopes)


def backward_local(gathered, pre_act, grad_gathered, weight, weight_second):
    activated, slopes = activate(pre_act)
    grad_second = jnp.einsum(
        "srh,srd->hd", activated, grad_gathered, preferred_element_type=jnp.float32
    )
    grad_mixed = jnp.einsum(
        "srd,hd->srh", grad_gathered, weight_second, preferred_element_type=jnp.float32
    )
    grad_pre = grad_mixed[0] * slopes + slopes * (1.0 - slopes) * jnp.sum(
        grad_mixed[1:] * pre_act[1:], 0
    )
    grad_stack = jnp.concatenate([grad_pre[None], grad_mixed[1:] * slopes[None]], 0).astype(
        jnp.bfloat16
    )
    grad_first = jnp.einsum("srd,srh->dh", gathered, grad_stack, preferred_element_type=jnp.float32)
    grad_bias = jnp.sum(grad_stack[0].astype(jnp.float32), 0)
    back_term = jnp.einsum("srh,dh->srd", grad_stack, weight, preferred_element_type=jnp.float32)
    return (back_term, grad_first, grad_bias, grad_second)


def local(
    features,
    tangents,
    weight_in,
    bias_in,
    weight_out,
    bias_out,
    true_counts,
    cotangent_values,
    cotangent_tangents,
):
    row_count, half_width = features.shape
    sources = true_counts.shape[0]
    slot_rows = row_count // sources
    live_rows = (
        (lax.broadcasted_iota(jnp.int32, (sources, slot_rows), 1) < true_counts[:, None])
        .reshape(row_count)
        .astype(jnp.float32)
    )
    inputs = jnp.concatenate([features[None], tangents], 0)
    cotangents = jnp.concatenate([cotangent_values[None], cotangent_tangents], 0)
    first_weights, first_bias, second_weights, second_bias = (
        weight_in,
        bias_in,
        weight_out,
        bias_out,
    )
    stream_state = inputs.astype(jnp.float32)
    kept = []
    for block_id in range(2):
        outgoing = stream_state.astype(jnp.bfloat16)
        gathered = lax.all_gather(outgoing, "tensor", axis=2, tiled=True)
        pre_act = lift(gathered, first_weights[block_id], first_bias[block_id])
        activated, slopes = activate(pre_act)
        partial_value = jnp.einsum(
            "srh,hd->srd", activated, second_weights[block_id], preferred_element_type=jnp.float32
        )
        partial_value = lax.psum_scatter(partial_value, "tensor", scatter_dimension=2, tiled=True)
        stream_state = stream_state + partial_value.at[0].add(second_bias[block_id])
        kept.append((gathered, pre_act))
    results = (stream_state * live_rows[None, :, None]).astype(jnp.bfloat16)
    cotangent = cotangents.astype(jnp.float32) * live_rows[None, :, None]
    block_grads = [None, None]
    for block_id in (1, 0):
        gathered, pre_act = kept[block_id]
        low_grad = cotangent.astype(jnp.bfloat16)
        grad_gathered = lax.all_gather(low_grad, "tensor", axis=2, tiled=True)
        back_term, grad_first, grad_bias, grad_second = backward_local(
            gathered, pre_act, grad_gathered, first_weights[block_id], second_weights[block_id]
        )
        grad_out_bias = jnp.sum(cotangent[0], 0)
        back_term = lax.psum_scatter(back_term, "tensor", scatter_dimension=2, tiled=True)
        cotangent = cotangent + back_term
        block_grads[block_id] = (grad_first, grad_bias, grad_second, grad_out_bias)
    stacked = tuple((jnp.stack([block_grads[0][item], block_grads[1][item]]) for item in range(4)))
    grad_first, grad_bias, grad_second, grad_out_bias = lax.psum(stacked, "dp")
    back_out = cotangent.astype(jnp.bfloat16)
    return (
        results[0],
        results[1:],
        back_out[0],
        back_out[1:],
        grad_first,
        grad_bias,
        grad_second,
        grad_out_bias,
    )


def solution(mesh):
    in_specs = (
        P("dp", "tensor"),
        P(None, "dp", "tensor"),
        P(None, None, "tensor"),
        P(None, "tensor"),
        P(None, "tensor", None),
        P(None, "tensor"),
        P("dp"),
        P("dp", "tensor"),
        P(None, "dp", "tensor"),
    )
    out_specs = (
        P("dp", "tensor"),
        P(None, "dp", "tensor"),
        P("dp", "tensor"),
        P(None, "dp", "tensor"),
        P(None, None, "tensor"),
        P(None, "tensor"),
        P(None, "tensor", None),
        P(None, "tensor"),
    )
    return jax.shard_map(local, mesh=mesh, in_specs=in_specs, out_specs=out_specs, check_vma=False)
```

profile of v0, /device:TPU:10, one launch (start us, length us, event | category | flops | bytes accessed | tf_op | source)
XLA Modules:
  0.0 2593.3 jit_solution(1413878566596877833)
XLA Ops:
  7.2 7.4 pad_maximum_fusion
  15.3 199.5 %all-gather.5.cloned.1.call-done = bf16[4,4096,512]{2,1,0:T(8,128)(2,1)} async-done(((bf16[4,4096,256]{2,1,0:T(8,128)(2,1)}), bf16[4,4096,512]{2,1,0:T(8,128)(2,1)}) %all-gather.5.cloned.1.call-update) | async-done | bytes 16777232 | tf_op jit(solution)/shard_map/all_gather | solution.py:77
  214.8 8.1 fusion.37
  233.5 9.9 multiply_convert_fusion.4
  243.5 18.4 fusion.8
  263.4 11.3 convert_multiply_fusion
  275.4 355.5 %reduce-scatter.5.cloned.1.call-done = f32[4,4096,256]{2,1,0:T(8,128)} async-done(((f32[4,4096,512]{2,1,0:T(8,128)}), f32[4,4096,256]{2,1,0:T(8,128)}) %reduce-scatter.5.cloned.1.call-update) | async-done | bytes 16777232 | tf_op jit(solution)/shard_map/reduce_scatter | solution.py:83
  635.4 15.3 fusion
  650.8 180.5 %all-gather.9.cloned.1.call-done = bf16[4,4096,512]{2,1,0:T(8,128)(2,1)} async-done(((bf16[4,4096,256]{2,1,0:T(8,128)(2,1)}), bf16[4,4096,512]{2,1,0:T(8,128)(2,1)}) %all-gather.9.cloned.1.call-update) | async-done | bytes 16777232 | tf_op jit(solution)/shard_map/all_gather | solution.py:92
  831.3 19.8 fusion.27
  851.1 180.5 %all-gather.7.cloned.1.call-done = bf16[4,4096,512]{2,1,0:T(8,128)(2,1)} async-done(((bf16[4,4096,256]{2,1,0:T(8,128)(2,1)}), bf16[4,4096,512]{2,1,0:T(8,128)(2,1)}) %all-gather.7.cloned.1.call-update) | async-done | bytes 16777232 | tf_op jit(solution)/shard_map/all_gather | solution.py:77
  1031.6 16.2 fusion.31
  1047.8 7.0 multiply_reduce_fusion.1
  1054.8 7.7 convert_reduce_fusion
  1062.5 11.6 multiply_convert_fusion.2
  1074.0 19.0 fusion.6
  1094.6 18.8 fusion.4
  1113.5 348.6 %reduce-scatter.7.cloned.1.call-done = f32[4,4096,256]{2,1,0:T(8,128)} async-done(((f32[4,4096,512]{2,1,0:T(8,128)}), f32[4,4096,256]{2,1,0:T(8,128)}) %reduce-scatter.7.cloned.1.call-update) | async-done | bytes 16777232 | tf_op jit(solution)/shard_map/reduce_scatter | solution.py:83
  1466.6 366.6 %reduce-scatter.9.cloned.1.call-done = f32[4,4096,256]{2,1,0:T(8,128)} async-done(((f32[4,4096,512]{2,1,0:T(8,128)}), f32[4,4096,256]{2,1,0:T(8,128)}) %reduce-scatter.9.cloned.1.call-update) | async-done | bytes 16777232 | tf_op jit(solution)/shard_map/reduce_scatter | solution.py:97
  1833.2 32.9 %fusion.59 = (bf16[4,4096,256]{2,1,0:T(8,128)(2,1)}, f32[4,4096,256]{2,1,0:T(8,128)}, bf16[4,4096,256]{2,1,0:T(8,128)(2,1)}) fusion(f32[4,4096,256]{2,1,0:T(8,128)} %reduce-scatter.9.cloned.1.call-done, f32[4096]{0:T(1024)S(1)} %bitcast.83, bf16[3,4096,256]{2,1,0:T(8,128)(2,1)} %param.25, bf16[1,4096,256]{2,1,0:T(8,128)(2,1)} %bitcast.80, ...), kind=kLoop, calls=%fused_computation.96 | loop fusion | flops 46137344 | bytes 100679680 | tf_op jit(solution)/shard_map/convert_element_type | solution.py:91
  1866.4 198.7 %all-gather.11.cloned.1.call-done = bf16[4,4096,512]{2,1,0:T(8,128)(2,1)} async-done(((bf16[4,4096,256]{2,1,0:T(8,128)(2,1)}), bf16[4,4096,512]{2,1,0:T(8,128)(2,1)}) %all-gather.11.cloned.1.call-update) | async-done | bytes 16777232 | tf_op jit(solution)/shard_map/all_gather | solution.py:92
  2065.1 8.2 fusion.33
  2073.3 13.4 multiply_reduce_fusion
  2092.1 19.0 fusion.2
  2114.4 13.5 fusion.22
  2128.0 11.3 fusion.23
  2146.9 21.9 all-reduce
  2168.8 13.2 fusion.21
  2183.1 10.5 fusion.24
  2194.7 285.6 %reduce-scatter.11.cloned.1.call-done = f32[4,4096,256]{2,1,0:T(8,128)} async-done(((f32[4,4096,512]{2,1,0:T(8,128)}), f32[4,4096,256]{2,1,0:T(8,128)}) %reduce-scatter.11.cloned.1.call-update) | async-done | bytes 16777232 | tf_op jit(solution)/shard_map/reduce_scatter | solution.py:97
  2480.3 11.5 add_convert_fusion
  2496.4 85.4 %all-reduce.4.cloned.1.call-done = (f32[2,512,256]{2,1,0:T(8,128)}, f32[2,256,512]{2,1,0:T(8,128)}) async-done(((f32[2,512,256]{2,1,0:T(8,128)}, f32[2,256,512]{2,1,0:T(8,128)}), (f32[2,512,256]{2,1,0:T(8,128)}, f32[2,256,512]{2,1,0:T(8,128)})) %all-reduce.4.cloned.1.call-update) | async-done | bytes 2097168 | tf_op jit(solution)/shard_map/psum | solution.py:101
  (88 shorter events, 52.0 us)
Async XLA Ops:
  7.2 207.6 %all-gather.5.cloned.1.call-start = ((), (), s32[]{:S(2)}) async-start(), calls=%async_computation.4 | async-start | bytes 25165824 | tf_op jit(solution)/shard_map/all_gather | solution.py:77
  14.6 0.7 copy-start.15
  14.6 200.2 %copy-start.9 = (bf16[2,512,256]{2,1,0:T(8,128)(2,1)S(1)}, bf16[2,512,256]{2,1,0:T(8,128)(2,1)}, u32[]{:S(2)}) copy-start(bf16[2,512,256]{2,1,0:T(8,128)(2,1)} %param.19) | copy-start | bytes 1572868
  14.6 616.3 %reduce-scatter.5.cloned.1.call-start = ((), (), s32[]{:S(2)}) async-start(), calls=%async_computation.5 | async-start | bytes 50331648 | tf_op jit(solution)/shard_map/reduce_scatter | solution.py:83
  15.3 207.6 %copy-start.12 = (f32[1,256]{1,0:T(1,128)}, f32[1,256]{1,0:T(1,128)S(1)}, u32[]{:S(2)}) copy-start(f32[1,256]{1,0:T(1,128)S(1)} %get-tuple-element.80) | copy-start | bytes 3076
  222.9 5.8 copy-start
  233.5 9.9 copy-start.4
  233.5 9.9 copy-start.8
  261.8 1.6 copy-start.7
  261.9 569.5 %all-gather.9.cloned.1.call-start = ((), (), s32[]{:S(2)}) async-start(), calls=%async_computation.8 | async-start | bytes 25165824 | tf_op jit(solution)/shard_map/all_gather | solution.py:92
  262.6 12.2 copy-start.10
  274.8 0.7 copy-start.16
  274.8 360.7 %copy-start.2 = (bf16[4096,256]{1,0:T(8,128)(2,1)S(1)}, bf16[4096,256]{1,0:T(8,128)(2,1)}, u32[]{:S(2)}) copy-start(bf16[4096,256]{1,0:T(8,128)(2,1)} %param.17) | copy-start | bytes 6291460
  274.8 756.8 %all-gather.7.cloned.1.call-start = ((), (), s32[]{:S(2)}) async-start(), calls=%async_computation.6 | async-start | bytes 25165824 | tf_op jit(solution)/shard_map/all_gather | solution.py:77
  650.7 811.3 %reduce-scatter.7.cloned.1.call-start = ((), (), s32[]{:S(2)}) async-start(), calls=%async_computation.7 | async-start | bytes 50331648 | tf_op jit(solution)/shard_map/reduce_scatter | solution.py:83
  1031.6 16.2 copy-start.1
  1093.0 1.6 copy-start.6
  1093.1 740.1 %reduce-scatter.9.cloned.1.call-start = ((), (), s32[]{:S(2)}) async-start(), calls=%async_computation.9 | async-start | bytes 50331648 | tf_op jit(solution)/shard_map/reduce_scatter | solution.py:97
  1113.4 719.8 %copy-start.3 = (bf16[4096,256]{1,0:T(8,128)(2,1)S(1)}, bf16[4096,256]{1,0:T(8,128)(2,1)}, u32[]{:S(2)}) copy-start(bf16[4096,256]{1,0:T(8,128)(2,1)} %param.17) | copy-start | bytes 6291460
  1113.4 719.8 %copy-start.11 = (f32[2,2,8,128]{3,1,2,0:T(2,128)S(1)}, f32[2,2,8,128]{3,1,2,0:T(2,128)}, u32[]{:S(2)}) copy-start(f32[2,2,8,128]{3,1,2,0:T(2,128)} %copy-done.10) | copy-start | bytes 49156
  1113.4 951.7 %all-gather.11.cloned.1.call-start = ((), (), s32[]{:S(2)}) async-start(), calls=%async_computation.10 | async-start | bytes 25165824 | tf_op jit(solution)/shard_map/all_gather | solution.py:92
  1866.1 614.1 %reduce-scatter.11.cloned.1.call-start = ((), (), s32[]{:S(2)}) async-start(), calls=%async_computation.11 | async-start | bytes 50331648 | tf_op jit(solution)/shard_map/reduce_scatter | solution.py:97
  2073.3 13.4 copy-start.13
  2111.2 16.8 slice-start.2
  2111.2 470.6 %all-reduce.4.cloned.1.call-start = ((), (), s32[]{:S(2)}) async-start(), calls=%async_computation.12 | async-start | bytes 4194304 | tf_op jit(solution)/shard_map/psum | solution.py:101
  2111.5 16.5 slice-start.3
  2114.4 24.9 slice-start
  2128.0 11.3 slice-start.1
  2139.4 7.6 copy-start.14
  2145.5 37.6 %slice-start.4 = ((s8[6291456]{0:T(1024)(128)(4,1)}), s8[2097152]{0:T(1024)(128)(4,1)S(1)}, s32[]{:S(2)}) async-start(s8[6291456]{0:T(1024)(128)(4,1)} %bitcast.75), calls=%async_computation.17 | async-start | bytes 4194304
  2168.8 14.3 slice-start.5
  2168.8 14.3 copy-start.5
  (1 other events, 0.7 us)
Sparse Core Ops, SparseCore 0:
  14.8 199.9 all-gather.4
  262.0 368.8 reduce-scatter.4
  632.5 198.8 all-gather.8
  832.7 198.8 all-gather.6
  1093.2 368.8 reduce-scatter.6
  1464.2 368.8 reduce-scatter.8
  1866.3 198.8 all-gather.10
  2111.3 368.8 reduce-scatter.10
  2484.5 97.2 all-reduce.3
where the time goes:
time: 2600 us; the launch traced here: 2590 us
  waiting for transfers between devices  2200 us (85%)
  matrix products  176 us (7%)
  other arithmetic  155 us (6%)
    reduce_scatter x2, waiting for transfers between devices, local(): lax.psum_scatter(partial_value, 'tensor', scatter_dimension=2, tiled=True)  704 us
    reduce_scatter x2, waiting for transfers between devices, local(): lax.psum_scatter(back_term, 'tensor', scatter_dimension=2, tiled=True)  652 us
    all_gather x2, waiting for transfers between devices, local(): gathered = lax.all_gather(outgoing, 'tensor', axis=2, tiled=True)  380 us
    all_gather x2, waiting for transfers between devices, local(): grad_gathered = lax.all_gather(low_grad, 'tensor', axis=2, tiled=True)  379 us
    psum x1, waiting for transfers between devices, local(): grad_first, grad_bias, grad_second, grad_out_bias = lax.psum(stacked, 'dp')  85.4 us
  transfers between devices with their start and end apart: 9, of which 9 were waited for; matrix products, arithmetic and copies ran while one was open for 6% of the time, Pallas kernels for 0%

commit v1 on v0

v1 whole, which is shorter than its diff:
```python
import functools
import math

import jax
import jax.numpy as jnp
from jax import lax
from jax.experimental import pallas as pl
from jax.experimental.pallas import tpu as pltpu
from jax.sharding import PartitionSpec as P

LOG_TWO = math.log(2.0)
GROUP = 16
BF16, F32 = jnp.bfloat16, jnp.float32
ANY = pl.BlockSpec(memory_space=pl.ANY)
ON_CHIP = pl.BlockSpec(memory_space=pltpu.VMEM)
MIB = 1 << 20


def aligned(value):
    return pl.multiple_of(value, GROUP)


def make_table(counts, side):
    padded = (counts + GROUP - 1) // GROUP * GROUP
    starts = jnp.cumsum(padded) - padded
    table = jnp.concatenate([starts, padded, counts, side[None]]).astype(jnp.int32)
    return table, jnp.sum(padded)


def run_of(table, sources, slot, source, low, rows):
    start, padded = table[source], table[sources + source]
    first = jnp.maximum(start, low)
    size = jnp.maximum(jnp.minimum(start + padded, low + rows) - first, 0)
    return aligned(source * slot + first - start), aligned(first - low), aligned(size)


def each_run(table, sources, slot, low, rows, visit):
    def step(source, carry):
        row, place, size = run_of(table, sources, slot, source, low, rows)

        @pl.when(size > 0)
        def _():
            visit(source, row, place, size)

        return carry

    lax.fori_loop(0, sources, step, 0)


def start_and_wait(moves):
    for wait in (False, True):
        for table, sources, slot, low, rows, copies in moves:

            def visit(source, row, place, size, copies=copies):
                for copy in copies(source, row, place, size):
                    copy.wait() if wait else copy.start()

            each_run(table, sources, slot, low, rows, visit)


def pack_kernel(sources, slot, base, rows, table, values, tangents, keep, send, sems):
    side = table[3 * sources]

    def move(which, target, low):
        def copies(source, row, place, size):
            return (
                pltpu.make_async_copy(
                    values.at[pl.ds(row, size)], target.at[0, pl.ds(place, size)], sems.at[which, 0, source]
                ),
                pltpu.make_async_copy(
                    tangents.at[:, pl.ds(row, size)],
                    target.at[pl.ds(1, 3), pl.ds(place, size)],
                    sems.at[which, 1, source],
                ),
            )

        return (table, sources, slot, low, rows, copies)

    start_and_wait(
        [move(0, send, base + (1 - side) * rows), move(1, keep, base + side * rows)]
    )


def pack(table, values, tangents, base, rows, sources):
    half = values.shape[1]
    shape = jax.ShapeDtypeStruct((4, rows, half), BF16)
    return pl.pallas_call(
        functools.partial(pack_kernel, sources, values.shape[0] // sources, base, rows),
        out_shape=(shape, shape),
        in_specs=[pl.BlockSpec(memory_space=pltpu.SMEM), ANY, ANY],
        out_specs=(ON_CHIP, ON_CHIP),
        scratch_shapes=[pltpu.SemaphoreType.DMA((2, 2, sources))],
        cost_estimate=pl.CostEstimate(flops=0, bytes_accessed=32 * rows * half, transcendentals=0),
        compiler_params=pltpu.CompilerParams(vmem_limit_bytes=40 * MIB),
        name="pack",
    )(table, values, tangents)


def unpack_kernel(sources, slot, base, rows, table, mine, theirs, _v, _t, values, tangents, sems):
    side = table[3 * sources]

    def move(which, origin, low):
        def copies(source, row, place, size):
            return (
                pltpu.make_async_copy(
                    origin.at[0, pl.ds(place, size)], values.at[pl.ds(row, size)], sems.at[which, 0, source]
                ),
                pltpu.make_async_copy(
                    origin.at[pl.ds(1, 3), pl.ds(place, size)],
                    tangents.at[:, pl.ds(row, size)],
                    sems.at[which, 1, source],
                ),
            )

        return (table, sources, slot, low, rows, copies)

    start_and_wait(
        [move(0, theirs, base + (1 - side) * rows), move(1, mine, base + side * rows)]
    )


def unpack(table, mine, theirs, values, tangents, base, rows, sources):
    half = values.shape[1]
    return pl.pallas_call(
        functools.partial(unpack_kernel, sources, values.shape[0] // sources, base, rows),
        out_shape=(
            jax.ShapeDtypeStruct(values.shape, BF16),
            jax.ShapeDtypeStruct(tangents.shape, BF16),
        ),
        in_specs=[pl.BlockSpec(memory_space=pltpu.SMEM), ON_CHIP, ON_CHIP, ANY, ANY],
        out_specs=(ANY, ANY),
        input_output_aliases={3: 0, 4: 1},
        scratch_shapes=[pltpu.SemaphoreType.DMA((2, 2, sources))],
        cost_estimate=pl.CostEstimate(flops=0, bytes_accessed=32 * rows * half, transcendentals=0),
        compiler_params=pltpu.CompilerParams(vmem_limit_bytes=40 * MIB),
        name="unpack",
    )(table, mine, theirs, values, tangents)


def blank_kernel(sources, slot, table, values, tangents, other_values, other_tangents, zeros, sems):
    zeros[...] = jnp.zeros_like(zeros)

    for wait in (False, True):

        def step(source, carry, wait=wait):
            padded = table[sources + source]
            size = aligned(slot - padded)
            row = aligned(source * slot + padded)

            @pl.when(size > 0)
            def _():
                for place, (low, high) in enumerate(
                    ((values, tangents), (other_values, other_tangents))
                ):
                    for copy in (
                        pltpu.make_async_copy(
                            zeros.at[0, pl.ds(0, size)], low.at[pl.ds(row, size)], sems.at[place, 0, source]
                        ),
                        pltpu.make_async_copy(
                            zeros.at[:, pl.ds(0, size)], high.at[:, pl.ds(row, size)], sems.at[place, 1, source]
                        ),
                    ):
                        copy.wait() if wait else copy.start()

            return carry

        lax.fori_loop(0, sources, step, 0)


def blank(table, row_count, half, sources):
    slot = row_count // sources
    values = jax.ShapeDtypeStruct((row_count, half), BF16)
    tangents = jax.ShapeDtypeStruct((3, row_count, half), BF16)
    return pl.pallas_call(
        functools.partial(blank_kernel, sources, slot),
        out_shape=(values, tangents, values, tangents),
        in_specs=[pl.BlockSpec(memory_space=pltpu.SMEM)],
        out_specs=(ANY, ANY, ANY, ANY),
        scratch_shapes=[
            pltpu.VMEM((3, slot, half), BF16),
            pltpu.SemaphoreType.DMA((2, 2, sources)),
        ],
        cost_estimate=pl.CostEstimate(flops=0, bytes_accessed=8 * row_count * half, transcendentals=0),
        name="blank",
    )(table)


NN = (((1,), (0,)), ((), ()))
TN = (((0,), (0,)), ((), ()))


def dot(a, b, dims=NN):
    return lax.dot_general(a, b, dims, preferred_element_type=F32)


def blocks_kernel(
    sources,
    base,
    rows,
    tile,
    first,
    table,
    x_own,
    x_got,
    g_own,
    g_got,
    w_in,
    w_out,
    w_in_t,
    w_out_t,
    b_in,
    b_out,
    *rest,
):
    if first:
        grads_before = bias_before = None
    else:
        grads_before, bias_before, *rest = rest
    (y_own, y_send, d_own, d_send, grads, biases, x_low, acts, slopes, lin) = rest
    step = pl.program_id(0)
    side = table[3 * sources]
    wide = w_in.shape[1]
    half = wide // 2
    flat = 4 * tile

    @pl.when(step == 0)
    def _():
        if first:
            grads[...] = jnp.zeros_like(grads)
            biases[...] = jnp.zeros_like(biases)
        else:
            grads[...] = grads_before[...]
            biases[...] = bias_before[...]

    packed = base + side * rows + step * tile + lax.broadcasted_iota(jnp.int32, (tile, 128), 0)
    live = jnp.zeros((tile, 128), F32)
    for source in range(sources):
        start, count = table[source], table[2 * sources + source]
        live = jnp.where((packed >= start) & (packed < start + count), 1.0, live)
    live = jnp.concatenate([live] * (wide // 128), axis=1)
    is_live = live > 0.0

    def load(own, got, stream):
        own, got = own[stream].astype(F32), got[stream].astype(F32)
        left = jnp.where(side == 0, own, got)
        right = jnp.where(side == 0, got, own)
        return jnp.where(is_live, jnp.concatenate([left, right], axis=1), 0.0)

    def store(own, send, stream, value):
        left, right = value[:, :half].astype(BF16), value[:, half:].astype(BF16)
        own[stream] = jnp.where(side == 0, left, right)
        send[stream] = jnp.where(side == 0, right, left)

    def add_grad(place, value):
        rows_in = value.shape[0]
        for part in range(2):
            grads[part, place : place + rows_in, :] += value[:, part * half : (part + 1) * half]

    def add_bias(place, value):
        biases[place] += jnp.sum(value.reshape(tile // 8, 8, wide), axis=0)

    x = [load(x_own, x_got, stream) for stream in range(4)]
    for block in range(2):
        for stream in range(4):
            x_low[block, stream * tile : (stream + 1) * tile] = x[stream].astype(BF16)
        pre = dot(x_low[block], w_in[block])
        z = pre[:tile] + b_in[block][None, :]
        small = jnp.exp(-jnp.abs(z))
        whole = 1.0 / (1.0 + small)
        slope = jnp.where(z >= 0.0, whole, small * whole)
        slopes[block] = slope
        acts[block, :tile] = (jnp.maximum(z, 0.0) + jnp.log1p(small) - LOG_TWO).astype(BF16)
        for stream in range(1, 4):
            part = pre[stream * tile : (stream + 1) * tile]
            lin[block, stream - 1] = part
            acts[block, stream * tile : (stream + 1) * tile] = (slope * part).astype(BF16)
        out = dot(acts[block], w_out[block])
        x = [x[stream] + out[stream * tile : (stream + 1) * tile] for stream in range(4)]
        x[0] = x[0] + b_out[block][None, :]
    for stream in range(4):
        store(y_own, y_send, stream, x[stream] * live)

    g = [load(g_own, g_got, stream) for stream in range(4)]
    for block in (1, 0):
        add_bias(2 + block, g[0])
        g_low = jnp.concatenate([part.astype(BF16) for part in g], axis=0)
        value = dot(acts[block], g_low, TN)
        for part in range(2):
            place = 2 * wide + block * wide + part * half
            grads[0, place : place + half, :] += value[:half, part * half : (part + 1) * half]
            grads[1, place : place + half, :] += value[half:, part * half : (part + 1) * half]
        mixed = dot(g_low, w_out_t[block])
        slope = slopes[block]
        total = jnp.zeros((tile, wide), F32)
        lower = []
        for stream in range(1, 4):
            part = mixed[stream * tile : (stream + 1) * tile]
            total = total + part * lin[block, stream - 1]
            lower.append((part * slope).astype(BF16))
        g_pre = (mixed[:tile] * slope + slope * (1.0 - slope) * total).astype(BF16)
        add_bias(block, g_pre.astype(F32))
        stack = jnp.concatenate([g_pre] + lower, axis=0)
        add_grad(block * wide, dot(x_low[block], stack, TN))
        back = dot(stack, w_in_t[block])
        g = [g[stream] + back[stream * tile : (stream + 1) * tile] for stream in range(4)]
    for stream in range(4):
        store(d_own, d_send, stream, g[stream])


def tile_of(rows):
    best = GROUP
    for tile in range(GROUP, 161, GROUP):
        if rows % tile == 0:
            best = tile
    return best


def run_blocks(table, x_own, x_got, g_own, g_got, weights, biases, sums, base, sources):
    rows, half = x_own.shape[1:]
    wide = 2 * half
    tile = tile_of(rows)
    first = sums is None
    piece = pl.BlockSpec((4, tile, half), lambda i: (0, i, 0))

    def whole(array):
        return pl.BlockSpec(
            array.shape, lambda i, rank=len(array.shape): (0,) * rank, pipeline_mode=pl.Buffered(1)
        )

    sum_shapes = (
        jax.ShapeDtypeStruct((2, 4 * wide, half), F32),
        jax.ShapeDtypeStruct((4, 8, wide), F32),
    )
    out_piece = jax.ShapeDtypeStruct((4, rows, half), BF16)
    extra = () if first else sums
    operands = (table, x_own, x_got, g_own, g_got, *weights, *biases, *extra)
    return pl.pallas_call(
        functools.partial(blocks_kernel, sources, base, rows, tile, first),
        grid=(rows // tile,),
        out_shape=(out_piece,) * 4 + sum_shapes,
        in_specs=[pl.BlockSpec(memory_space=pltpu.SMEM)]
        + [piece] * 4
        + [whole(item) for item in operands[5:]],
        out_specs=[piece] * 4 + [whole(item) for item in sum_shapes],
        input_output_aliases={} if first else {len(operands) - 2: 4, len(operands) - 1: 5},
        scratch_shapes=[
            pltpu.VMEM((2, 4 * tile, wide), BF16),
            pltpu.VMEM((2, 4 * tile, wide), BF16),
            pltpu.VMEM((2, tile, wide), F32),
            pltpu.VMEM((2, 3, tile, wide), F32),
        ],
        cost_estimate=pl.CostEstimate(
            flops=12 * 2 * 4 * rows * wide * wide,
            bytes_accessed=16 * 2 * rows * wide + 16 * wide * wide,
            transcendentals=4 * rows * wide,
        ),
        compiler_params=pltpu.CompilerParams(vmem_limit_bytes=56 * MIB),
        name="blocks",
    )(*operands)


def swap_tensor(value):
    return lax.ppermute(value, "tensor", [(0, 1), (1, 0)])


def swap_bit(value, bit, size):
    return lax.ppermute(value, "dp", [(i, i ^ (1 << bit)) for i in range(size)])


def in_order(flag, mine, other, axis):
    return jnp.where(
        flag == 0, jnp.concatenate([mine, other], axis), jnp.concatenate([other, mine], axis)
    )


def partner_weights_start(weight_in, weight_out, place, size):
    half = weight_in.shape[2]
    flat = jnp.concatenate([weight_in.reshape(-1, half), weight_out.reshape(-1, half)], 0)
    rows = flat.shape[0] // 4
    quarter = (place & 1) * 2 + ((place >> 1) & 1)
    return swap_tensor(lax.dynamic_slice_in_dim(flat, quarter * rows, rows, 0))


def partner_weights_finish(piece, weight_in, weight_out, place, size):
    piece = in_order((place >> 1) & 1, piece, swap_bit(piece, 1, size), 0)
    piece = in_order(place & 1, piece, swap_bit(piece, 0, size), 0)
    rows = weight_in.shape[0] * weight_in.shape[1]
    return piece[:rows].reshape(weight_in.shape), piece[rows:].reshape(weight_out.shape)


def reduce_over_dp(grads, place, size):
    for bit in range(size.bit_length() - 1):
        flag = (place >> bit) & 1
        rows = grads.shape[1] // 2
        kept = lax.dynamic_slice_in_dim(grads, flag * rows, rows, 1)
        sent = lax.dynamic_slice_in_dim(grads, (1 - flag) * rows, rows, 1)
        if bit > 0:
            sent = sent.astype(BF16)
        grads = kept + swap_bit(sent, bit, size).astype(F32)
    return grads


def gather_over_dp(total, place, size):
    for bit in reversed(range(size.bit_length() - 1)):
        total = in_order((place >> bit) & 1, total, swap_bit(total, bit, size), 0)
    return total


def bias_rows(biases, half, size):
    flat = jnp.swapaxes(jnp.sum(biases, 1).reshape(4, 2, half), 0, 1)
    return jnp.pad(flat, ((0, 0), (0, 8 * size - 4), (0, 0)))


def local(
    dp_size,
    features,
    tangents,
    weight_in,
    bias_in,
    weight_out,
    bias_out,
    true_counts,
    cotangent_values,
    cotangent_tangents,
):
    row_count, half = features.shape
    sources = true_counts.shape[0]
    side = lax.axis_index("tensor")
    place = lax.axis_index("dp")
    table, packed_rows = make_table(true_counts, side)
    most = lax.pmax(packed_rows, "dp")
    quarter = partner_weights_start(weight_in, weight_out, place, dp_size)
    bias_pair = jnp.stack([bias_in, bias_out])
    bias_got = swap_tensor(bias_pair)
    unit = row_count // 32
    levels = [unit * k for k in LEVELS]

    def at_level(level):
        first = min(level, (level * 5 // 8 + 127) // 128 * 128)
        chunks = [(0, first)]
        if first < level:
            chunks.append((2 * first, level - first))

        def branch(
            table,
            features,
            tangents,
            weight_in,
            weight_out,
            cotangent_values,
            cotangent_tangents,
            quarter,
            bias_pair,
            bias_got,
        ):
            got_in, got_out = partner_weights_finish(quarter, weight_in, weight_out, place, dp_size)
            w_in = in_order(side, weight_in, got_in, 2)
            w_out = in_order(side, weight_out, got_out, 1)
            weights = (w_in, w_out, jnp.swapaxes(w_in, 1, 2), jnp.swapaxes(w_out, 1, 2))
            b_in, b_out = in_order(side, bias_pair, bias_got, 2)
            outs = blank(table, row_count, half, sources)
            arrived = []
            for base, rows in chunks:
                x_own, x_send = pack(table, features, tangents, base, rows, sources)
                if base > 0:
                    x_send, outs = lax.optimization_barrier((x_send, outs))
                x_got = swap_tensor(x_send)
                g_own, g_send = pack(
                    table, cotangent_values, cotangent_tangents, base, rows, sources
                )
                arrived.append((base, rows, x_own, x_got, g_own, swap_tensor(g_send)))
            sums = None
            results = []
            for base, rows, x_own, x_got, g_own, g_got in arrived:
                y_own, y_send, d_own, d_send, *sums = run_blocks(
                    table, x_own, x_got, g_own, g_got, weights, (b_in, b_out), sums, base, sources
                )
                results.append((base, rows, y_own, y_send, d_own, d_send))
            grads, biases = sums
            grads = jnp.concatenate([grads, bias_rows(biases, half, dp_size)], 1)
            grads = reduce_over_dp(grads, place, dp_size)
            mine = lax.dynamic_index_in_dim(grads, side, 0, keepdims=False)
            other = lax.dynamic_index_in_dim(grads, 1 - side, 0, keepdims=False).astype(BF16)
            values, slants, values_grad, slants_grad = outs
            for base, rows, y_own, y_send, d_own, d_send in results:
                if base > 0 or len(chunks) == 1:
                    other, y_send, d_send = lax.optimization_barrier((other, y_send, d_send))
                y_got = swap_tensor(y_send)
                d_got = swap_tensor(d_send)
                values, slants = unpack(table, y_own, y_got, values, slants, base, rows, sources)
                values_grad, slants_grad = unpack(
                    table, d_own, d_got, values_grad, slants_grad, base, rows, sources
                )
            total = (mine + swap_tensor(other).astype(F32)).astype(BF16)
            total = gather_over_dp(total, place, dp_size)
            return values, slants, values_grad, slants_grad, total

        return branch

    index = sum((most > 2 * level).astype(jnp.int32) for level in levels[:-1])
    values, slants, values_grad, slants_grad, total = lax.switch(
        index,
        [at_level(level) for level in levels],
        table,
        features,
        tangents,
        weight_in,
        weight_out,
        cotangent_values,
        cotangent_tangents,
        quarter,
        bias_pair,
        bias_got,
    )
    wide = 2 * half
    total = total.astype(F32)
    grad_in = total[: 2 * wide].reshape(2, wide, half)
    grad_out = (
        total[2 * wide : 4 * wide].reshape(2, 2, half, half).transpose(0, 2, 1, 3).reshape(2, half, wide)
    )
    bias_in_grad = total[4 * wide : 4 * wide + 2]
    bias_out_grad = total[4 * wide + 2 : 4 * wide + 4]
    return (
        values,
        slants,
        values_grad,
        slants_grad,
        grad_in,
        bias_in_grad,
        grad_out,
        bias_out_grad,
    )


LEVELS = (6, 10, 11, 12, 13, 16)


def solution(mesh):
    in_specs = (
        P("dp", "tensor"),
        P(None, "dp", "tensor"),
        P(None, None, "tensor"),
        P(None, "tensor"),
        P(None, "tensor", None),
        P(None, "tensor"),
        P("dp"),
        P("dp", "tensor"),
        P(None, "dp", "tensor"),
    )
    out_specs = (
        P("dp", "tensor"),
        P(None, "dp", "tensor"),
        P("dp", "tensor"),
        P(None, "dp", "tensor"),
        P(None, None, "tensor"),
        P(None, "tensor"),
        P(None, "tensor", None),
        P(None, "tensor"),
    )
    return jax.shard_map(
        functools.partial(local, mesh.shape["dp"]),
        mesh=mesh,
        in_specs=in_specs,
        out_specs=out_specs,
        check_vma=False,
    )
```

time: 2600 us -> 404 us (0.16)
  waiting for transfers between devices: 2200 us -> 191 us
  matrix products: 176 us -> 0 us
  other arithmetic: 155 us -> 22.2 us
  Pallas kernels: 0 us -> 102 us
    reduce_scatter x4 -> x0, waiting for transfers between devices: 1360 us -> none  [the longest x2 704 us: local(): lax.psum_scatter(partial_value, 'tensor', scatter_dimension=2, tiled=True)]
    all_gather x4 -> x0, waiting for transfers between devices: 759 us -> none  [the longest x2 380 us: local(): gathered = lax.all_gather(outgoing, 'tensor', axis=2, tiled=True)]
    ppermute x0 -> x21, waiting for transfers between devices: none -> 191 us  [the longest x11 148 us: swap_tensor(): return lax.ppermute(value, 'tensor', [(0, 1), (1, 0)])]
    dot_general x12 -> x0, matrix products: 176 us -> none  [the longest x2 37.8 us: backward_local(): jnp.einsum('srh,dh->srd', grad_stack, weight, preferred_element_type=jnp....]
    pallas_call x0 -> x11, Pallas kernels: none -> 102 us  [the longest x2 66.7 us: run_blocks(): pl.pallas_call(functools.partial(blocks_kernel, sources, base, rows, tile...]
    psum x1 -> x0, waiting for transfers between devices: 85.4 us -> none  [local(): grad_first, grad_bias, grad_second, grad_out_bias = lax.psum(stacked, 'dp')]
    convert_element_type x3 -> x1, other arithmetic: 59.8 us -> 0.02 us  [branch(): total = (mine + swap_tensor(other).astype(F32)).astype(BF16)]
    reduce_sum x6 -> x2, other arithmetic: 39.4 us -> 1.51 us  [the longest x1 0.87 us: bias_rows(): flat = jnp.swapaxes(jnp.sum(biases, 1).reshape(4, 2, half), 0, 1)]
  transfers between devices with their start and end apart: 9 -> 21, of which waited for: 9 -> 12; matrix products, arithmetic and copies ran while one was open for 6% -> 7% of each run, Pallas kernels for 0% -> 18%
where the time goes in v1:
time: 404 us; the launch traced here: 398 us
  waiting for transfers between devices  191 us (47%)
  Pallas kernels  102 us (25%)
  local copies, waits for them, and re-layouts  30.9 us (8%)
  other arithmetic  22.2 us (5%)
  starting transfers between devices  22.2 us (5%)
  loops' own time  14.4 us (4%)
  blocking collectives  11.1 us (3%)
  between operations  4.18 us (1%)
    ppermute x11, waiting for transfers between devices, swap_tensor(): return lax.ppermute(value, 'tensor', [(0, 1), (1, 0)])  148 us
    pallas_call x2, Pallas kernels, run_blocks(): pl.pallas_call(functools.partial(blocks_kernel, sources, base, rows, tile...  66.7 us
    ppermute x10, waiting for transfers between devices, swap_bit(): return lax.ppermute(value, 'dp', [(i, i ^ 1 << bit) for i in range(size)])  42.6 us
    pallas_call x4, Pallas kernels, pack(): pl.pallas_call(functools.partial(pack_kernel, sources, values.shape[0] //...  16.9 us
    another operation x1, loops' own time, local(): lax.switch(index, [at_level(level) for level in levels], table, features,...  14.4 us
    pallas_call x4, Pallas kernels, unpack(): pl.pallas_call(functools.partial(unpack_kernel, sources, values.shape[0]...  14.4 us
    ppermute x11, starting transfers between devices, swap_tensor(): return lax.ppermute(value, 'tensor', [(0, 1), (1, 0)])  11.5 us
    pmax x1, blocking collectives, local(): most = lax.pmax(packed_rows, 'dp')  11.1 us
  transfers between devices with their start and end apart: 21, of which 12 were waited for; matrix products, arithmetic and copies ran while one was open for 7% of the time, Pallas kernels for 18%

profile of v1, /device:TPU:10, one launch (start us, length us, event | category | flops | bytes accessed | tf_op | source)
XLA Modules:
  0.0 398.1 jit_solution(10800297625994423892)
XLA Ops:
  6.4 11.1 %pmax.7 = s32[]{:T(128)} all-reduce(s32[]{:T(128)} %get-tuple-element.618), channel_id=1, replica_groups=mesh['dp'=16,'tensor'=2] {'dp'}, use_global_device_ids=true, to_apply=%region_1.2 | all-reduce | flops 1 | bytes 8 | tf_op jit(solution)/shard_map/pmax | solution.py:431
  20.8 372.3 %conditional.1 = (bf16[4096,256]{1,0:T(8,128)(2,1)}, bf16[3,4096,256]{2,1,0:T(8,128)(2,1)}, bf16[4096,256]{1,0:T(8,128)(2,1)}, bf16[3,4096,256]{2,1,0:T(8,128)(2,1)}, bf16[2176,256]{1,0:T(8,128)(2,1)}) conditional(s32[]{:T(128)} %clamp.3, (s32[49]{0:T(128)S(1)}, bf16[4096,256]{1,0:T(8,128)(2,1)}, ...), branch_computations={%region_3.5_spmd, %region_5.7_spmd, %region_7.9_spmd, %region_9.11... | conditional | flops 51570528256 | bytes 390694048 | solution.py:501
  27.5 3.7 pack.38
  34.1 6.5 %pack.39 = (bf16[4,1024,256]{2,1,0:T(8,128)(2,1)S(1)}, bf16[4,1024,256]{2,1,0:T(8,128)(2,1)}) custom-call(s32[49]{0:T(128)S(1)} %get-tuple-element.300.table, bf16[4096,256]{1,0:T(8,128)(2,1)S(1)} %copy-done.61, bf16[3,4096,256]{2,1,0:T(8,128)(2,1)S(1)} %copy-done.52), custom_call_target="tpu_custom_call" | custom-call | bytes 8388608 | tf_op jit(solution)/shard_map/cond/branch_3_fun/pack/pallas_call | solution.py:87
  43.6 5.2 %collective-permute-done.59 = bf16[512,256]{1,0:T(8,128)(2,1)S(1)} collective-permute-done((bf16[512,256]{1,0:T(8,128)(2,1)S(1)}, bf16[512,256]{1,0:T(8,128)(2,1)S(1)}, u32[]{:S(2)}, u32[]{:S(2)}) %collective-permute-start.59) | collective-permute-done | bytes 262176 | tf_op jit(solution)/shard_map/cond/branch_3_fun/ppermute | solution.py:367
  49.8 4.0 blank.9
  53.8 2.8 pack.36
  58.8 3.9 pack.37
  77.9 4.1 %maximum_select_fusion.29 = (bf16[2,512,512]{1,2,0:T(8,128)(2,1)}, bf16[2,512,512]{1,2,0:T(8,128)(2,1)}) fusion(bf16[2,512,256]{1,2,0:T(8,128)(2,1)} %copy.139, bf16[2,512,256]{1,2,0:T(8,128)(2,1)} %copy.170, pred[]{:T(512)S(6)} %eq.108, bf16[2,256,512]{1,2,0:T(8,128)(2,1)} %copy.171, bf16[2,256,512]{1,2,0:T(8,128)(2,1)} %copy.141), kind=kLoop, calls=%fused_computation.82 | loop fusion | flops 9437184 | bytes 4194305 | tf_op jit(solution)/shard_map/cond/branch_3_fun/jit(_where)/select_n | solution.py:371
  86.5 39.6 %collective-permute-done.62.g_got = bf16[4,1024,256]{2,1,0:T(8,128)(2,1)} collective-permute-done((bf16[4,1024,256]{2,1,0:T(8,128)(2,1)}, bf16[4,1024,256]{2,1,0:T(8,128)(2,1)}, u32[]{:S(2)}, u32[]{:S(2)}) %collective-permute-start.62) | collective-permute-done | bytes 2097184 | tf_op jit(solution)/shard_map/cond/branch_3_fun/ppermute | solution.py:363
  126.2 41.8 %blocks.18 = (bf16[4,1024,256]{2,1,0:T(8,128)(2,1)}, bf16[4,1024,256]{2,1,0:T(8,128)(2,1)}, bf16[4,1024,256]{2,1,0:T(8,128)(2,1)}, bf16[4,1024,256]{2,1,0:T(8,12...) custom-call(s32[49]{0:T(128)S(1)} %get-tuple-element.300.table, bf16[4,1024,256]{2,1,0:T(8,128)(2,1)} %copy-done.28, ...), custom_call_target="tpu_custom_call" | custom-call | flops 25769803776 | bytes 20971520 | tf_op jit(solution)/shard_map/cond/branch_3_fun/blocks/pallas_call | solution.py:337
  168.0 25.0 %blocks.19 = (bf16[4,512,256]{2,1,0:T(8,128)(2,1)}, bf16[4,512,256]{2,1,0:T(8,128)(2,1)}, bf16[4,512,256]{2,1,0:T(8,128)(2,1)}, bf16[4,512,256]{2,1,0:T(8,128)(2...) custom-call(s32[49]{0:T(128)S(1)} %get-tuple-element.300.table, ...), custom_call_target="tpu_custom_call", output_to_operand_aliasing={{4}: (11, {}), {5}: (12, {})} | custom-call | flops 12884901888 | bytes 12582912 | tf_op jit(solution)/shard_map/cond/branch_3_fun/blocks/pallas_call | solution.py:337
  193.8 2.5 select_maximum_fusion.3
  198.4 4.5 %collective-permute-done.63 = f32[2,1088,256]{2,1,0:T(8,128)} collective-permute-done((f32[2,1088,256]{2,1,0:T(8,128)S(1)}, f32[2,1088,256]{2,1,0:T(8,128)}, u32[]{:S(2)}, u32[]{:S(2)}) %collective-permute-start.63) | collective-permute-done | bytes 2228256 | tf_op jit(solution)/shard_map/cond/branch_3_fun/ppermute | solution.py:367
  202.9 2.6 dynamic-slice_add_fusion.3
  206.8 13.6 %collective-permute-done.64 = bf16[2,544,256]{2,1,0:T(8,128)(2,1)} collective-permute-done((bf16[2,544,256]{2,1,0:T(8,128)(2,1)S(1)}, bf16[2,544,256]{2,1,0:T(8,128)(2,1)}, u32[]{:S(2)}, u32[]{:S(2)}) %collective-permute-start.64) | collective-permute-done | bytes 557088 | tf_op jit(solution)/shard_map/cond/branch_3_fun/ppermute | solution.py:367
  223.9 6.5 %collective-permute-done.65 = bf16[2,272,256]{2,1,0:T(8,128)(2,1)} collective-permute-done((bf16[2,272,256]{2,1,0:T(8,128)(2,1)}, bf16[2,272,256]{2,1,0:T(8,128)(2,1)}, u32[]{:S(2)}, u32[]{:S(2)}) %collective-permute-start.65) | collective-permute-done | bytes 278560 | tf_op jit(solution)/shard_map/cond/branch_3_fun/ppermute | solution.py:367
  234.8 3.6 collective-permute-done.66
  241.0 84.1 %collective-permute-done.71 = bf16[136,256]{1,0:T(8,128)(2,1)S(1)} collective-permute-done((bf16[136,256]{1,0:T(8,128)(2,1)S(1)}, bf16[136,256]{1,0:T(8,128)(2,1)S(1)}, u32[]{:S(2)}, u32[]{:S(2)}) %collective-permute-start.71) | collective-permute-done | bytes 69664 | tf_op jit(solution)/shard_map/cond/branch_3_fun/ppermute | solution.py:363
  325.1 2.6 collective-permute-start.72
  327.7 2.7 collective-permute-done.72
  330.4 2.3 collective-permute-start.73
  332.7 3.0 collective-permute-done.73
  339.2 3.4 collective-permute-done.74
  343.6 4.4 %unpack.38 = (bf16[4096,256]{1,0:T(8,128)(2,1)}, bf16[3,4096,256]{2,1,0:T(8,128)(2,1)}) custom-call(s32[49]{0:T(128)S(1)} %get-tuple-element.300.table, bf16[4,1024,256]{2,1,0:T(8,128)(2,1)S(1)} %copy-done.5, bf16[4,1024,256]{2,1,0:T(8,128)(2,1)} %collective-permute-done.70.theirs, ...), custom_call_target="tpu_custom_call", output_to_operand_aliasing={{0}: (3, {}), {1}: (4, {})} | custom-call | bytes 8388608 | tf_op jit(solution)/shard_map/cond/branch_3_fun/unpack/pallas_call | solution.py:124
  348.0 4.3 %unpack.36 = (bf16[4096,256]{1,0:T(8,128)(2,1)}, bf16[3,4096,256]{2,1,0:T(8,128)(2,1)}) custom-call(s32[49]{0:T(128)S(1)} %get-tuple-element.300.table, bf16[4,1024,256]{2,1,0:T(8,128)(2,1)S(1)} %copy-done.4, bf16[4,1024,256]{2,1,0:T(8,128)(2,1)} %collective-permute-done.68.theirs, ...), custom_call_target="tpu_custom_call", output_to_operand_aliasing={{0}: (3, {}), {1}: (4, {})} | custom-call | bytes 8388608 | tf_op jit(solution)/shard_map/cond/branch_3_fun/unpack/pallas_call | solution.py:124
  352.4 11.2 %collective-permute-done.69.theirs = bf16[4,512,256]{2,1,0:T(8,128)(2,1)} collective-permute-done((bf16[4,512,256]{2,1,0:T(8,128)(2,1)}, bf16[4,512,256]{2,1,0:T(8,128)(2,1)}, u32[]{:S(2)}, u32[]{:S(2)}) %collective-permute-start.69) | collective-permute-done | bytes 1048608 | tf_op jit(solution)/shard_map/cond/branch_3_fun/ppermute | solution.py:363
  363.5 3.2 unpack.39
  366.8 13.5 %collective-permute-done.67.theirs = bf16[4,512,256]{2,1,0:T(8,128)(2,1)S(1)} collective-permute-done((bf16[4,512,256]{2,1,0:T(8,128)(2,1)}, bf16[4,512,256]{2,1,0:T(8,128)(2,1)S(1)}, u32[]{:S(2)}, u32[]{:S(2)}) %collective-permute-start.67) | collective-permute-done | bytes 1048608 | tf_op jit(solution)/shard_map/cond/branch_3_fun/ppermute | solution.py:363
  380.3 2.4 unpack.37
  382.8 2.9 maximum_select_fusion.27
  393.1 2.3 fusion.23
  (96 shorter events, 56.1 us)
Async XLA Ops:
  0.6 4.2 %copy-start.82 = (f32[2,256]{1,0:T(2,128)S(1)}, f32[2,256]{1,0:T(2,128)}, u32[]{:S(2)}) copy-start(f32[2,256]{1,0:T(2,128)} %param.18) | copy-start | bytes 6148
  0.6 4.2 %copy-start.81 = (f32[2,256]{1,0:T(2,128)S(1)}, f32[2,256]{1,0:T(2,128)}, u32[]{:S(2)}) copy-start(f32[2,256]{1,0:T(2,128)} %param.20) | copy-start | bytes 6148
  0.7 4.7 %copy-start.83 = (s32[16]{0:T(128)S(1)}, s32[16]{0:T(128)}, u32[]{:S(2)}) copy-start(s32[16]{0:T(128)} %param.21) | copy-start | bytes 196
  3.2 17.5 %collective-permute-start.114 = (bf16[512,256]{1,0:T(8,128)(2,1)S(1)}, bf16[512,256]{1,0:T(8,128)(2,1)S(1)}, u32[]{:S(2)}, u32[]{:S(2)}) collective-permute-start(bf16[512,256]{1,0:T(8,128)(2,1)S(1)} %fusion.12), channel_id=1, source_target_pairs={{0,1},{1,0},{2,3},{3,2},{4,5},{5,4},{6,7},{7,6},{8,9},{9,8},{10,11... | collective-permute-start | bytes 786440 | tf_op jit(solution)/shard_map/ppermute | solution.py:363
  4.8 15.9 %collective-permute-start.115 = (f32[2,2,256]{2,1,0:T(2,128)S(1)}, f32[2,2,256]{2,1,0:T(2,128)S(1)}, u32[]{:S(2)}, u32[]{:S(2)}) collective-permute-start(f32[2,2,256]{2,1,0:T(2,128)S(1)} %pad_maximum_fusion), channel_id=1, source_target_pairs={{0,1},{1,0},{2,3},{3,2},{4,5},{5,4},{6,7},{7,6},{8,9},{9,8},{10,11... | collective-permute-start | bytes 12296 | tf_op jit(solution)/shard_map/ppermute | solution.py:363
  27.5 6.6 %copy-start.52 = (bf16[3,4096,256]{2,1,0:T(8,128)(2,1)S(1)}, bf16[3,4096,256]{2,1,0:T(8,128)(2,1)}, u32[]{:S(2)}) copy-start(bf16[3,4096,256]{2,1,0:T(8,128)(2,1)} %get-tuple-element.311.tangents) | copy-start | bytes 18874372 | tf_op jit(solution)/shard_map/cond
  27.5 6.6 %copy-start.61 = (bf16[4096,256]{1,0:T(8,128)(2,1)S(1)}, bf16[4096,256]{1,0:T(8,128)(2,1)}, u32[]{:S(2)}) copy-start(bf16[4096,256]{1,0:T(8,128)(2,1)} %get-tuple-element.310.values) | copy-start | bytes 6291460 | tf_op jit(solution)/shard_map/cond
  32.6 54.0 %collective-permute-start.61 = (bf16[4,1024,256]{2,1,0:T(8,128)(2,1)S(1)}, bf16[4,1024,256]{2,1,0:T(8,128)(2,1)}, u32[]{:S(2)}, u32[]{:S(2)}) collective-permute-start(bf16[4,1024,256]{2,1,0:T(8,128)(2,1)S(1)} %get-tuple-element.322), channel_id=1, source_target_pairs={{0,1},{1,0},{2,3},{3,2},{4,5},{5,4},{6,7},{7,6},{8,9},{9,8},{10,11... | collective-permute-start | bytes 6291464 | tf_op jit(solution)/shard_map/cond/branch_3_fun/ppermute | solution.py:363
  41.9 84.3 %collective-permute-start.62 = (bf16[4,1024,256]{2,1,0:T(8,128)(2,1)}, bf16[4,1024,256]{2,1,0:T(8,128)(2,1)}, u32[]{:S(2)}, u32[]{:S(2)}) collective-permute-start(bf16[4,1024,256]{2,1,0:T(8,128)(2,1)} %get-tuple-element.324), channel_id=1, source_target_pairs={{0,1},{1,0},{2,3},{3,2},{4,5},{5,4},{6,7},{7,6},{8,9},{9,8},{10,11... | collective-permute-start | bytes 6291464 | tf_op jit(solution)/shard_map/cond/branch_3_fun/ppermute | solution.py:363
  42.4 6.4 %collective-permute-start.59 = (bf16[512,256]{1,0:T(8,128)(2,1)S(1)}, bf16[512,256]{1,0:T(8,128)(2,1)S(1)}, u32[]{:S(2)}, u32[]{:S(2)}) collective-permute-start(bf16[512,256]{1,0:T(8,128)(2,1)S(1)} %get-tuple-element.317), channel_id=1, source_target_pairs={{0,4},{2,6},{4,0},{6,2},{8,12},{10,14},{12,8},{14,10},{16,20},{18,... | collective-permute-start | bytes 786440 | tf_op jit(solution)/shard_map/cond/branch_3_fun/ppermute | solution.py:367
  49.8 19.0 %collective-permute-start.60 = (bf16[1024,256]{1,0:T(8,128)(2,1)}, bf16[1024,256]{1,0:T(8,128)(2,1)}, u32[]{:S(2)}, u32[]{:S(2)}) collective-permute-start(bf16[1024,256]{1,0:T(8,128)(2,1)} %maximum_select_fusion.32), channel_id=1, source_target_pairs={{0,2},{2,0},{4,6},{6,4},{8,10},{10,8},{12,14},{14,12},{16,18},{18,... | collective-permute-start | bytes 1572872 | tf_op jit(solution)/shard_map/cond/branch_3_fun/ppermute | solution.py:367
  53.8 5.0 %copy-start.62 = (bf16[4096,256]{1,0:T(8,128)(2,1)S(1)}, bf16[4096,256]{1,0:T(8,128)(2,1)}, u32[]{:S(2)}) copy-start(bf16[4096,256]{1,0:T(8,128)(2,1)} %get-tuple-element.310.values) | copy-start | bytes 6291460 | tf_op jit(solution)/shard_map/cond
  57.5 110.4 %collective-permute-start.57 = (bf16[4,512,256]{2,1,0:T(8,128)(2,1)S(1)}, bf16[4,512,256]{2,1,0:T(8,128)(2,1)}, u32[]{:S(2)}, u32[]{:S(2)}) collective-permute-start(bf16[4,512,256]{2,1,0:T(8,128)(2,1)S(1)} %get-tuple-element.309), channel_id=1, source_target_pairs={{0,1},{1,0},{2,3},{3,2},{4,5},{5,4},{6,7},{7,6},{8,9},{9,8},{10,11... | collective-permute-start | bytes 3145736 | tf_op jit(solution)/shard_map/cond/branch_3_fun/ppermute | solution.py:363
  63.6 104.3 %collective-permute-start.58 = (bf16[4,512,256]{2,1,0:T(8,128)(2,1)}, bf16[4,512,256]{2,1,0:T(8,128)(2,1)}, u32[]{:S(2)}, u32[]{:S(2)}) collective-permute-start(bf16[4,512,256]{2,1,0:T(8,128)(2,1)} %get-tuple-element.313), channel_id=1, source_target_pairs={{0,1},{1,0},{2,3},{3,2},{4,5},{5,4},{6,7},{7,6},{8,9},{9,8},{10,11... | collective-permute-start | bytes 3145736 | tf_op jit(solution)/shard_map/cond/branch_3_fun/ppermute | solution.py:363
  196.3 2.1 copy-start.71
  198.4 4.5 %collective-permute-start.63 = (f32[2,1088,256]{2,1,0:T(8,128)S(1)}, f32[2,1088,256]{2,1,0:T(8,128)}, u32[]{:S(2)}, u32[]{:S(2)}) collective-permute-start(f32[2,1088,256]{2,1,0:T(8,128)S(1)} %constant_dynamic-slice_fusion.3), channel_id=1, source_target_pairs={{0,2},{2,0},{4,6},{6,4},{8,10},{10,8},{12,14},{14,12},{16,18},{18,... | collective-permute-start | bytes 6684680 | tf_op jit(solution)/shard_map/cond/branch_3_fun/ppermute | solution.py:367
  205.5 14.8 %collective-permute-start.64 = (bf16[2,544,256]{2,1,0:T(8,128)(2,1)S(1)}, bf16[2,544,256]{2,1,0:T(8,128)(2,1)}, u32[]{:S(2)}, u32[]{:S(2)}) collective-permute-start(bf16[2,544,256]{2,1,0:T(8,128)(2,1)S(1)} %dynamic-slice_convert_fusion.12), channel_id=1, source_target_pairs={{0,4},{2,6},{4,0},{6,2},{8,12},{10,14},{12,8},{14,10},{16,20},{18,... | collective-permute-start | bytes 1671176 | tf_op jit(solution)/shard_map/cond/branch_3_fun/ppermute | solution.py:367
  222.3 8.2 %collective-permute-start.65 = (bf16[2,272,256]{2,1,0:T(8,128)(2,1)}, bf16[2,272,256]{2,1,0:T(8,128)(2,1)}, u32[]{:S(2)}, u32[]{:S(2)}) collective-permute-start(bf16[2,272,256]{2,1,0:T(8,128)(2,1)} %dynamic-slice_convert_fusion.13), channel_id=1, source_target_pairs={{0,8},{2,10},{4,12},{6,14},{8,0},{10,2},{12,4},{14,6},{16,24},{18,... | collective-permute-start | bytes 835592 | tf_op jit(solution)/shard_map/cond/branch_3_fun/ppermute | solution.py:367
  223.9 119.7 %copy-start.5 = (bf16[4,1024,256]{2,1,0:T(8,128)(2,1)S(1)}, bf16[4,1024,256]{2,1,0:T(8,128)(2,1)}, u32[]{:S(2)}) copy-start(bf16[4,1024,256]{2,1,0:T(8,128)(2,1)} %get-tuple-element.343.mine) | copy-start | bytes 6291460 | tf_op jit(solution)/shard_map/cond
  232.3 6.1 %collective-permute-start.66 = (bf16[2,136,256]{2,1,0:T(8,128)(2,1)S(1)}, bf16[2,136,256]{2,1,0:T(8,128)(2,1)S(1)}, u32[]{:S(2)}, u32[]{:S(2)}) collective-permute-start(bf16[2,136,256]{2,1,0:T(8,128)(2,1)S(1)} %dynamic-slice_convert_fusion.14), channel_id=1, source_target_pairs={{0,16},{2,18},{4,20},{6,22},{8,24},{10,26},{12,28},{14,30},{16,0},... | collective-permute-start | bytes 417800 | tf_op jit(solution)/shard_map/cond/branch_3_fun/ppermute | solution.py:367
  232.7 110.8 %collective-permute-start.70 = (bf16[4,1024,256]{2,1,0:T(8,128)(2,1)}, bf16[4,1024,256]{2,1,0:T(8,128)(2,1)}, u32[]{:S(2)}, u32[]{:S(2)}) collective-permute-start(bf16[4,1024,256]{2,1,0:T(8,128)(2,1)} %get-tuple-element.344), channel_id=1, source_target_pairs={{0,1},{1,0},{2,3},{3,2},{4,5},{5,4},{6,7},{7,6},{8,9},{9,8},{10,11... | collective-permute-start | bytes 6291464 | tf_op jit(solution)/shard_map/cond/branch_3_fun/ppermute | solution.py:363
  234.1 113.9 %collective-permute-start.68 = (bf16[4,1024,256]{2,1,0:T(8,128)(2,1)}, bf16[4,1024,256]{2,1,0:T(8,128)(2,1)}, u32[]{:S(2)}, u32[]{:S(2)}) collective-permute-start(bf16[4,1024,256]{2,1,0:T(8,128)(2,1)} %get-tuple-element.334), channel_id=1, source_target_pairs={{0,1},{1,0},{2,3},{3,2},{4,5},{5,4},{6,7},{7,6},{8,9},{9,8},{10,11... | collective-permute-start | bytes 6291464 | tf_op jit(solution)/shard_map/cond/branch_3_fun/ppermute | solution.py:363
  239.4 85.6 %collective-permute-start.71 = (bf16[136,256]{1,0:T(8,128)(2,1)S(1)}, bf16[136,256]{1,0:T(8,128)(2,1)S(1)}, u32[]{:S(2)}, u32[]{:S(2)}) collective-permute-start(bf16[136,256]{1,0:T(8,128)(2,1)S(1)} %fusion.7), channel_id=1, source_target_pairs={{0,1},{1,0},{2,3},{3,2},{4,5},{5,4},{6,7},{7,6},{8,9},{9,8},{10,11... | collective-permute-start | bytes 208904 | tf_op jit(solution)/shard_map/cond/branch_3_fun/ppermute | solution.py:363
  325.1 5.3 %collective-permute-start.72 = (bf16[136,256]{1,0:T(8,128)(2,1)S(1)}, bf16[136,256]{1,0:T(8,128)(2,1)S(1)}, u32[]{:S(2)}, u32[]{:S(2)}) collective-permute-start(bf16[136,256]{1,0:T(8,128)(2,1)S(1)} %fusion.6), channel_id=1, source_target_pairs={{0,16},{2,18},{4,20},{6,22},{8,24},{10,26},{12,28},{14,30},{16,0},... | collective-permute-start | bytes 208904 | tf_op jit(solution)/shard_map/cond/branch_3_fun/ppermute | solution.py:367
  330.4 5.4 %collective-permute-start.73 = (bf16[272,256]{1,0:T(8,128)(2,1)S(1)}, bf16[272,256]{1,0:T(8,128)(2,1)S(1)}, u32[]{:S(2)}, u32[]{:S(2)}) collective-permute-start(bf16[272,256]{1,0:T(8,128)(2,1)S(1)} %maximum_select_fusion.34), channel_id=1, source_target_pairs={{0,8},{2,10},{4,12},{6,14},{8,0},{10,2},{12,4},{14,6},{16,24},{18,... | collective-permute-start | bytes 417800 | tf_op jit(solution)/shard_map/cond/branch_3_fun/ppermute | solution.py:367
  335.9 6.6 %collective-permute-start.74 = (bf16[544,256]{1,0:T(8,128)(2,1)S(1)}, bf16[544,256]{1,0:T(8,128)(2,1)S(1)}, u32[]{:S(2)}, u32[]{:S(2)}) collective-permute-start(bf16[544,256]{1,0:T(8,128)(2,1)S(1)} %maximum_select_fusion.33), channel_id=1, source_target_pairs={{0,4},{2,6},{4,0},{6,2},{8,12},{10,14},{12,8},{14,10},{16,20},{18,... | collective-permute-start | bytes 835592 | tf_op jit(solution)/shard_map/cond/branch_3_fun/ppermute | solution.py:367
  337.1 26.4 %collective-permute-start.69 = (bf16[4,512,256]{2,1,0:T(8,128)(2,1)}, bf16[4,512,256]{2,1,0:T(8,128)(2,1)}, u32[]{:S(2)}, u32[]{:S(2)}) collective-permute-start(bf16[4,512,256]{2,1,0:T(8,128)(2,1)} %get-tuple-element.342), channel_id=1, source_target_pairs={{0,1},{1,0},{2,3},{3,2},{4,5},{5,4},{6,7},{7,6},{8,9},{9,8},{10,11... | collective-permute-start | bytes 3145736 | tf_op jit(solution)/shard_map/cond/branch_3_fun/ppermute | solution.py:363
  338.5 41.8 %collective-permute-start.67 = (bf16[4,512,256]{2,1,0:T(8,128)(2,1)}, bf16[4,512,256]{2,1,0:T(8,128)(2,1)S(1)}, u32[]{:S(2)}, u32[]{:S(2)}) collective-permute-start(bf16[4,512,256]{2,1,0:T(8,128)(2,1)} %get-tuple-element.332), channel_id=1, source_target_pairs={{0,1},{1,0},{2,3},{3,2},{4,5},{5,4},{6,7},{7,6},{8,9},{9,8},{10,11... | collective-permute-start | bytes 3145736 | tf_op jit(solution)/shard_map/cond/branch_3_fun/ppermute | solution.py:363
  343.6 39.2 %collective-permute-start.75 = (bf16[1088,256]{1,0:T(8,128)(2,1)}, bf16[1088,256]{1,0:T(8,128)(2,1)}, u32[]{:S(2)}, u32[]{:S(2)}) collective-permute-start(bf16[1088,256]{1,0:T(8,128)(2,1)} %maximum_select_fusion.31), channel_id=1, source_target_pairs={{0,2},{2,0},{4,6},{6,4},{8,10},{10,8},{12,14},{14,12},{16,18},{18,... | collective-permute-start | bytes 1671176 | tf_op jit(solution)/shard_map/cond/branch_3_fun/ppermute | solution.py:367
  343.6 4.4 %copy-start.4 = (bf16[4,1024,256]{2,1,0:T(8,128)(2,1)S(1)}, bf16[4,1024,256]{2,1,0:T(8,128)(2,1)}, u32[]{:S(2)}) copy-start(bf16[4,1024,256]{2,1,0:T(8,128)(2,1)} %get-tuple-element.333.mine) | copy-start | bytes 6291460 | tf_op jit(solution)/shard_map/cond
  348.0 15.5 %copy-start.17 = (bf16[4,512,256]{2,1,0:T(8,128)(2,1)S(1)}, bf16[4,512,256]{2,1,0:T(8,128)(2,1)}, u32[]{:S(2)}) copy-start(bf16[4,512,256]{2,1,0:T(8,128)(2,1)} %get-tuple-element.341.mine) | copy-start | bytes 3145732 | tf_op jit(solution)/shard_map/cond
  363.5 16.8 %copy-start.13 = (bf16[4,512,256]{2,1,0:T(8,128)(2,1)S(1)}, bf16[4,512,256]{2,1,0:T(8,128)(2,1)}, u32[]{:S(2)}) copy-start(bf16[4,512,256]{2,1,0:T(8,128)(2,1)} %get-tuple-element.327.mine) | copy-start | bytes 3145732 | tf_op jit(solution)/shard_map/cond
  (5 other events, 5.4 us)

commit v2 on v0

v2 whole, which is shorter than its diff:
```python
import functools
import math

import jax
import jax.numpy as jnp
import numpy as np
from jax import lax
from jax.experimental import pallas as pl
from jax.experimental.pallas import tpu as pltpu
from jax.sharding import PartitionSpec as P

LOG_TWO = math.log(2.0)
GROUP = 16
BF16, F32 = jnp.bfloat16, jnp.float32
SCALARS = pl.BlockSpec(memory_space=pltpu.SMEM)
HBM = pl.BlockSpec(memory_space=pltpu.HBM)
MIB = 1 << 20

ROWS, FIRST, MOVED, EXTRA = 80, 36, 28, 8
OVER = -1

PLACE, SIDE, TOTAL, QUARTER, TAILS = range(5)
ROUNDS, OUT_LEFT, IN_LEFT, OUT_RIGHT, IN_RIGHT, KEPT, OVER_FIRST, OVER_LEFT = range(8)


def aligned(value):
    return pl.multiple_of(value, GROUP)


def round_up(count):
    return (count + GROUP - 1) // GROUP * GROUP


NO_COST = pl.CostEstimate(flops=0, bytes_accessed=1024, transcendentals=0)
COST_PER_ROW = 7 * 10**7


PARAMS = pltpu.CompilerParams(vmem_limit_bytes=60 * MIB)


def chain_order(size):
    around = (0, 1, 3, 2)
    order = []
    for block in range(size // 4):
        order += [4 * block + i for i in (around if block % 2 == 0 else around[::-1])]
    return order


def plan_kernel(order, most, early, moved, extra, who, totals, plan, flows):
    size = len(order)

    def most_out(total):
        return jnp.clip((total - early) // 2 // GROUP * GROUP, 0, moved)

    def total_of(i):
        return totals[order[i]]

    flow, rounds = jnp.int32(0), jnp.int32(0)
    flows[0] = flow
    for i in range(size):
        here = total_of(i) + flow
        if i + 1 < size:
            flow = jnp.clip(here - most, -most_out(total_of(i + 1)), most_out(total_of(i)))
        else:
            flow = jnp.int32(0)
        flows[i + 1] = flow
        over = jnp.maximum(here - flow - most, 0)
        rounds = jnp.maximum(rounds, (over + extra - 1) // extra)
    place = who[PLACE]
    left, right, total = flows[place], flows[place + 1], who[TOTAL]
    out_left, out_right = jnp.maximum(-left, 0), jnp.maximum(right, 0)
    over = jnp.maximum(total + left - right - most, 0)
    kept = total - out_left - out_right - over
    plan[ROUNDS] = rounds
    plan[OUT_LEFT] = out_left
    plan[IN_LEFT] = jnp.maximum(left, 0)
    plan[OUT_RIGHT] = out_right
    plan[IN_RIGHT] = jnp.maximum(-right, 0)
    plan[KEPT] = kept
    plan[OVER_FIRST] = kept
    plan[OVER_LEFT] = over


def make_plan(who, totals, order, level, early, moved, extra):
    return pl.pallas_call(
        functools.partial(plan_kernel, order, 2 * level, early, moved, 2 * extra),
        out_shape=jax.ShapeDtypeStruct((8,), jnp.int32),
        in_specs=[SCALARS] * 2,
        out_specs=SCALARS,
        scratch_shapes=[pltpu.SMEM((len(order) + 1,), jnp.int32)],
        cost_estimate=NO_COST,
        name="plan",
    )(who, totals)


def own_piece(limit, plan, base, rows):
    if base == OVER:
        first, size = plan[OVER_FIRST], jnp.clip(plan[OVER_LEFT], 0, 2 * rows)
    else:
        first, size = jnp.int32(base), jnp.clip(limit - base, 0, 2 * rows)
    return first, first + size, size


def moved_pieces(dims, plan, base, rows):
    top = 2 * dims[2] - base
    left, right = plan[IN_LEFT], plan[IN_RIGHT]
    return (aligned(top - left - right), aligned(left)), (aligned(top - right), aligned(right))


def sent_pieces(who, plan):
    left, right, total = plan[OUT_LEFT], plan[OUT_RIGHT], who[TOTAL]
    return (total - right - left, total - right, left), (total - right, total, right)


def whole_groups(count):
    return count // GROUP * GROUP


def each_run(dims, who, counts, piece, visit):
    sources, slot = dims[:2]
    first, end = piece[:2]

    def step(source, start):
        after = start + whole_groups(counts[source])
        begin = jnp.maximum(start, first)
        stop = jnp.minimum(after, end)

        @pl.when(stop > begin)
        def _():
            row = source * slot + begin - start
            visit(aligned(row), aligned(begin - first), aligned(stop - begin))

        return after

    lax.fori_loop(0, sources, step, who[TAILS])


def copies_between(held, streams, place, values, tangents, row, size):
    return (
        (values.at[pl.ds(row, size)], held.at[streams, pl.ds(place, size)]),
        (tangents.at[:, pl.ds(row, size)], held.at[pl.ds(streams + 1, 3), pl.ds(place, size)]),
    )


def wait_for(held, streams, size, sem):
    @pl.when(size > 0)
    def _():
        part = held.at[streams, pl.ds(0, aligned(size))]
        pltpu.make_async_copy(part, part, sem).wait()


def each_tail(dims, counts, visit):
    sources, slot = dims[:2]

    def step(source, found):
        left = counts[source] % GROUP
        row = source * slot + jnp.minimum(whole_groups(counts[source]), slot - GROUP)
        visit(source, aligned(row), left)
        return found + jnp.minimum(left, 1)

    return lax.fori_loop(0, sources, step, jnp.int32(0))


def tail_matrix(dims, counts):
    wide = dims[0] * GROUP
    lane = lax.broadcasted_iota(jnp.int32, (8, wide), 1)
    target = jnp.full((8, wide), -1, jnp.int32)
    start = jnp.int32(0)
    for source in range(dims[0]):
        left = counts[source] % GROUP
        row = lane - source * GROUP
        target = jnp.where((row >= 0) & (row < left), start + row, target)
        start = start + left
    number = lax.broadcasted_iota(jnp.int32, (wide, wide), 0)
    return jnp.where(number == target[:1], 1.0, 0.0).astype(BF16)


def make_who(dims, counts, who):
    place = lax.axis_index("dp")
    around = (place & 3) ^ ((place & 3) >> 1)
    back = (place >> 2) & 1
    who[PLACE] = (place >> 2) * 4 + around * (1 - back) + (3 - around) * back
    who[SIDE] = lax.axis_index("tensor")
    who[QUARTER] = my_quarter()

    def step(source, carry):
        whole, left = carry
        return whole + whole_groups(counts[source]), left + counts[source] % GROUP

    whole, left = lax.fori_loop(0, dims[0], step, (jnp.int32(0), jnp.int32(0)))
    left = (left + GROUP - 1) // GROUP * GROUP
    who[TOTAL] = whole + left
    who[TAILS] = left


def start_copies(held, place, sources, row, size, sem):
    for streams, (values, tangents) in zip((0, 4), sources):
        for copy in copies_between(held, streams, place, values, tangents, row, size):
            pltpu.make_async_copy(*copy, sem).start()


def pack_kernel(dims, base, rows, moving, who, counts, *refs):
    plan = None
    if moving or base == OVER:
        plan, *refs = refs
    sources, refs = (refs[:2], refs[2:4]), refs[4:]
    neighbours = ()
    if moving:
        neighbours, refs = refs[:2], refs[2:]
    keep, send, held, sems, *tails = refs
    side = who[SIDE]
    piece = own_piece(plan[KEPT] if moving else who[TOTAL], plan, base, rows)
    size = piece[2]

    if base == 0:
        ends, packed = tails

        def start_tail(source, row, left):
            start_copies(ends, aligned(source * GROUP), sources, row, GROUP, sems.at[1])

        each_tail(dims, counts, start_tail)
        size = size - who[TAILS]

    def start(row, place, size):
        start_copies(held, place, sources, row, size, sems.at[0])

    each_run(dims, who, counts, piece, start)
    arrivals = []
    if moving:
        pieces = moved_pieces(dims, plan, base, rows)
        for number, neighbour in enumerate(neighbours):
            place, moved = pieces[number]
            copy = pltpu.make_async_copy(
                neighbour.at[:, pl.ds(0, moved)], held.at[:, pl.ds(place, moved)], sems.at[1 + number]
            )
            arrivals.append((moved, copy))
        for moved, copy in arrivals:
            pl.when(moved > 0)(copy.start)
    if base == 0:
        matrix = tail_matrix(dims, counts)
        wait_for(ends, slice(0, 8), jnp.int32(dims[0] * GROUP), sems.at[1])
        for stream in range(8):
            packed[stream] = dot(matrix, ends[stream]).astype(BF16)

        def put(group, carry):
            here = pl.ds(aligned(group * GROUP), GROUP)
            held[:, here, :] = packed[:, here, :]
            return carry

        lax.fori_loop(0, who[TAILS] // GROUP, put, 0)
    wait_for(held, slice(0, 8), size, sems.at[0])
    for moved, copy in arrivals:
        pl.when(moved > 0)(copy.wait)
    out = [
        pltpu.make_async_copy(
            held.at[:, pl.ds(aligned(part * rows), rows)], target, sems.at[5 + number]
        )
        for number, (part, target) in enumerate(((1 - side, send), (side, keep)))
    ]
    for copy in out:
        copy.start()
    for copy in out:
        copy.wait()


def pack(dims, who, counts, plan, arrays, base, rows, neighbours=()):
    half = arrays[0].shape[1]
    shape = jax.ShapeDtypeStruct((8, rows, half), BF16)
    plans = (plan,) if neighbours or base == OVER else ()
    tails = [pltpu.VMEM((8, dims[0] * GROUP, half), BF16)] * 2 if base == 0 else []
    return pl.pallas_call(
        functools.partial(pack_kernel, dims, base, rows, len(neighbours) > 0),
        out_shape=(shape, shape),
        in_specs=[SCALARS] * (2 + len(plans)) + [HBM] * (4 + len(neighbours)),
        out_specs=(HBM, HBM),
        scratch_shapes=[pltpu.VMEM((8, 2 * rows, half), BF16), pltpu.SemaphoreType.DMA((7,))] + tails,
        cost_estimate=NO_COST,
        compiler_params=PARAMS,
        name="pack",
    )(who, counts, *plans, *arrays, *neighbours)


def export_kernel(dims, moved, who, counts, plan, x, x3, g, g3, *refs):
    targets, (held, sems) = refs[:2], refs[2:]
    pieces = sent_pieces(who, plan)
    for number, piece in enumerate(pieces):

        def start(row, place, size, number=number):
            place = aligned(number * moved + place)
            start_copies(held, place, ((x, x3), (g, g3)), row, size, sems.at[number])

        @pl.when(piece[2] > 0)
        def _(piece=piece, start=start):
            each_run(dims, who, counts, piece, start)

    for number, piece in enumerate(pieces):
        wait_for(held, slice(0, 8), piece[2], sems.at[number])
    out = [
        pltpu.make_async_copy(
            held.at[:, pl.ds(number * moved, moved)], target, sems.at[2 + number]
        )
        for number, target in enumerate(targets)
    ]
    for copy in out:
        copy.start()
    for copy in out:
        copy.wait()


def export(dims, who, counts, plan, x, x3, g, g3, moved):
    half = x.shape[1]
    return pl.pallas_call(
        functools.partial(export_kernel, dims, moved),
        out_shape=(jax.ShapeDtypeStruct((8, moved, half), BF16),) * 2,
        in_specs=[SCALARS] * 3 + [HBM] * 4,
        out_specs=(HBM,) * 2,
        scratch_shapes=[pltpu.VMEM((8, 2 * moved, half), BF16), pltpu.SemaphoreType.DMA((4,))],
        cost_estimate=NO_COST,
        compiler_params=PARAMS,
        name="export",
    )(who, counts, plan, x, x3, g, g3)


def load_results(held, rows, side, mine, theirs, sems):
    loads = [
        pltpu.make_async_copy(
            origin, held.at[:, pl.ds(aligned(part * rows), rows)], sems.at[number]
        )
        for number, (part, origin) in enumerate(((1 - side, theirs), (side, mine)))
    ]
    for load in loads:
        load.start()
    for load in loads:
        load.wait()


def handback_kernel(dims, base, rows, who, plan, mine, theirs, to_left, to_right, held, sems):
    load_results(held, rows, who[SIDE], mine, theirs, sems)
    copies = []
    pieces = moved_pieces(dims, plan, base, rows)
    for number, ((place, size), target) in enumerate(zip(pieces, (to_left, to_right))):
        copy = pltpu.make_async_copy(
            held.at[:, pl.ds(place, size)], target.at[:, pl.ds(0, size)], sems.at[2 + number]
        )
        copies.append((size, copy))
    for size, copy in copies:
        pl.when(size > 0)(copy.start)
    for size, copy in copies:
        pl.when(size > 0)(copy.wait)


def handback(dims, who, plan, mine, theirs, base, rows, moved):
    half = mine.shape[2]
    shape = jax.ShapeDtypeStruct((4, moved, half), BF16)
    return pl.pallas_call(
        functools.partial(handback_kernel, dims, base, rows),
        out_shape=(shape, shape),
        in_specs=[SCALARS] * 2 + [HBM] * 2,
        out_specs=(HBM, HBM),
        scratch_shapes=[pltpu.VMEM((4, 2 * rows, half), BF16), pltpu.SemaphoreType.DMA((4,))],
        cost_estimate=NO_COST,
        compiler_params=PARAMS,
        name="handback",
    )(who, plan, mine, theirs)


def unpack_kernel(dims, base, rows, streams, who, counts, plan, *refs):
    pairs = streams // 4
    mine, theirs, refs = refs[:pairs], refs[pairs], refs[pairs + 1 :]
    outs, (held, sems, *tails) = refs[2 * pairs : 4 * pairs], refs[4 * pairs :]
    side = 1 if base is None else who[SIDE]
    loads = [(pl.ds(0, streams), 1 - side, theirs)]
    loads += [(pl.ds(4 * number, 4), side, part) for number, part in enumerate(mine)]
    loads = [
        pltpu.make_async_copy(
            origin, held.at[where, pl.ds(aligned(part * rows), rows)], sems.at[number]
        )
        for number, (where, part, origin) in enumerate(loads)
    ]
    for load in loads:
        load.start()
    for load in loads:
        load.wait()
    pieces = sent_pieces(who, plan)
    if base is not None:
        pieces = (own_piece(plan[KEPT], plan, base, rows),)
    sizes = [piece[2] for piece in pieces]
    if base == 0:
        sizes = [sizes[0] - who[TAILS]]

    def start_out(origin, place, row, size, sem):
        for number in range(pairs):
            copies = copies_between(
                origin, 4 * number, place, outs[2 * number], outs[2 * number + 1], row, size
            )
            for there, here in copies:
                pltpu.make_async_copy(here, there, sem).start()

    for number, piece in enumerate(pieces):

        def start(row, place, size, number=number):
            start_out(held, aligned(number * rows + place), row, size, sems.at[3 + number])

        @pl.when(piece[2] > 0)
        def _(piece=piece, start=start):
            each_run(dims, who, counts, piece, start)

    if base == 0:
        (ends,) = tails
        matrix = tail_matrix(dims, counts)
        for stream in range(streams):
            packed = held[stream, : dims[0] * GROUP, :]
            ends[stream] = dot(matrix, packed, TN).astype(BF16)

        def start_tail(source, row, left):
            @pl.when(left > 0)
            def _():
                start_out(ends, aligned(source * GROUP), row, GROUP, sems.at[4])

        found = each_tail(dims, counts, start_tail)
        wait_for(ends, slice(0, streams), found * GROUP, sems.at[4])
    for number, size in enumerate(sizes):
        wait_for(held, slice(0, streams), size, sems.at[3 + number])


def unpack(dims, who, counts, plan, mine, theirs, outs, base, rows):
    half = outs[0].shape[1]
    streams = theirs.shape[0]
    tails = [pltpu.VMEM((streams, dims[0] * GROUP, half), BF16)] if base == 0 else []
    first = 4 + len(mine)
    return pl.pallas_call(
        functools.partial(unpack_kernel, dims, base, rows, streams),
        out_shape=[jax.ShapeDtypeStruct(out.shape, BF16) for out in outs],
        in_specs=[SCALARS] * 3 + [HBM] * (len(mine) + 1 + len(outs)),
        out_specs=[HBM] * len(outs),
        input_output_aliases={first + number: number for number in range(len(outs))},
        scratch_shapes=[
            pltpu.VMEM((streams, 2 * rows, half), BF16),
            pltpu.SemaphoreType.DMA((5,)),
        ]
        + tails,
        cost_estimate=NO_COST,
        compiler_params=PARAMS,
        name="unpack",
    )(who, counts, plan, *mine, theirs, *outs)


def blank_kernel(sources, slot, counts, values, tangents, other_values, other_tangents, zeros, sem):
    zeros[...] = jnp.zeros_like(zeros)

    def step(source, total):
        padded = round_up(counts[source])
        size = aligned(slot - padded)
        row = aligned(source * slot + padded)

        @pl.when(size > 0)
        def _():
            for low, high in ((values, tangents), (other_values, other_tangents)):
                for here, there in (
                    (zeros.at[0, pl.ds(0, size)], low.at[pl.ds(row, size)]),
                    (zeros.at[:, pl.ds(0, size)], high.at[:, pl.ds(row, size)]),
                ):
                    pltpu.make_async_copy(here, there, sem).start()

        return total + size

    total = lax.fori_loop(0, sources, step, jnp.int32(0))
    for low, high in ((values, tangents), (other_values, other_tangents)):

        @pl.when(total > 0)
        def _():
            low_part, high_part = low.at[pl.ds(0, aligned(total))], high.at[:, pl.ds(0, aligned(total))]
            pltpu.make_async_copy(low_part, low_part, sem).wait()
            pltpu.make_async_copy(high_part, high_part, sem).wait()


def blank(counts, row_count, half, sources):
    slot = row_count // sources
    values = jax.ShapeDtypeStruct((row_count, half), BF16)
    tangents = jax.ShapeDtypeStruct((3, row_count, half), BF16)
    return pl.pallas_call(
        functools.partial(blank_kernel, sources, slot),
        out_shape=(values, tangents, values, tangents),
        in_specs=[SCALARS],
        out_specs=(HBM, HBM, HBM, HBM),
        scratch_shapes=[pltpu.VMEM((3, slot, half), BF16), pltpu.SemaphoreType.DMA],
        cost_estimate=NO_COST,
        compiler_params=PARAMS,
        name="blank",
    )(counts)


NN = (((1,), (0,)), ((), ()))
TN = (((0,), (0,)), ((), ()))


def dot(a, b, dims=NN):
    return lax.dot_general(a, b, dims, preferred_element_type=F32)


def blocks_kernel(
    dims,
    base,
    rows,
    tile,
    first,
    final,
    merged,
    who,
    own,
    got,
    w_in,
    w_out,
    w_in_t,
    w_out_t,
    bias,
    *rest,
):
    if base != 0:
        plan, *rest = rest
    if first:
        grads_before = bias_before = None
    else:
        grads_before, bias_before, *rest = rest
    y_own, d_own, *rest = rest
    if merged:
        send, *rest = rest
        y_send, d_send = send.at[pl.ds(0, 4)], send.at[pl.ds(4, 4)]
    else:
        y_send, d_send, *rest = rest
    if final:
        kept, *rest = rest
        sent, rest = rest[:2], rest[2:]
    grads, biases, x_low, acts, slopes, lin = rest
    step = pl.program_id(0)
    side = who[SIDE]
    wide = w_in.shape[1]
    half = wide // 2

    @pl.when(step == 0)
    def _():
        if first:
            grads[...] = jnp.zeros_like(grads)
            biases[...] = jnp.zeros_like(biases)
        else:
            grads[...] = grads_before[...]
            biases[...] = bias_before[...]

    packed = side * rows + step * tile + lax.broadcasted_iota(jnp.int32, (tile, 128), 0)
    if base == OVER:
        filled = packed < plan[OVER_LEFT]
    elif base == 0:
        filled = packed < who[TOTAL]
    else:
        packed = packed + base
        top = 2 * dims[2] - plan[IN_LEFT] - plan[IN_RIGHT]
        filled = (packed < plan[KEPT]) | (packed >= top)
    filled = jnp.where(filled, 1.0, 0.0)
    is_filled = jnp.concatenate([filled] * (wide // 128), axis=1) > 0.0

    def load(stream):
        mine, theirs = own[stream].astype(F32), got[stream].astype(F32)
        left = jnp.where(side == 0, mine, theirs)
        right = jnp.where(side == 0, theirs, mine)
        return jnp.where(is_filled, jnp.concatenate([left, right], axis=1), 0.0)

    def store(own, send, stream, value):
        left, right = value[:, :half].astype(BF16), value[:, half:].astype(BF16)
        own[stream] = jnp.where(side == 0, left, right)
        send[stream] = jnp.where(side == 0, right, left)

    def add_bias(place, value):
        biases[place] += jnp.sum(value.reshape(tile // 8, 8, wide), axis=0)

    x = [load(stream) for stream in range(4)]
    for block in range(2):
        for stream in range(4):
            x_low[block, stream * tile : (stream + 1) * tile] = x[stream].astype(BF16)
        pre = dot(x_low[block], w_in[block])
        z = pre[:tile] + bias[0, block][None, :]
        small = jnp.exp(-jnp.abs(z))
        whole = 1.0 / (1.0 + small)
        slope = jnp.where(z >= 0.0, whole, small * whole)
        slopes[block] = slope
        acts[block, :tile] = (jnp.maximum(z, 0.0) + jnp.log1p(small) - LOG_TWO).astype(BF16)
        for stream in range(1, 4):
            part = pre[stream * tile : (stream + 1) * tile]
            lin[block, stream - 1] = part
            acts[block, stream * tile : (stream + 1) * tile] = (slope * part).astype(BF16)
        out = dot(acts[block], w_out[block])
        x = [x[stream] + out[stream * tile : (stream + 1) * tile] for stream in range(4)]
        x[0] = x[0] + bias[1, block][None, :]
    for stream in range(4):
        store(y_own, y_send, stream, x[stream])

    g = [load(4 + stream) for stream in range(4)]
    for block in (1, 0):
        add_bias(2 + block, g[0])
        g_low = jnp.concatenate([part.astype(BF16) for part in g], axis=0)
        value = dot(acts[block], g_low, TN)
        for part in range(2):
            place = 2 * wide + block * wide + part * half
            grads[0, place : place + half, :] += value[:half, part * half : (part + 1) * half]
            grads[1, place : place + half, :] += value[half:, part * half : (part + 1) * half]
        mixed = dot(g_low, w_out_t[block])
        slope = slopes[block]
        total = jnp.zeros((tile, wide), F32)
        lower = []
        for stream in range(1, 4):
            part = mixed[stream * tile : (stream + 1) * tile]
            total = total + part * lin[block, stream - 1]
            lower.append((part * slope).astype(BF16))
        g_pre = (mixed[:tile] * slope + slope * (1.0 - slope) * total).astype(BF16)
        add_bias(block, g_pre.astype(F32))
        stack = jnp.concatenate([g_pre] + lower, axis=0)
        value = dot(x_low[block], stack, TN)
        for part in range(2):
            grads[part, block * wide : (block + 1) * wide, :] += value[:, part * half : (part + 1) * half]
        back = dot(stack, w_in_t[block])
        g = [g[stream] + back[stream * tile : (stream + 1) * tile] for stream in range(4)]
    for stream in range(4):
        store(d_own, d_send, stream, g[stream])

    if final:

        @pl.when(step == rows // tile - 1)
        def _():
            total = jnp.sum(biases[...], axis=1)
            for part in range(2):
                grads[part, 4 * wide : 4 * wide + 4, :] = total[:, part * half : (part + 1) * half]
            flag = who[QUARTER] >> 1
            size = kept.shape[1]
            kept[...] = grads[:, pl.ds(aligned(flag * size), size), :]
            for part in range(2):
                other = grads[part, pl.ds(aligned((1 - flag) * size), size), :]
                sent[part][...] = other.astype(BF16)


def tile_of(rows):
    return max(tile for tile in range(GROUP, 193, GROUP) if rows % tile == 0)


def run_blocks(dims, who, plan, own, got, weights, sums, base, final, merged):
    rows, half = own.shape[1:]
    wide = 2 * half
    tile = tile_of(rows)
    first = sums is None
    piece = pl.BlockSpec((8, tile, half), lambda i: (0, i, 0))

    def whole(array):
        return pl.BlockSpec(
            array.shape, lambda i, rank=len(array.shape): (0,) * rank, pipeline_mode=pl.Buffered(1)
        )

    sum_rows = 4 * wide + dims[3]
    sums_held = [((2, sum_rows, half), F32), ((4, 8, wide), F32)]
    if final:
        results = [((2, sum_rows // 2, half), F32)] + [((sum_rows // 2, half), BF16)] * 2
        scratch = [pltpu.VMEM(*item) for item in sums_held]
    else:
        results, scratch = sums_held, []
    results = [jax.ShapeDtypeStruct(*item) for item in results]
    sizes = (4, 4, 8) if merged else (4, 4, 4, 4)
    out_shapes = [jax.ShapeDtypeStruct((size, rows, half), BF16) for size in sizes]
    out_pieces = [pl.BlockSpec((size, tile, half), lambda i: (0, i, 0)) for size in sizes]
    plans = () if base == 0 else (plan,)
    extra = () if first else sums
    operands = (who, own, got, *weights, *plans, *extra)
    aliases = {}
    if not first and not final:
        aliases = {len(operands) - 2 + i: len(sizes) + i for i in range(2)}
    return pl.pallas_call(
        functools.partial(blocks_kernel, dims, base, rows, tile, first, final, merged),
        grid=(rows // tile,),
        out_shape=out_shapes + results,
        in_specs=[SCALARS]
        + [piece] * 2
        + [whole(item) for item in weights]
        + [SCALARS] * len(plans)
        + [whole(item) for item in extra],
        out_specs=out_pieces + [whole(item) for item in results],
        input_output_aliases=aliases,
        scratch_shapes=scratch
        + [
            pltpu.VMEM((2, 4 * tile, wide), BF16),
            pltpu.VMEM((2, 4 * tile, wide), BF16),
            pltpu.VMEM((2, tile, wide), F32),
            pltpu.VMEM((2, 3, tile, wide), F32),
        ],
        cost_estimate=pl.CostEstimate(
            flops=rows * COST_PER_ROW if base == 0 else 0, bytes_accessed=1024, transcendentals=0
        ),
        compiler_params=PARAMS,
        name="blocks",
    )(*operands)


def swap_tensor(value):
    return lax.ppermute(value, "tensor", [(0, 1), (1, 0)])


def shift(value, order, step):
    pairs = list(zip(order[:-1], order[1:]))
    return lax.ppermute(value, "dp", pairs if step == 1 else [(b, a) for a, b in pairs])


def in_order(flag, mine, other, axis):
    return jnp.where(
        flag == 0, jnp.concatenate([mine, other], axis), jnp.concatenate([other, mine], axis)
    )


def my_quarter():
    place = lax.axis_index("dp")
    return (place & 1) * 2 + ((place >> 1) & 1)


def quarter_kernel(dims, counts, w_in, w_out, who, piece, sems):
    half = w_in.shape[2]
    mine = my_quarter()
    make_who(dims, counts, who)
    for number in range(4):

        @pl.when(mine == number)
        def _(number=number):
            if number < 2:
                copies = [pltpu.make_async_copy(w_in.at[number], piece, sems.at[0])]
            else:
                copies = [
                    pltpu.make_async_copy(
                        w_out.at[number - 2, :, pl.ds(part * half, half)],
                        piece.at[pl.ds(part * half, half)],
                        sems.at[part],
                    )
                    for part in range(2)
                ]
            for copy in copies:
                copy.start()
            for copy in copies:
                copy.wait()


def quarter_of(dims, counts, weight_in, weight_out):
    on_chip = pl.BlockSpec(memory_space=pltpu.VMEM)
    return pl.pallas_call(
        functools.partial(quarter_kernel, dims),
        out_shape=(
            jax.ShapeDtypeStruct((8,), jnp.int32),
            jax.ShapeDtypeStruct(weight_in.shape[1:], BF16),
        ),
        in_specs=[SCALARS] + [on_chip] * 2,
        out_specs=(SCALARS, on_chip),
        scratch_shapes=[pltpu.SemaphoreType.DMA((2,))],
        cost_estimate=NO_COST,
        name="quarter",
    )(counts, weight_in, weight_out)


def assemble_kernel(
    who, w_in, w_out, b_in, b_out, b_got, *refs
):
    pieces, (in_all, out_all, in_turned, out_turned, b_all, held, sems) = refs[:4], refs[4:]
    side, own = who[SIDE], who[QUARTER]
    half = w_in.shape[2]
    copies = [
        pltpu.make_async_copy(piece, held.at[own ^ number], sems.at[number])
        for number, piece in enumerate(pieces)
    ]
    for copy in copies:
        copy.start()
    for copy in copies:
        copy.wait()

    def ordered(mine, other, axis):
        return jnp.where(
            side == 0,
            jnp.concatenate([mine, other], axis),
            jnp.concatenate([other, mine], axis),
        )

    for block in range(2):
        value = ordered(w_in[block], held[block], 1)
        in_all[block] = value
        in_turned[block] = value.T
        other = jnp.concatenate([held[2 + block, :half], held[2 + block, half:]], axis=1)
        value = ordered(w_out[block], other, 0)
        out_all[block] = value
        out_turned[block] = value.T
    for number, mine in enumerate((b_in, b_out)):
        b_all[number] = ordered(mine[...], b_got[number], 1)


def assemble(who, weight_in, weight_out, bias_in, bias_out, bias_got, pieces):
    blocks, wide, half = weight_in.shape
    whole = jax.ShapeDtypeStruct((blocks, wide, wide), BF16)
    on_chip = pl.BlockSpec(memory_space=pltpu.VMEM)
    return pl.pallas_call(
        assemble_kernel,
        out_shape=(whole,) * 4 + (jax.ShapeDtypeStruct((2, blocks, wide), F32),),
        in_specs=[SCALARS] + [on_chip] * 5 + [HBM] * 4,
        out_specs=(on_chip,) * 5,
        scratch_shapes=[pltpu.VMEM((4, wide, half), BF16), pltpu.SemaphoreType.DMA((4,))],
        cost_estimate=NO_COST,
        compiler_params=PARAMS,
        name="assemble",
    )(who, weight_in, weight_out, bias_in, bias_out, bias_got, *pieces)


def flipped(value, flip, size):
    return lax.ppermute(value, "dp", [(i, i ^ flip) for i in range(size)])


def groups_of(bits):
    return [(0, 1), (1, 1)] + [(bit, min(2, bits - bit)) for bit in range(2, bits, 2)]


def reduce_step(grads, group, place, size):
    bit, many = group
    mine = (place >> bit) & ((1 << many) - 1)
    rows = grads.shape[1] >> many
    kept = lax.dynamic_slice_in_dim(grads, mine * rows, rows, 1)
    for flip in range(1, 1 << many):
        sent = lax.dynamic_slice_in_dim(grads, (mine ^ flip) * rows, rows, 1).astype(BF16)
        kept = kept + flipped(sent, flip << bit, size).astype(F32)
    return kept


def join_kernel(mine, *refs):
    parts, (whole, sems) = refs[:-2], refs[-2:]
    rows = parts[0].shape[0]
    copies = [
        pltpu.make_async_copy(
            part, whole.at[pl.ds(aligned((mine[0] ^ flip) * rows), rows)], sems.at[flip]
        )
        for flip, part in enumerate(parts)
    ]
    for copy in copies:
        copy.start()
    for copy in copies:
        copy.wait()


def gather_step(total, group, place, size):
    bit, many = group
    mine = (place >> bit) & ((1 << many) - 1)
    parts = [total] + [flipped(total, flip << bit, size) for flip in range(1, 1 << many)]
    rows, half = total.shape
    return pl.pallas_call(
        join_kernel,
        out_shape=jax.ShapeDtypeStruct((rows << many, half), BF16),
        in_specs=[SCALARS] + [HBM] * len(parts),
        out_specs=pl.BlockSpec(memory_space=pltpu.VMEM),
        scratch_shapes=[pltpu.SemaphoreType.DMA((len(parts),))],
        cost_estimate=NO_COST,
        name="join",
    )(mine.astype(jnp.int32)[None], *parts)


def sum_in_fours(values, step, size):
    flips = (step, 2 * step, 3 * step) if 2 * step < size else (step,)
    return values + sum(
        flipped(values, flip, size) for flip in flips
    )


def finish_kernel(flag, mine, other, grad_in, grad_out, bias_in, bias_out, held, sems):
    rows, half = mine.shape
    copies = [
        pltpu.make_async_copy(part, held.at[pl.ds(aligned(which * rows), rows)], sems.at[number])
        for number, (which, part) in enumerate(((flag[0], mine), (1 - flag[0], other)))
    ]
    for copy in copies:
        copy.start()
    for copy in copies:
        copy.wait()
    wide = 2 * half
    for block in range(2):
        grad_in[block] = held[block * wide : (block + 1) * wide, :].astype(F32)
        for part in range(2):
            first = (2 + block) * wide + part * half
            grad_out[block, :, part * half : (part + 1) * half] = held[first : first + half, :].astype(F32)
    last = held[4 * wide : 4 * wide + GROUP, :].astype(F32)
    bias_in[...] = last[:2]
    bias_out[...] = last[2:4]


def finish(flag, mine, other):
    rows, half = mine.shape
    on_chip = pl.BlockSpec(memory_space=pltpu.VMEM)
    return pl.pallas_call(
        finish_kernel,
        out_shape=(
            jax.ShapeDtypeStruct((2, 2 * half, half), F32),
            jax.ShapeDtypeStruct((2, half, 2 * half), F32),
            jax.ShapeDtypeStruct((2, half), F32),
            jax.ShapeDtypeStruct((2, half), F32),
        ),
        in_specs=[SCALARS] + [HBM] * 2,
        out_specs=(on_chip,) * 4,
        scratch_shapes=[pltpu.VMEM((2 * rows, half), BF16), pltpu.SemaphoreType.DMA((2,))],
        cost_estimate=NO_COST,
        compiler_params=PARAMS,
        name="finish",
    )(flag, mine, other)


def together(*values):
    return lax.optimization_barrier(values)


def local(
    dp_size,
    features,
    tangents,
    weight_in,
    bias_in,
    weight_out,
    bias_out,
    counts,
    cotangent_values,
    cotangent_tangents,
):
    row_count, half = features.shape
    sources = counts.shape[0]
    unit = row_count // 256
    level, first, moved, extra = (unit * part for part in (ROWS, FIRST, MOVED, EXTRA))
    order = chain_order(dp_size)
    bits = dp_size.bit_length() - 1
    dims = (sources, row_count // sources, level, 8 * dp_size)
    side = lax.axis_index("tensor")
    place = lax.axis_index("dp")
    arrays = (features, tangents, cotangent_values, cotangent_tangents)
    middle = (2 * first, level - first - moved)
    last = (2 * (level - moved), moved)

    who, piece = quarter_of(dims, counts, weight_in, weight_out)
    piece_got = swap_tensor(piece)
    bias_got = swap_tensor(jnp.stack([bias_in, bias_out]))
    totals = jnp.where(jnp.arange(dp_size, dtype=jnp.int32) == place, who[TOTAL], 0)
    totals = sum_in_fours(totals, 1, dp_size)
    who, totals = together(who, totals)
    own1, send1 = pack(dims, who, counts, None, arrays, 0, first)
    send1, piece_got, bias_got = together(send1, piece_got, bias_got)
    got1 = swap_tensor(send1)
    pieces = [piece_got] + [flipped(piece_got, flip, dp_size) for flip in (2, 1, 3)]
    who, own1 = together(who, own1)
    own2, send2 = pack(dims, who, counts, None, arrays, *middle)
    got2 = swap_tensor(send2)
    for step in range(2, bits, 2):
        totals = sum_in_fours(totals, 1 << step, dp_size)
    totals, own2 = together(totals, own2)
    plan = make_plan(who, totals, order, level, 2 * first, moved, extra)
    plan, pieces = together(plan, pieces)
    to_left, to_right = export(dims, who, counts, plan, *arrays, moved)
    neighbours = (shift(to_right, order, 1), shift(to_left, order, -1))
    pieces, to_left = together(pieces, to_left)
    weights = assemble(who, weight_in, weight_out, bias_in, bias_out, bias_got, pieces)
    who, weights, neighbours = together(who, weights, neighbours)
    own3, send3 = pack(dims, who, counts, plan, arrays, *last, neighbours)
    got3 = swap_tensor(send3)
    own3, weights, got2 = together(own3, weights, got2)

    def blocks(base, plan, arrived, sums, final=False, merged=False):
        results = run_blocks(dims, who, plan, *arrived, weights, sums, base, final, merged)
        count = 3 if merged else 4
        return results[:count], tuple(results[count:])

    def place_all(outs, base, rows, plan, result, got):
        return unpack(dims, who, counts, plan, result[:2], got, outs, base, rows)

    def place_values(outs, base, rows, own, got):
        return (*unpack(dims, who, counts, plan, [own], got, outs[:2], base, rows), *outs[2:])

    def place_grads(outs, base, rows, own, got):
        return (*outs[:2], *unpack(dims, who, counts, plan, [own], got, outs[2:], base, rows))

    result1, sums = blocks(0, plan, (own1, got1), None)
    later_counts, sums = together(counts, sums)
    outs = blank(later_counts, row_count, half, sources)

    def more(carry):
        return carry[0] < plan[ROUNDS]

    def extra_round(carry):
        number, sums, outs = carry
        done = number * (2 * extra)
        here = plan + jnp.zeros((8,), jnp.int32).at[OVER_FIRST].set(done).at[OVER_LEFT].set(-done)
        own, send = pack(dims, who, counts, here, arrays, OVER, extra)
        result, sums = blocks(OVER, here, (own, swap_tensor(send)), sums, merged=True)
        outs = place_all(outs, OVER, extra, here, result, swap_tensor(result[2]))
        return number + 1, sums, tuple(outs)

    _, sums, outs = lax.while_loop(more, extra_round, (jnp.int32(0), sums, tuple(outs)))
    y1_got, d1_got = swap_tensor(result1[2]), swap_tensor(result1[3])
    result2, sums = blocks(middle[0], plan, (own2, got2), sums, merged=True)
    sums, outs = together(sums, outs)
    result3, sums = blocks(last[0], plan, (own3, got3), sums, final=True)

    sums, y1_got = together(sums, y1_got)
    kept, *sent = sums
    core, across, *others = groups_of(bits)
    came = jnp.stack([flipped(part, 1, dp_size) for part in sent])
    grads = kept + came.astype(F32)
    grads = reduce_step(grads, across, place, dp_size)
    outs = place_values(outs, 0, first, result1[0], y1_got)
    grads, d1_got, outs = together(grads, d1_got, outs)
    for group in others:
        grads = reduce_step(grads, group, place, dp_size)
    outs = place_grads(outs, 0, first, result1[1], d1_got)
    grads, outs = together(grads, outs)
    y3_got = swap_tensor(result3[2])
    mine = lax.dynamic_index_in_dim(grads, side, 0, keepdims=False)
    other = lax.dynamic_index_in_dim(grads, 1 - side, 0, keepdims=False).astype(BF16)
    total = (mine + swap_tensor(other).astype(F32)).astype(BF16)
    total, d3_send, y3_got = together(total, result3[3], y3_got)
    d3_got = swap_tensor(d3_send)
    y_left, y_right = handback(dims, who, plan, result3[0], y3_got, *last, moved)
    y_back = (shift(y_left, order, -1), shift(y_right, order, 1))
    outs = place_values(outs, *last, result3[0], y3_got)
    for group in reversed(others):
        total = gather_step(total, group, place, dp_size)
    total, d3_got, outs = together(total, d3_got, outs)
    yd2_got = swap_tensor(result2[2])
    d_left, d_right = handback(dims, who, plan, result3[1], d3_got, *last, moved)
    d_back = (shift(d_left, order, -1), shift(d_right, order, 1))
    total = gather_step(total, across, place, dp_size)
    outs = place_grads(outs, *last, result3[1], d3_got)
    total, outs = together(total, outs)
    total_got = flipped(total, 1, dp_size)
    outs = place_values(outs, None, moved, *y_back)
    sums = finish((place & 1).astype(jnp.int32)[None], total, total_got)
    outs, sums = together(outs, sums)
    outs = place_grads(outs, None, moved, *d_back)
    outs = place_all(outs, *middle, plan, result2, yd2_got)
    grad_in, grad_out, bias_in_grad, bias_out_grad = sums
    return (*outs, grad_in, bias_in_grad, grad_out, bias_out_grad)


def solution(mesh):
    in_specs = (
        P("dp", "tensor"),
        P(None, "dp", "tensor"),
        P(None, None, "tensor"),
        P(None, "tensor"),
        P(None, "tensor", None),
        P(None, "tensor"),
        P("dp"),
        P("dp", "tensor"),
        P(None, "dp", "tensor"),
    )
    out_specs = (
        P("dp", "tensor"),
        P(None, "dp", "tensor"),
        P("dp", "tensor"),
        P(None, "dp", "tensor"),
        P(None, None, "tensor"),
        P(None, "tensor"),
        P(None, "tensor", None),
        P(None, "tensor"),
    )
    return jax.shard_map(
        functools.partial(local, mesh.shape["dp"]),
        mesh=mesh,
        in_specs=in_specs,
        out_specs=out_specs,
        check_vma=False,
    )
```

time: 2600 us -> 274 us (0.11)
  waiting for transfers between devices: 2200 us -> 72.5 us
  matrix products: 176 us -> 0 us
  other arithmetic: 155 us -> 7.22 us
  Pallas kernels: 0 us -> 129 us
  starting transfers between devices: 1.22 us -> 54.1 us
    reduce_scatter x4 -> x0, waiting for transfers between devices: 1360 us -> none  [the longest x2 704 us: local(): lax.psum_scatter(partial_value, 'tensor', scatter_dimension=2, tiled=True)]
    all_gather x4 -> x0, waiting for transfers between devices: 759 us -> none  [the longest x2 380 us: local(): gathered = lax.all_gather(outgoing, 'tensor', axis=2, tiled=True)]
    dot_general x12 -> x0, matrix products: 176 us -> none  [the longest x2 37.8 us: backward_local(): jnp.einsum('srh,dh->srd', grad_stack, weight, preferred_element_type=jnp....]
    pallas_call x0 -> x23, Pallas kernels: none -> 129 us  [the longest x3 61.6 us: run_blocks(): pl.pallas_call(functools.partial(blocks_kernel, dims, base, rows, tile, f...]
    psum x1 -> x0, waiting for transfers between devices: 85.4 us -> none  [local(): grad_first, grad_bias, grad_second, grad_out_bias = lax.psum(stacked, 'dp')]
    ppermute x0 -> x37, waiting for transfers between devices: none -> 72.5 us  [the longest x11 27.4 us: swap_tensor(): return lax.ppermute(value, 'tensor', [(0, 1), (1, 0)])]
    convert_element_type x3 -> x1, other arithmetic: 59.8 us -> 0.02 us  [local(): total = (mine + swap_tensor(other).astype(F32)).astype(BF16)]
    ppermute x0 -> x37, starting transfers between devices: none -> 54.1 us  [the longest x20 23.5 us: flipped(): return lax.ppermute(value, 'dp', [(i, i ^ flip) for i in range(size)])]
  transfers between devices with their start and end apart: 9 -> 37, of which waited for: 9 -> 15; matrix products, arithmetic and copies ran while one was open for 6% -> 3% of each run, Pallas kernels for 0% -> 45%
where the time goes in v2:
time: 274 us; the launch traced here: 272 us
  Pallas kernels  129 us (47%)
  waiting for transfers between devices  72.5 us (26%)
  starting transfers between devices  54.1 us (20%)
  other arithmetic  7.22 us (3%)
  local copies, waits for them, and re-layouts  7.18 us (3%)
    pallas_call x3, Pallas kernels, run_blocks(): pl.pallas_call(functools.partial(blocks_kernel, dims, base, rows, tile, f...  61.6 us
    ppermute x11, waiting for transfers between devices, swap_tensor(): return lax.ppermute(value, 'tensor', [(0, 1), (1, 0)])  27.4 us
    ppermute x20, waiting for transfers between devices, flipped(): return lax.ppermute(value, 'dp', [(i, i ^ flip) for i in range(size)])  25.8 us
    pallas_call x7, Pallas kernels, unpack(): pl.pallas_call(functools.partial(unpack_kernel, dims, base, rows, streams...  25.2 us
    ppermute x20, starting transfers between devices, flipped(): return lax.ppermute(value, 'dp', [(i, i ^ flip) for i in range(size)])  23.5 us
    ppermute x6, waiting for transfers between devices, shift(): lax.ppermute(value, 'dp', pairs if step == 1 else [(b, a) for a, b in pai...  19.3 us
    ppermute x6, starting transfers between devices, shift(): lax.ppermute(value, 'dp', pairs if step == 1 else [(b, a) for a, b in pai...  17.2 us
    pallas_call x3, Pallas kernels, pack(): pl.pallas_call(functools.partial(pack_kernel, dims, base, rows, len(neigh...  14.6 us
  transfers between devices with their start and end apart: 37, of which 15 were waited for; matrix products, arithmetic and copies ran while one was open for 3% of the time, Pallas kernels for 45%

profile of v2, /device:TPU:10, one launch (start us, length us, event | category | flops | bytes accessed | tf_op | source)
XLA Modules:
  0.0 272.3 jit_solution(2034430422101445783)
XLA Ops:
  9.7 5.7 %pack.8 = (bf16[8,576,256]{2,1,0:T(8,128)(2,1)}, bf16[8,576,256]{2,1,0:T(8,128)(2,1)}) custom-call(s32[8]{0:T(128)S(1)} %get-tuple-element.799.who, s32[16]{0:T(128)} %counts.24, bf16[4096,256]{1,0:T(8,128)(2,1)} %refs_1_.5, bf16[3,4096,256]{2,1,0:T(8,128)(2,1)} %refs_2_.5, bf16[4096,256]{1,0:T(8,128)(2,1)} %refs_3_.5, bf16[3,4096,256]{2,1,0:T(8,128)(2,1)} %refs_4_.1), custom_call_target="tpu_custom_call" | custom-call | bytes 1024 | tf_op jit(solution)/shard_map/pack/pallas_call | solution.py:271
  26.4 4.2 %collective-permute-start.8 = (s32[16]{0:T(128)S(1)}, s32[16]{0:T(128)S(1)}, u32[]{:S(2)}, u32[]{:S(2)}) collective-permute-start(s32[16]{0:T(128)S(1)} %add_add_fusion.1), channel_id=1, source_target_pairs={{0,16},{2,18},{4,20},{6,22},{8,24},{10,26},{12,28},{14,30},{16,0},... | collective-permute-start | bytes 200 | tf_op jit(solution)/shard_map/ppermute | solution.py:810
  30.7 3.8 %pack.9 = (bf16[8,256,256]{2,1,0:T(8,128)(2,1)}, bf16[8,256,256]{2,1,0:T(8,128)(2,1)}) custom-call(s32[8]{0:T(128)S(1)} %get-tuple-element.799.who, s32[16]{0:T(128)S(1)} %copy-done.16, bf16[4096,256]{1,0:T(8,128)(2,1)S(1)} %copy-done, bf16[3,4096,256]{2,1,0:T(8,128)(2,1)} %refs_2_.5, bf16[4096,256]{1,0:T(8,128)(2,1)} %refs_3_.5, bf16[3,4096,256]{2,1,0:T(8,128)(2,1)} %refs_4_.1), custom_call_target="tpu_custom_call" | custom-call | bytes 1024 | tf_op jit(solution)/shard_map/pack/pallas_call | solution.py:271
  36.6 4.4 %export.1 = (bf16[8,448,256]{2,1,0:T(8,128)(2,1)}, bf16[8,448,256]{2,1,0:T(8,128)(2,1)}) custom-call(s32[8]{0:T(128)S(1)} %get-tuple-element.799.who, s32[16]{0:T(128)S(1)} %copy-done.16, s32[8]{0:T(128)} %plan.1.refs_0_.rest_0_, bf16[4096,256]{1,0:T(8,128)(2,1)S(1)} %copy-done, bf16[3,4096,256]{2,1,0:T(8,128)(2,1)} %refs_2_.5, bf16[4096,256]{1,0:T(8,128)(2,1)} %refs_3_.5, ...), custom_call_target="tpu_custom_call" | custom-call | bytes 1024 | tf_op jit(solution)/shard_map/export/pallas_call | solution.py:312
  43.0 3.9 %collective-permute-start.14 = (bf16[8,448,256]{2,1,0:T(8,128)(2,1)}, bf16[8,448,256]{2,1,0:T(8,128)(2,1)}, u32[]{:S(2)}, u32[]{:S(2)}) collective-permute-start(bf16[8,448,256]{2,1,0:T(8,128)(2,1)} %get-tuple-element.482), channel_id=1, source_target_pairs={{2,0},{6,2},{4,6},{12,4},{14,12},{10,14},{8,10},{16,8},{18,16},{22... | collective-permute-start | bytes 5505032 | tf_op jit(solution)/shard_map/ppermute | solution.py:704
  47.5 4.6 %assemble.1 = (bf16[2,512,512]{2,1,0:T(8,128)(2,1)S(1)}, bf16[2,512,512]{2,1,0:T(8,128)(2,1)}, bf16[2,512,512]{2,1,0:T(8,128)(2,1)}, bf16[2,512,512]{2,1,0:T(8,128)(2,1)}, f32[2,2,512]{2,1,0:T(2,128)S(1)}) custom-call(s32[8]{0:T(128)S(1)} %get-tuple-element.799.who, bf16[2,512,256]{2,1,0:T(8,128)(2,1)} %w_in.3, bf16[2,256,512]{2,1,0:T(8,128)(2,1)} %w_out.3, ...), custom_call_target="tpu_custom_call" | custom-call | bytes 1024 | tf_op jit(solution)/shard_map/assemble/pallas_call | solution.py:797
  52.1 14.4 %collective-permute-done.13.refs_5_ = bf16[8,448,256]{2,1,0:T(8,128)(2,1)} collective-permute-done((bf16[8,448,256]{2,1,0:T(8,128)(2,1)}, bf16[8,448,256]{2,1,0:T(8,128)(2,1)}, u32[]{:S(2)}, u32[]{:S(2)}) %collective-permute-start.13) | collective-permute-done | bytes 1835040 | tf_op jit(solution)/shard_map/ppermute | solution.py:704
  68.0 5.1 %pack.10 = (bf16[8,448,256]{2,1,0:T(8,128)(2,1)}, bf16[8,448,256]{2,1,0:T(8,128)(2,1)}) custom-call(s32[8]{0:T(128)S(1)} %get-tuple-element.799.who, s32[16]{0:T(128)S(1)} %copy-done.16, s32[8]{0:T(128)} %plan.1.refs_0_.rest_0_, bf16[4096,256]{1,0:T(8,128)(2,1)S(1)} %copy-done, bf16[3,4096,256]{2,1,0:T(8,128)(2,1)} %refs_2_.5, bf16[4096,256]{1,0:T(8,128)(2,1)} %refs_3_.5, ...), custom_call_target="tpu_custom_call" | custom-call | bytes 1024 | tf_op jit(solution)/shard_map/pack/pallas_call | solution.py:271
  73.0 17.7 %collective-permute-done.15.got = bf16[8,256,256]{2,1,0:T(8,128)(2,1)} collective-permute-done((bf16[8,256,256]{2,1,0:T(8,128)(2,1)}, bf16[8,256,256]{2,1,0:T(8,128)(2,1)}, u32[]{:S(2)}, u32[]{:S(2)}) %collective-permute-start.15) | collective-permute-done | bytes 1048608 | tf_op jit(solution)/shard_map/ppermute | solution.py:699
  92.2 24.5 %blocks.8 = (bf16[4,576,256]{2,1,0:T(8,128)(2,1)}, bf16[4,576,256]{2,1,0:T(8,128)(2,1)}, bf16[4,576,256]{2,1,0:T(8,128)(2,1)}, bf16[4,576,256]{2,1,0:T(8,128)(2,...) custom-call(s32[8]{0:T(128)S(1)} %get-tuple-element.799.who, bf16[8,576,256]{2,1,0:T(8,128)(2,1)} %get-tuple-element.510.own, ...), custom_call_target="tpu_custom_call" | custom-call | flops 40320000000 | bytes 1024 | tf_op jit(solution)/shard_map/blocks/pallas_call | solution.py:672
  117.3 2.8 %blank.1 = (bf16[4096,256]{1,0:T(8,128)(2,1)}, bf16[3,4096,256]{2,1,0:T(8,128)(2,1)}, bf16[4096,256]{1,0:T(8,128)(2,1)}, bf16[3,4096,256]{2,1,0:T(8,128)(2,1)}) custom-call(s32[16]{0:T(128)S(1)} %copy-done.16), custom_call_target="tpu_custom_call" | custom-call | bytes 1024 | tf_op jit(solution)/shard_map/blank/pallas_call | solution.py:481
  120.9 15.2 %blocks.9 = (bf16[4,256,256]{2,1,0:T(8,128)(2,1)}, bf16[4,256,256]{2,1,0:T(8,128)(2,1)}, bf16[8,256,256]{2,1,0:T(8,128)(2,1)}, f32[2,2176,256]{2,1,0:T(8,128)}, f32[4,8,512]{2,1,0:T(8,128)S(1)}) custom-call(s32[8]{0:T(128)S(1)} %get-tuple-element.868, bf16[8,256,256]{2,1,0:T(8,128)(2,1)} %get-tuple-element.494.own, ...), custom_call_target="tpu_custom_call", output_to_operand_aliasing={{3}: (9, {}), {4}: (10, {})} | custom-call | bytes 1024 | tf_op jit(solution)/shard_map/blocks/pallas_call | solution.py:672
  136.2 22.0 %blocks.10 = (bf16[4,448,256]{2,1,0:T(8,128)(2,1)}, bf16[4,448,256]{2,1,0:T(8,128)(2,1)}, bf16[4,448,256]{2,1,0:T(8,128)(2,1)}, bf16[4,448,256]{2,1,0:T(8,128)(2...) custom-call(s32[8]{0:T(128)S(1)} %get-tuple-element.868, ...), custom_call_target="tpu_custom_call" | custom-call | bytes 1024 | tf_op jit(solution)/shard_map/blocks/pallas_call | solution.py:672
  167.4 4.9 %unpack.12 = (bf16[4096,256]{1,0:T(8,128)(2,1)S(1)}, bf16[3,4096,256]{2,1,0:T(8,128)(2,1)}) custom-call(s32[8]{0:T(128)S(1)} %get-tuple-element.868, s32[16]{0:T(128)S(1)} %get-tuple-element.881, s32[8]{0:T(128)} %plan.1.refs_0_.rest_0_, bf16[4,576,256]{2,1,0:T(8,128)(2,1)} %get-tuple-element.545.refs_0_, ...), custom_call_target="tpu_custom_call", output_to_operand_aliasing={{0}: (5, {}), {1}: (6, {})} | custom-call | bytes 1024 | tf_op jit(solution)/shard_map/unpack/pallas_call | solution.py:431
  172.3 8.1 %collective-permute-done.22 = bf16[2,544,256]{2,1,0:T(8,128)(2,1)} collective-permute-done((bf16[2,544,256]{2,1,0:T(8,128)(2,1)}, bf16[2,544,256]{2,1,0:T(8,128)(2,1)}, u32[]{:S(2)}, u32[]{:S(2)}) %collective-permute-start.22) | collective-permute-done | bytes 557088 | tf_op jit(solution)/shard_map/ppermute | solution.py:810
  181.9 6.0 %collective-permute-done.23.refs_1_ = bf16[4,576,256]{2,1,0:T(8,128)(2,1)} collective-permute-done((bf16[4,576,256]{2,1,0:T(8,128)(2,1)}, bf16[4,576,256]{2,1,0:T(8,128)(2,1)}, u32[]{:S(2)}, u32[]{:S(2)}) %collective-permute-start.23) | collective-permute-done | bytes 1179680 | tf_op jit(solution)/shard_map/ppermute | solution.py:699
  192.9 3.8 %unpack.13 = (bf16[4096,256]{1,0:T(8,128)(2,1)}, bf16[3,4096,256]{2,1,0:T(8,128)(2,1)}) custom-call(s32[8]{0:T(128)S(1)} %get-tuple-element.868, s32[16]{0:T(128)S(1)} %get-tuple-element.881, s32[8]{0:T(128)} %plan.1.refs_0_.rest_0_, bf16[4,576,256]{2,1,0:T(8,128)(2,1)} %get-tuple-element.556.refs_0_, ...), custom_call_target="tpu_custom_call", output_to_operand_aliasing={{0}: (5, {}), {1}: (6, {})} | custom-call | bytes 1024 | tf_op jit(solution)/shard_map/unpack/pallas_call | solution.py:431
  196.7 3.3 %collective-permute-done.26 = bf16[2,136,256]{2,1,0:T(8,128)(2,1)S(1)} collective-permute-done((bf16[2,136,256]{2,1,0:T(8,128)(2,1)}, bf16[2,136,256]{2,1,0:T(8,128)(2,1)S(1)}, u32[]{:S(2)}, u32[]{:S(2)}) %collective-permute-start.26) | collective-permute-done | bytes 139296 | tf_op jit(solution)/shard_map/ppermute | solution.py:810
  204.2 3.8 %collective-permute-done.27 = bf16[136,256]{1,0:T(8,128)(2,1)S(1)} collective-permute-done((bf16[136,256]{1,0:T(8,128)(2,1)S(1)}, bf16[136,256]{1,0:T(8,128)(2,1)S(1)}, u32[]{:S(2)}, u32[]{:S(2)}) %collective-permute-start.27) | collective-permute-done | bytes 69664 | tf_op jit(solution)/shard_map/ppermute | solution.py:699
  209.7 3.0 %handback.2 = (bf16[4,448,256]{2,1,0:T(8,128)(2,1)}, bf16[4,448,256]{2,1,0:T(8,128)(2,1)}) custom-call(s32[8]{0:T(128)S(1)} %get-tuple-element.868, s32[8]{0:T(128)} %plan.1.refs_0_.rest_0_, bf16[4,448,256]{2,1,0:T(8,128)(2,1)} %get-tuple-element.536.mine.refs_0_, bf16[4,448,256]{2,1,0:T(8,128)(2,1)} %copy-done.7), custom_call_target="tpu_custom_call" | custom-call | bytes 1024 | tf_op jit(solution)/shard_map/handback/pallas_call | solution.py:355
  212.7 3.5 %collective-permute-start.29 = (bf16[4,448,256]{2,1,0:T(8,128)(2,1)}, bf16[4,448,256]{2,1,0:T(8,128)(2,1)}, u32[]{:S(2)}, u32[]{:S(2)}) collective-permute-start(bf16[4,448,256]{2,1,0:T(8,128)(2,1)} %get-tuple-element.566), channel_id=1, source_target_pairs={{2,0},{6,2},{4,6},{12,4},{14,12},{10,14},{8,10},{16,8},{18,16},{22... | collective-permute-start | bytes 2752520 | tf_op jit(solution)/shard_map/ppermute | solution.py:704
  219.7 3.4 %unpack.14 = (bf16[4096,256]{1,0:T(8,128)(2,1)S(1)}, bf16[3,4096,256]{2,1,0:T(8,128)(2,1)}) custom-call(s32[8]{0:T(128)S(1)} %get-tuple-element.868, s32[16]{0:T(128)S(1)} %get-tuple-element.881, s32[8]{0:T(128)} %plan.1.refs_0_.rest_0_, bf16[4,448,256]{2,1,0:T(8,128)(2,1)} %get-tuple-element.536.mine.refs_0_, ...), custom_call_target="tpu_custom_call", output_to_operand_aliasing={{0}: (5, {}), {1}: (6, {})} | custom-call | bytes 1024 | tf_op jit(solution)/shard_map/unpack/pallas_call | solution.py:431
  223.1 7.1 %collective-permute-done.31.refs_1_ = bf16[136,256]{1,0:T(8,128)(2,1)S(1)} collective-permute-done((bf16[136,256]{1,0:T(8,128)(2,1)S(1)}, bf16[136,256]{1,0:T(8,128)(2,1)S(1)}, u32[]{:S(2)}, u32[]{:S(2)}) %collective-permute-start.31) | collective-permute-done | bytes 69664 | tf_op jit(solution)/shard_map/ppermute | solution.py:810
  234.6 2.4 collective-permute-start.35
  239.8 3.0 %handback.3 = (bf16[4,448,256]{2,1,0:T(8,128)(2,1)}, bf16[4,448,256]{2,1,0:T(8,128)(2,1)}) custom-call(s32[8]{0:T(128)S(1)} %get-tuple-element.868, s32[8]{0:T(128)} %plan.1.refs_0_.rest_0_, bf16[4,448,256]{2,1,0:T(8,128)(2,1)} %get-tuple-element.579.refs_0_.mine, bf16[4,448,256]{2,1,0:T(8,128)(2,1)} %collective-permute-done.34.refs_1_.theirs), custom_call_target="tpu_custom_call" | custom-call | bytes 1024 | tf_op jit(solution)/shard_map/handback/pallas_call | solution.py:355
  242.8 4.1 %collective-permute-start.37 = (bf16[4,448,256]{2,1,0:T(8,128)(2,1)}, bf16[4,448,256]{2,1,0:T(8,128)(2,1)}, u32[]{:S(2)}, u32[]{:S(2)}) collective-permute-start(bf16[4,448,256]{2,1,0:T(8,128)(2,1)} %get-tuple-element.598), channel_id=1, source_target_pairs={{2,0},{6,2},{4,6},{12,4},{14,12},{10,14},{8,10},{16,8},{18,16},{22... | collective-permute-start | bytes 2752520 | tf_op jit(solution)/shard_map/ppermute | solution.py:704
  248.8 3.2 %unpack.15 = (bf16[4096,256]{1,0:T(8,128)(2,1)}, bf16[3,4096,256]{2,1,0:T(8,128)(2,1)}) custom-call(s32[8]{0:T(128)S(1)} %get-tuple-element.868, s32[16]{0:T(128)S(1)} %get-tuple-element.881, s32[8]{0:T(128)} %plan.1.refs_0_.rest_0_, bf16[4,448,256]{2,1,0:T(8,128)(2,1)} %get-tuple-element.579.refs_0_.mine, ...), custom_call_target="tpu_custom_call", output_to_operand_aliasing={{0}: (5, {}), {1}: (6, {})} | custom-call | bytes 1024 | tf_op jit(solution)/shard_map/unpack/pallas_call | solution.py:431
  254.0 3.2 %unpack.16 = (bf16[4096,256]{1,0:T(8,128)(2,1)S(1)}, bf16[3,4096,256]{2,1,0:T(8,128)(2,1)}) custom-call(s32[8]{0:T(128)S(1)} %get-tuple-element.868, s32[16]{0:T(128)S(1)} %get-tuple-element.881, s32[8]{0:T(128)} %plan.1.refs_0_.rest_0_, bf16[4,448,256]{2,1,0:T(8,128)(2,1)} %collective-permute-done.29.refs_0_, ...), custom_call_target="tpu_custom_call", output_to_operand_aliasing={{0}: (5, {}), {1}: (6, {})} | custom-call | bytes 1024 | tf_op jit(solution)/shard_map/unpack/pallas_call | solution.py:431
  257.2 2.6 finish.1
  259.9 3.4 %collective-permute-done.38.refs_1_ = bf16[4,448,256]{2,1,0:T(8,128)(2,1)} collective-permute-done((bf16[4,448,256]{2,1,0:T(8,128)(2,1)}, bf16[4,448,256]{2,1,0:T(8,128)(2,1)}, u32[]{:S(2)}, u32[]{:S(2)}) %collective-permute-start.38) | collective-permute-done | bytes 917536 | tf_op jit(solution)/shard_map/ppermute | solution.py:704
  263.3 3.1 %unpack.17 = (bf16[4096,256]{1,0:T(8,128)(2,1)}, bf16[3,4096,256]{2,1,0:T(8,128)(2,1)}) custom-call(s32[8]{0:T(128)S(1)} %get-tuple-element.868, s32[16]{0:T(128)S(1)} %get-tuple-element.881, s32[8]{0:T(128)} %plan.1.refs_0_.rest_0_, bf16[4,448,256]{2,1,0:T(8,128)(2,1)} %collective-permute-done.37.refs_0_, ...), custom_call_target="tpu_custom_call", output_to_operand_aliasing={{0}: (5, {}), {1}: (6, {})} | custom-call | bytes 1024 | tf_op jit(solution)/shard_map/unpack/pallas_call | solution.py:431
  267.4 3.6 %unpack.18 = (bf16[4096,256]{1,0:T(8,128)(2,1)S(1)}, bf16[3,4096,256]{2,1,0:T(8,128)(2,1)}, bf16[4096,256]{1,0:T(8,128)(2,1)}, bf16[3,4096,256]{2,1,0:T(8,128)(2,1)}) custom-call(s32[8]{0:T(128)S(1)} %get-tuple-element.868, s32[16]{0:T(128)S(1)} %get-tuple-element.881, ...), custom_call_target="tpu_custom_call", output_to_operand_aliasing={{0}: (6, {}), {1}: (7, {}), {2}: (8, {}), {3}: (9, {})} | custom-call | bytes 1024 | tf_op jit(solution)/shard_map/unpack/pallas_call | solution.py:431
  (120 shorter events, 67.3 us)
Async XLA Ops:
  4.1 4.9 %collective-permute-start.4 = (s32[16]{0:T(128)S(1)}, s32[16]{0:T(128)S(1)}, u32[]{:S(2)}, u32[]{:S(2)}) collective-permute-start(s32[16]{0:T(128)S(1)} %compare_select_fusion), channel_id=1, source_target_pairs={{0,6},{2,4},{4,2},{6,0},{8,14},{10,12},{12,10},{14,8},{16,22},{18,... | collective-permute-start | bytes 200 | tf_op jit(solution)/shard_map/ppermute | solution.py:810
  4.1 4.9 %collective-permute-start.2 = (s32[16]{0:T(128)S(1)}, s32[16]{0:T(128)S(1)}, u32[]{:S(2)}, u32[]{:S(2)}) collective-permute-start(s32[16]{0:T(128)S(1)} %compare_select_fusion), channel_id=1, source_target_pairs={{0,2},{2,0},{4,6},{6,4},{8,10},{10,8},{12,14},{14,12},{16,18},{18,... | collective-permute-start | bytes 200 | tf_op jit(solution)/shard_map/ppermute | solution.py:810
  4.8 4.2 %collective-permute-start.3 = (s32[16]{0:T(128)S(1)}, s32[16]{0:T(128)S(1)}, u32[]{:S(2)}, u32[]{:S(2)}) collective-permute-start(s32[16]{0:T(128)S(1)} %compare_select_fusion), channel_id=1, source_target_pairs={{0,4},{2,6},{4,0},{6,2},{8,12},{10,14},{12,8},{14,10},{16,20},{18,... | collective-permute-start | bytes 200 | tf_op jit(solution)/shard_map/ppermute | solution.py:810
  6.3 9.2 %collective-permute-start.5 = (bf16[512,256]{1,0:T(8,128)(2,1)}, bf16[512,256]{1,0:T(8,128)(2,1)S(1)}, u32[]{:S(2)}, u32[]{:S(2)}) collective-permute-start(bf16[512,256]{1,0:T(8,128)(2,1)} %get-tuple-element.471), channel_id=1, source_target_pairs={{0,1},{1,0},{2,3},{3,2},{4,5},{5,4},{6,7},{7,6},{8,9},{9,8},{10,11... | collective-permute-start | bytes 786440 | tf_op jit(solution)/shard_map/ppermute | solution.py:699
  8.5 6.9 %collective-permute-start.6 = (f32[2,2,256]{2,1,0:T(2,128)S(1)}, f32[2,2,256]{2,1,0:T(2,128)S(1)}, u32[]{:S(2)}, u32[]{:S(2)}) collective-permute-start(f32[2,2,256]{2,1,0:T(2,128)S(1)} %pad_maximum_fusion), channel_id=1, source_target_pairs={{0,1},{1,0},{2,3},{3,2},{4,5},{5,4},{6,7},{7,6},{8,9},{9,8},{10,11... | collective-permute-start | bytes 12296 | tf_op jit(solution)/shard_map/ppermute | solution.py:699
  15.5 76.8 %collective-permute-start.16 = (bf16[8,576,256]{2,1,0:T(8,128)(2,1)}, bf16[8,576,256]{2,1,0:T(8,128)(2,1)}, u32[]{:S(2)}, u32[]{:S(2)}) collective-permute-start(bf16[8,576,256]{2,1,0:T(8,128)(2,1)} %get-tuple-element.511), channel_id=1, source_target_pairs={{0,1},{1,0},{2,3},{3,2},{4,5},{5,4},{6,7},{7,6},{8,9},{9,8},{10,11... | collective-permute-start | bytes 7077896 | tf_op jit(solution)/shard_map/ppermute | solution.py:699
  17.1 19.5 %collective-permute-start.10 = (bf16[512,256]{1,0:T(8,128)(2,1)S(1)}, bf16[512,256]{1,0:T(8,128)(2,1)S(1)}, u32[]{:S(2)}, u32[]{:S(2)}) collective-permute-start(bf16[512,256]{1,0:T(8,128)(2,1)S(1)} %collective-permute-done.5.refs_0_), channel_id=1, source_target_pairs={{0,4},{2,6},{4,0},{6,2},{8,12},{10,14},{12,8},{14,10},{16,20},{18,... | collective-permute-start | bytes 786440 | tf_op jit(solution)/shard_map/ppermute | solution.py:810
  17.9 18.7 %collective-permute-start.11 = (bf16[512,256]{1,0:T(8,128)(2,1)S(1)}, bf16[512,256]{1,0:T(8,128)(2,1)S(1)}, u32[]{:S(2)}, u32[]{:S(2)}) collective-permute-start(bf16[512,256]{1,0:T(8,128)(2,1)S(1)} %collective-permute-done.5.refs_0_), channel_id=1, source_target_pairs={{0,2},{2,0},{4,6},{6,4},{8,10},{10,8},{12,14},{14,12},{16,18},{18,... | collective-permute-start | bytes 786440 | tf_op jit(solution)/shard_map/ppermute | solution.py:810
  17.9 18.7 %collective-permute-start.12 = (bf16[512,256]{1,0:T(8,128)(2,1)S(1)}, bf16[512,256]{1,0:T(8,128)(2,1)S(1)}, u32[]{:S(2)}, u32[]{:S(2)}) collective-permute-start(bf16[512,256]{1,0:T(8,128)(2,1)S(1)} %collective-permute-done.5.refs_0_), channel_id=1, source_target_pairs={{0,6},{2,4},{4,2},{6,0},{8,14},{10,12},{12,10},{14,8},{16,22},{18,... | collective-permute-start | bytes 786440 | tf_op jit(solution)/shard_map/ppermute | solution.py:810
  26.4 8.0 %collective-permute-start.8 = (s32[16]{0:T(128)S(1)}, s32[16]{0:T(128)S(1)}, u32[]{:S(2)}, u32[]{:S(2)}) collective-permute-start(s32[16]{0:T(128)S(1)} %add_add_fusion.1), channel_id=1, source_target_pairs={{0,16},{2,18},{4,20},{6,22},{8,24},{10,26},{12,28},{14,30},{16,0},... | collective-permute-start | bytes 200 | tf_op jit(solution)/shard_map/ppermute | solution.py:810
  41.1 25.4 %collective-permute-start.13 = (bf16[8,448,256]{2,1,0:T(8,128)(2,1)}, bf16[8,448,256]{2,1,0:T(8,128)(2,1)}, u32[]{:S(2)}, u32[]{:S(2)}) collective-permute-start(bf16[8,448,256]{2,1,0:T(8,128)(2,1)} %get-tuple-element.492), channel_id=1, source_target_pairs={{0,2},{2,6},{6,4},{4,12},{12,14},{14,10},{10,8},{8,16},{16,18},{18... | collective-permute-start | bytes 5505032 | tf_op jit(solution)/shard_map/ppermute | solution.py:704
  43.0 25.0 %collective-permute-start.14 = (bf16[8,448,256]{2,1,0:T(8,128)(2,1)}, bf16[8,448,256]{2,1,0:T(8,128)(2,1)}, u32[]{:S(2)}, u32[]{:S(2)}) collective-permute-start(bf16[8,448,256]{2,1,0:T(8,128)(2,1)} %get-tuple-element.482), channel_id=1, source_target_pairs={{2,0},{6,2},{4,6},{12,4},{14,12},{10,14},{8,10},{16,8},{18,16},{22... | collective-permute-start | bytes 5505032 | tf_op jit(solution)/shard_map/ppermute | solution.py:704
  46.9 43.8 %collective-permute-start.15 = (bf16[8,256,256]{2,1,0:T(8,128)(2,1)}, bf16[8,256,256]{2,1,0:T(8,128)(2,1)}, u32[]{:S(2)}, u32[]{:S(2)}) collective-permute-start(bf16[8,256,256]{2,1,0:T(8,128)(2,1)} %get-tuple-element.503), channel_id=1, source_target_pairs={{0,1},{1,0},{2,3},{3,2},{4,5},{5,4},{6,7},{7,6},{8,9},{9,8},{10,11... | collective-permute-start | bytes 3145736 | tf_op jit(solution)/shard_map/ppermute | solution.py:699
  90.7 45.4 %collective-permute-start.18 = (bf16[8,448,256]{2,1,0:T(8,128)(2,1)}, bf16[8,448,256]{2,1,0:T(8,128)(2,1)}, u32[]{:S(2)}, u32[]{:S(2)}) collective-permute-start(bf16[8,448,256]{2,1,0:T(8,128)(2,1)} %get-tuple-element.527), channel_id=1, source_target_pairs={{0,1},{1,0},{2,3},{3,2},{4,5},{5,4},{6,7},{7,6},{8,9},{9,8},{10,11... | collective-permute-start | bytes 5505032 | tf_op jit(solution)/shard_map/ppermute | solution.py:699
  116.7 41.4 %collective-permute-start.19 = (bf16[4,576,256]{2,1,0:T(8,128)(2,1)}, bf16[4,576,256]{2,1,0:T(8,128)(2,1)}, u32[]{:S(2)}, u32[]{:S(2)}) collective-permute-start(bf16[4,576,256]{2,1,0:T(8,128)(2,1)} %get-tuple-element.540), channel_id=1, source_target_pairs={{0,1},{1,0},{2,3},{3,2},{4,5},{5,4},{6,7},{7,6},{8,9},{9,8},{10,11... | collective-permute-start | bytes 3538952 | tf_op jit(solution)/shard_map/ppermute | solution.py:699
  158.7 29.1 %collective-permute-start.23 = (bf16[4,576,256]{2,1,0:T(8,128)(2,1)}, bf16[4,576,256]{2,1,0:T(8,128)(2,1)}, u32[]{:S(2)}, u32[]{:S(2)}) collective-permute-start(bf16[4,576,256]{2,1,0:T(8,128)(2,1)} %get-tuple-element.544), channel_id=1, source_target_pairs={{0,1},{1,0},{2,3},{3,2},{4,5},{5,4},{6,7},{7,6},{8,9},{9,8},{10,11... | collective-permute-start | bytes 3538952 | tf_op jit(solution)/shard_map/ppermute | solution.py:699
  165.4 15.0 %collective-permute-start.22 = (bf16[2,544,256]{2,1,0:T(8,128)(2,1)}, bf16[2,544,256]{2,1,0:T(8,128)(2,1)}, u32[]{:S(2)}, u32[]{:S(2)}) collective-permute-start(bf16[2,544,256]{2,1,0:T(8,128)(2,1)} %dynamic-slice_convert_fusion), channel_id=1, source_target_pairs={{0,4},{2,6},{4,0},{6,2},{8,12},{10,14},{12,8},{14,10},{16,20},{18,... | collective-permute-start | bytes 1671176 | tf_op jit(solution)/shard_map/ppermute | solution.py:810
  165.8 42.3 %collective-permute-start.28 = (bf16[4,448,256]{2,1,0:T(8,128)(2,1)}, bf16[4,448,256]{2,1,0:T(8,128)(2,1)S(1)}, u32[]{:S(2)}, u32[]{:S(2)}) collective-permute-start(bf16[4,448,256]{2,1,0:T(8,128)(2,1)} %get-tuple-element.564), channel_id=1, source_target_pairs={{0,1},{1,0},{2,3},{3,2},{4,5},{5,4},{6,7},{7,6},{8,9},{9,8},{10,11... | collective-permute-start | bytes 2752520 | tf_op jit(solution)/shard_map/ppermute | solution.py:699
  188.6 11.4 %collective-permute-start.26 = (bf16[2,136,256]{2,1,0:T(8,128)(2,1)}, bf16[2,136,256]{2,1,0:T(8,128)(2,1)S(1)}, u32[]{:S(2)}, u32[]{:S(2)}) collective-permute-start(bf16[2,136,256]{2,1,0:T(8,128)(2,1)} %get-tuple-element.651), channel_id=1, source_target_pairs={{0,24},{2,26},{4,28},{6,30},{8,16},{10,18},{12,20},{14,22},{16,8},... | collective-permute-start | bytes 417800 | tf_op jit(solution)/shard_map/ppermute | solution.py:810
  189.8 11.0 %collective-permute-start.25 = (bf16[2,136,256]{2,1,0:T(8,128)(2,1)}, bf16[2,136,256]{2,1,0:T(8,128)(2,1)S(1)}, u32[]{:S(2)}, u32[]{:S(2)}) collective-permute-start(bf16[2,136,256]{2,1,0:T(8,128)(2,1)} %get-tuple-element.652), channel_id=1, source_target_pairs={{0,16},{2,18},{4,20},{6,22},{8,24},{10,26},{12,28},{14,30},{16,0},... | collective-permute-start | bytes 417800 | tf_op jit(solution)/shard_map/ppermute | solution.py:810
  191.8 9.6 %collective-permute-start.24 = (bf16[2,136,256]{2,1,0:T(8,128)(2,1)S(1)}, bf16[2,136,256]{2,1,0:T(8,128)(2,1)}, u32[]{:S(2)}, u32[]{:S(2)}) collective-permute-start(bf16[2,136,256]{2,1,0:T(8,128)(2,1)S(1)} %get-tuple-element.650), channel_id=1, source_target_pairs={{0,8},{2,10},{4,12},{6,14},{8,0},{10,2},{12,4},{14,6},{16,24},{18,... | collective-permute-start | bytes 417800 | tf_op jit(solution)/shard_map/ppermute | solution.py:810
  202.7 5.4 %collective-permute-start.27 = (bf16[136,256]{1,0:T(8,128)(2,1)S(1)}, bf16[136,256]{1,0:T(8,128)(2,1)S(1)}, u32[]{:S(2)}, u32[]{:S(2)}) collective-permute-start(bf16[136,256]{1,0:T(8,128)(2,1)S(1)} %fusion.1), channel_id=1, source_target_pairs={{0,1},{1,0},{2,3},{3,2},{4,5},{5,4},{6,7},{7,6},{8,9},{9,8},{10,11... | collective-permute-start | bytes 208904 | tf_op jit(solution)/shard_map/ppermute | solution.py:699
  208.1 26.5 %collective-permute-start.34 = (bf16[4,448,256]{2,1,0:T(8,128)(2,1)}, bf16[4,448,256]{2,1,0:T(8,128)(2,1)}, u32[]{:S(2)}, u32[]{:S(2)}) collective-permute-start(bf16[4,448,256]{2,1,0:T(8,128)(2,1)} %get-tuple-element.569), channel_id=1, source_target_pairs={{0,1},{1,0},{2,3},{3,2},{4,5},{5,4},{6,7},{7,6},{8,9},{9,8},{10,11... | collective-permute-start | bytes 2752520 | tf_op jit(solution)/shard_map/ppermute | solution.py:699
  212.7 41.3 %collective-permute-start.29 = (bf16[4,448,256]{2,1,0:T(8,128)(2,1)}, bf16[4,448,256]{2,1,0:T(8,128)(2,1)}, u32[]{:S(2)}, u32[]{:S(2)}) collective-permute-start(bf16[4,448,256]{2,1,0:T(8,128)(2,1)} %get-tuple-element.566), channel_id=1, source_target_pairs={{2,0},{6,2},{4,6},{12,4},{14,12},{10,14},{8,10},{16,8},{18,16},{22... | collective-permute-start | bytes 2752520 | tf_op jit(solution)/shard_map/ppermute | solution.py:704
  216.1 14.1 %collective-permute-start.31 = (bf16[136,256]{1,0:T(8,128)(2,1)S(1)}, bf16[136,256]{1,0:T(8,128)(2,1)S(1)}, u32[]{:S(2)}, u32[]{:S(2)}) collective-permute-start(bf16[136,256]{1,0:T(8,128)(2,1)S(1)} %fusion.refs_0_), channel_id=1, source_target_pairs={{0,8},{2,10},{4,12},{6,14},{8,0},{10,2},{12,4},{14,6},{16,24},{18,... | collective-permute-start | bytes 208904 | tf_op jit(solution)/shard_map/ppermute | solution.py:810
  216.2 16.0 %collective-permute-start.32 = (bf16[136,256]{1,0:T(8,128)(2,1)S(1)}, bf16[136,256]{1,0:T(8,128)(2,1)S(1)}, u32[]{:S(2)}, u32[]{:S(2)}) collective-permute-start(bf16[136,256]{1,0:T(8,128)(2,1)S(1)} %fusion.refs_0_), channel_id=1, source_target_pairs={{0,16},{2,18},{4,20},{6,22},{8,24},{10,26},{12,28},{14,30},{16,0},... | collective-permute-start | bytes 208904 | tf_op jit(solution)/shard_map/ppermute | solution.py:810
  217.4 14.8 %collective-permute-start.33 = (bf16[136,256]{1,0:T(8,128)(2,1)S(1)}, bf16[136,256]{1,0:T(8,128)(2,1)S(1)}, u32[]{:S(2)}, u32[]{:S(2)}) collective-permute-start(bf16[136,256]{1,0:T(8,128)(2,1)S(1)} %fusion.refs_0_), channel_id=1, source_target_pairs={{0,24},{2,26},{4,28},{6,30},{8,16},{10,18},{12,20},{14,22},{16,8},... | collective-permute-start | bytes 208904 | tf_op jit(solution)/shard_map/ppermute | solution.py:810
  234.6 12.2 %collective-permute-start.35 = (bf16[544,256]{1,0:T(8,128)(2,1)}, bf16[544,256]{1,0:T(8,128)(2,1)S(1)}, u32[]{:S(2)}, u32[]{:S(2)}) collective-permute-start(bf16[544,256]{1,0:T(8,128)(2,1)} %join.2.refs_0_), channel_id=1, source_target_pairs={{0,4},{2,6},{4,0},{6,2},{8,12},{10,14},{12,8},{14,10},{16,20},{18,... | collective-permute-start | bytes 835592 | tf_op jit(solution)/shard_map/ppermute | solution.py:810
  237.0 29.4 %collective-permute-start.17 = (bf16[8,256,256]{2,1,0:T(8,128)(2,1)}, bf16[8,256,256]{2,1,0:T(8,128)(2,1)S(1)}, u32[]{:S(2)}, u32[]{:S(2)}) collective-permute-start(bf16[8,256,256]{2,1,0:T(8,128)(2,1)} %get-tuple-element.525), channel_id=1, source_target_pairs={{0,1},{1,0},{2,3},{3,2},{4,5},{5,4},{6,7},{7,6},{8,9},{9,8},{10,11... | collective-permute-start | bytes 3145736 | tf_op jit(solution)/shard_map/ppermute | solution.py:699
  237.9 16.2 %collective-permute-start.30 = (bf16[4,448,256]{2,1,0:T(8,128)(2,1)}, bf16[4,448,256]{2,1,0:T(8,128)(2,1)}, u32[]{:S(2)}, u32[]{:S(2)}) collective-permute-start(bf16[4,448,256]{2,1,0:T(8,128)(2,1)} %get-tuple-element.567), channel_id=1, source_target_pairs={{0,2},{2,6},{6,4},{4,12},{12,14},{14,10},{10,8},{8,16},{16,18},{18... | collective-permute-start | bytes 2752520 | tf_op jit(solution)/shard_map/ppermute | solution.py:704
  242.8 17.1 %collective-permute-start.37 = (bf16[4,448,256]{2,1,0:T(8,128)(2,1)}, bf16[4,448,256]{2,1,0:T(8,128)(2,1)}, u32[]{:S(2)}, u32[]{:S(2)}) collective-permute-start(bf16[4,448,256]{2,1,0:T(8,128)(2,1)} %get-tuple-element.598), channel_id=1, source_target_pairs={{2,0},{6,2},{4,6},{12,4},{14,12},{10,14},{8,10},{16,8},{18,16},{22... | collective-permute-start | bytes 2752520 | tf_op jit(solution)/shard_map/ppermute | solution.py:704
  246.9 16.4 %collective-permute-start.38 = (bf16[4,448,256]{2,1,0:T(8,128)(2,1)}, bf16[4,448,256]{2,1,0:T(8,128)(2,1)}, u32[]{:S(2)}, u32[]{:S(2)}) collective-permute-start(bf16[4,448,256]{2,1,0:T(8,128)(2,1)} %get-tuple-element.599), channel_id=1, source_target_pairs={{0,2},{2,6},{6,4},{4,12},{12,14},{14,10},{10,8},{8,16},{16,18},{18... | collective-permute-start | bytes 2752520 | tf_op jit(solution)/shard_map/ppermute | solution.py:704
  (26 other events, 190.4 us)

commit v3 on v2

--- a/solution.py
+++ b/solution.py
@@ -16,7 +16,7 @@
 HBM = pl.BlockSpec(memory_space=pltpu.HBM)
 MIB = 1 << 20
 
-ROWS, FIRST, MOVED, EXTRA = 80, 36, 28, 8
+ROWS, FIRST, MOVED, EXTRA = 79, 36, 28, 8
 OVER = -1
 
 PLACE, SIDE, TOTAL, QUARTER, TAILS = range(5)
@@ -32,6 +32,7 @@
 
 
 NO_COST = pl.CostEstimate(flops=0, bytes_accessed=1024, transcendentals=0)
+SOME_COST = pl.CostEstimate(flops=10**10, bytes_accessed=1024, transcendentals=0)
 COST_PER_ROW = 7 * 10**7
 
 
@@ -322,11 +323,15 @@
 
 
 def load_results(held, rows, side, mine, theirs, sems):
+    loads = [(0, 1 - side, part) for part in theirs[:1]] + [(4, 1 - side, part) for part in theirs[1:]]
+    loads += [(4 * number, side, part) for number, part in enumerate(mine)]
     loads = [
         pltpu.make_async_copy(
-            origin, held.at[:, pl.ds(aligned(part * rows), rows)], sems.at[number]
+            origin,
+            held.at[pl.ds(first, origin.shape[0]), pl.ds(aligned(part * rows), rows)],
+            sems.at[number],
         )
-        for number, (part, origin) in enumerate(((1 - side, theirs), (side, mine)))
+        for number, (first, part, origin) in enumerate(loads)
     ]
     for load in loads:
         load.start()
@@ -334,13 +339,14 @@
         load.wait()
 
 
-def handback_kernel(dims, base, rows, who, plan, mine, theirs, to_left, to_right, held, sems):
+def handback_kernel(dims, base, rows, who, plan, *refs):
+    mine, theirs, targets, (held, sems) = refs[:2], refs[2:4], refs[4:6], refs[6:]
     load_results(held, rows, who[SIDE], mine, theirs, sems)
     copies = []
     pieces = moved_pieces(dims, plan, base, rows)
-    for number, ((place, size), target) in enumerate(zip(pieces, (to_left, to_right))):
+    for number, ((place, size), target) in enumerate(zip(pieces, targets)):
         copy = pltpu.make_async_copy(
-            held.at[:, pl.ds(place, size)], target.at[:, pl.ds(0, size)], sems.at[2 + number]
+            held.at[:, pl.ds(place, size)], target.at[:, pl.ds(0, size)], sems.at[4 + number]
         )
         copies.append((size, copy))
     for size, copy in copies:
@@ -350,37 +356,25 @@
 
 
 def handback(dims, who, plan, mine, theirs, base, rows, moved):
-    half = mine.shape[2]
-    shape = jax.ShapeDtypeStruct((4, moved, half), BF16)
+    half = mine[0].shape[2]
+    shape = jax.ShapeDtypeStruct((8, moved, half), BF16)
     return pl.pallas_call(
         functools.partial(handback_kernel, dims, base, rows),
         out_shape=(shape, shape),
-        in_specs=[SCALARS] * 2 + [HBM] * 2,
+        in_specs=[SCALARS] * 2 + [HBM] * 4,
         out_specs=(HBM, HBM),
-        scratch_shapes=[pltpu.VMEM((4, 2 * rows, half), BF16), pltpu.SemaphoreType.DMA((4,))],
-        cost_estimate=NO_COST,
+        scratch_shapes=[pltpu.VMEM((8, 2 * rows, half), BF16), pltpu.SemaphoreType.DMA((6,))],
+        cost_estimate=SOME_COST,
         compiler_params=PARAMS,
         name="handback",
-    )(who, plan, mine, theirs)
-
-
-def unpack_kernel(dims, base, rows, streams, who, counts, plan, *refs):
+    )(who, plan, *mine, *theirs)
+
+
+def unpack_kernel(dims, base, rows, streams, parts, who, counts, plan, *refs):
     pairs = streams // 4
-    mine, theirs, refs = refs[:pairs], refs[pairs], refs[pairs + 1 :]
+    mine, theirs, refs = refs[:parts], refs[parts], refs[parts + 1 :]
     outs, (held, sems, *tails) = refs[2 * pairs : 4 * pairs], refs[4 * pairs :]
-    side = 1 if base is None else who[SIDE]
-    loads = [(pl.ds(0, streams), 1 - side, theirs)]
-    loads += [(pl.ds(4 * number, 4), side, part) for number, part in enumerate(mine)]
-    loads = [
-        pltpu.make_async_copy(
-            origin, held.at[where, pl.ds(aligned(part * rows), rows)], sems.at[number]
-        )
-        for number, (where, part, origin) in enumerate(loads)
-    ]
-    for load in loads:
-        load.start()
-    for load in loads:
-        load.wait()
+    load_results(held, rows, 1 if base is None else who[SIDE], mine, [theirs], sems)
     pieces = sent_pieces(who, plan)
     if base is not None:
         pieces = (own_piece(plan[KEPT], plan, base, rows),)
@@ -429,7 +423,7 @@
     tails = [pltpu.VMEM((streams, dims[0] * GROUP, half), BF16)] if base == 0 else []
     first = 4 + len(mine)
     return pl.pallas_call(
-        functools.partial(unpack_kernel, dims, base, rows, streams),
+        functools.partial(unpack_kernel, dims, base, rows, streams, len(mine)),
         out_shape=[jax.ShapeDtypeStruct(out.shape, BF16) for out in outs],
         in_specs=[SCALARS] * 3 + [HBM] * (len(mine) + 1 + len(outs)),
         out_specs=[HBM] * len(outs),
@@ -938,12 +932,11 @@
     bias_got = swap_tensor(jnp.stack([bias_in, bias_out]))
     totals = jnp.where(jnp.arange(dp_size, dtype=jnp.int32) == place, who[TOTAL], 0)
     totals = sum_in_fours(totals, 1, dp_size)
-    who, totals = together(who, totals)
     own1, send1 = pack(dims, who, counts, None, arrays, 0, first)
     send1, piece_got, bias_got = together(send1, piece_got, bias_got)
     got1 = swap_tensor(send1)
     pieces = [piece_got] + [flipped(piece_got, flip, dp_size) for flip in (2, 1, 3)]
-    who, own1 = together(who, own1)
+    who, own1, totals = together(who, own1, totals)
     own2, send2 = pack(dims, who, counts, None, arrays, *middle)
     got2 = swap_tensor(send2)
     for step in range(2, bits, 2):
@@ -955,7 +948,9 @@
     neighbours = (shift(to_right, order, 1), shift(to_left, order, -1))
     pieces, to_left = together(pieces, to_left)
     weights = assemble(who, weight_in, weight_out, bias_in, bias_out, bias_got, pieces)
-    who, weights, neighbours = together(who, weights, neighbours)
+    later_counts, weights = together(counts, weights)
+    outs = tuple(blank(later_counts, row_count, half, sources))
+    who, weights, neighbours, outs = together(who, weights, neighbours, outs)
     own3, send3 = pack(dims, who, counts, plan, arrays, *last, neighbours)
     got3 = swap_tensor(send3)
     own3, weights, got2 = together(own3, weights, got2)
@@ -974,9 +969,7 @@
     def place_grads(outs, base, rows, own, got):
         return (*outs[:2], *unpack(dims, who, counts, plan, [own], got, outs[2:], base, rows))
 
-    result1, sums = blocks(0, plan, (own1, got1), None)
-    later_counts, sums = together(counts, sums)
-    outs = blank(later_counts, row_count, half, sources)
+    result1, sums = blocks(0, plan, (own1, got1), None, merged=True)
 
     def more(carry):
         return carry[0] < plan[ROUNDS]
@@ -990,48 +983,49 @@
         outs = place_all(outs, OVER, extra, here, result, swap_tensor(result[2]))
         return number + 1, sums, tuple(outs)
 
-    _, sums, outs = lax.while_loop(more, extra_round, (jnp.int32(0), sums, tuple(outs)))
-    y1_got, d1_got = swap_tensor(result1[2]), swap_tensor(result1[3])
+    _, sums, outs = lax.while_loop(more, extra_round, (jnp.int32(0), sums, outs))
     result2, sums = blocks(middle[0], plan, (own2, got2), sums, merged=True)
+    yd2_got = swap_tensor(result2[2])
     sums, outs = together(sums, outs)
     result3, sums = blocks(last[0], plan, (own3, got3), sums, final=True)
-
-    sums, y1_got = together(sums, y1_got)
+    sums, yd2_got = together(sums, yd2_got)
+
     kept, *sent = sums
     core, across, *others = groups_of(bits)
+    y3_got = swap_tensor(result3[2])
+    d3_got = swap_tensor(result3[3])
     came = jnp.stack([flipped(part, 1, dp_size) for part in sent])
     grads = kept + came.astype(F32)
     grads = reduce_step(grads, across, place, dp_size)
-    outs = place_values(outs, 0, first, result1[0], y1_got)
-    grads, d1_got, outs = together(grads, d1_got, outs)
+    outs = place_all(outs, *middle, plan, result2, yd2_got)
+    grads, y3_got, outs = together(grads, y3_got, outs)
     for group in others:
         grads = reduce_step(grads, group, place, dp_size)
-    outs = place_grads(outs, 0, first, result1[1], d1_got)
-    grads, outs = together(grads, outs)
-    y3_got = swap_tensor(result3[2])
+    outs = place_values(outs, *last, result3[0], y3_got)
+    grads, d3_got, outs = together(grads, d3_got, outs)
     mine = lax.dynamic_index_in_dim(grads, side, 0, keepdims=False)
     other = lax.dynamic_index_in_dim(grads, 1 - side, 0, keepdims=False).astype(BF16)
     total = (mine + swap_tensor(other).astype(F32)).astype(BF16)
-    total, d3_send, y3_got = together(total, result3[3], y3_got)
-    d3_got = swap_tensor(d3_send)
-    y_left, y_right = handback(dims, who, plan, result3[0], y3_got, *last, moved)
-    y_back = (shift(y_left, order, -1), shift(y_right, order, 1))
-    outs = place_values(outs, *last, result3[0], y3_got)
-    for group in reversed(others):
-        total = gather_step(total, group, place, dp_size)
-    total, d3_got, outs = together(total, d3_got, outs)
-    yd2_got = swap_tensor(result2[2])
-    d_left, d_right = handback(dims, who, plan, result3[1], d3_got, *last, moved)
-    d_back = (shift(d_left, order, -1), shift(d_right, order, 1))
-    total = gather_step(total, across, place, dp_size)
+    total, yd1_send = together(total, result1[2])
+    yd1_got = swap_tensor(yd1_send)
+    plan, total = together(plan, total)
+    to_left, to_right = handback(
+        dims, who, plan, result3[:2], (y3_got, d3_got), *last, moved
+    )
+    total, to_left = together(total, to_left)
+    back = (shift(to_left, order, -1), shift(to_right, order, 1))
+    for bit, many in reversed(others):
+        for step in range(bit, bit + many):
+            total = gather_step(total, (step, 1), place, dp_size)
     outs = place_grads(outs, *last, result3[1], d3_got)
     total, outs = together(total, outs)
+    total = gather_step(total, across, place, dp_size)
+    outs = unpack(dims, who, counts, plan, back[:1], back[1], outs, None, moved)
+    total, outs, yd1_got = together(total, outs, yd1_got)
     total_got = flipped(total, 1, dp_size)
-    outs = place_values(outs, None, moved, *y_back)
+    outs = place_all(outs, 0, first, plan, result1, yd1_got)
+    outs, total_got = together(outs, total_got)
     sums = finish((place & 1).astype(jnp.int32)[None], total, total_got)
-    outs, sums = together(outs, sums)
-    outs = place_grads(outs, None, moved, *d_back)
-    outs = place_all(outs, *middle, plan, result2, yd2_got)
     grad_in, grad_out, bias_in_grad, bias_out_grad = sums
     return (*outs, grad_in, bias_in_grad, grad_out, bias_out_grad)
 

time: 274 us -> 271 us (0.989)
  waiting for transfers between devices: 72.5 us -> 83 us
  starting transfers between devices: 54.1 us -> 45 us
  Pallas kernels: 129 us -> 124 us
    ppermute x20 -> x19, waiting for transfers between devices: 25.8 us -> 49.2 us  [flipped(): return lax.ppermute(value, 'dp', [(i, i ^ flip) for i in range(size)])]
    ppermute x6 -> x4, starting transfers between devices: 17.2 us -> 10.2 us  [shift(): lax.ppermute(value, 'dp', pairs if step == 1 else [(b, a) for a, b in pai...]
    ppermute x6 -> x4, waiting for transfers between devices: 19.3 us -> 12.6 us  [shift(): lax.ppermute(value, 'dp', pairs if step == 1 else [(b, a) for a, b in pai...]
    ppermute x11 -> x10, waiting for transfers between devices: 27.4 us -> 21.2 us  [swap_tensor(): return lax.ppermute(value, 'tensor', [(0, 1), (1, 0)])]
    pallas_call x7 -> x5, Pallas kernels: 25.2 us -> 19.7 us  [unpack(): pl.pallas_call(functools.partial(unpack_kernel, dims, base, rows, streams...]
    pallas_call x2 -> x1, Pallas kernels: 5.98 us -> 3.62 us  [handback(): pl.pallas_call(functools.partial(handback_kernel, dims, base, rows), out_...]
    ppermute x20 -> x19, starting transfers between devices: 23.5 us -> 22.2 us  [flipped(): return lax.ppermute(value, 'dp', [(i, i ^ flip) for i in range(size)])]
    ppermute x11 -> x10, starting transfers between devices: 13.3 us -> 12.6 us  [swap_tensor(): return lax.ppermute(value, 'tensor', [(0, 1), (1, 0)])]
  transfers between devices with their start and end apart: 37 -> 33, of which waited for: 15 -> 17; matrix products, arithmetic and copies ran while one was open for 3% -> 3% of each run, Pallas kernels for 45% -> 45%
where the time goes in v3:
time: 271 us; the launch traced here: 268 us
  Pallas kernels  124 us (46%)
  waiting for transfers between devices  83 us (31%)
  starting transfers between devices  45 us (17%)
  other arithmetic  7.18 us (3%)
  local copies, waits for them, and re-layouts  6.37 us (2%)
    pallas_call x3, Pallas kernels, run_blocks(): pl.pallas_call(functools.partial(blocks_kernel, dims, base, rows, tile, f...  63.3 us
    ppermute x19, waiting for transfers between devices, flipped(): return lax.ppermute(value, 'dp', [(i, i ^ flip) for i in range(size)])  49.2 us
    ppermute x19, starting transfers between devices, flipped(): return lax.ppermute(value, 'dp', [(i, i ^ flip) for i in range(size)])  22.2 us
    ppermute x10, waiting for transfers between devices, swap_tensor(): return lax.ppermute(value, 'tensor', [(0, 1), (1, 0)])  21.2 us
    pallas_call x5, Pallas kernels, unpack(): pl.pallas_call(functools.partial(unpack_kernel, dims, base, rows, streams...  19.7 us
    pallas_call x3, Pallas kernels, pack(): pl.pallas_call(functools.partial(pack_kernel, dims, base, rows, len(neigh...  14.6 us
    ppermute x4, waiting for transfers between devices, shift(): lax.ppermute(value, 'dp', pairs if step == 1 else [(b, a) for a, b in pai...  12.6 us
    ppermute x10, starting transfers between devices, swap_tensor(): return lax.ppermute(value, 'tensor', [(0, 1), (1, 0)])  12.6 us
  transfers between devices with their start and end apart: 33, of which 17 were waited for; matrix products, arithmetic and copies ran while one was open for 3% of the time, Pallas kernels for 45%

profile of v3, /device:TPU:10, one launch (start us, length us, event | category | flops | bytes accessed | tf_op | source)
XLA Modules:
  0.0 268.1 jit_solution(8144689553522710100)
XLA Ops:
  0.6 2.2 quarter.1
  6.2 5.7 %pack.8 = (bf16[8,576,256]{2,1,0:T(8,128)(2,1)}, bf16[8,576,256]{2,1,0:T(8,128)(2,1)}) custom-call(s32[8]{0:T(128)S(1)} %get-tuple-element.807.who, s32[16]{0:T(128)} %counts.20, bf16[4096,256]{1,0:T(8,128)(2,1)} %refs_1_.5, bf16[3,4096,256]{2,1,0:T(8,128)(2,1)} %refs_2_.5, bf16[4096,256]{1,0:T(8,128)(2,1)} %refs_3_.5, bf16[3,4096,256]{2,1,0:T(8,128)(2,1)} %refs_4_.1), custom_call_target="tpu_custom_call" | custom-call | bytes 1024 | tf_op jit(solution)/shard_map/pack/pallas_call | solution.py:272
  22.8 2.2 collective-permute-start.7
  26.5 4.2 %collective-permute-start.8 = (s32[16]{0:T(128)S(1)}, s32[16]{0:T(128)S(1)}, u32[]{:S(2)}, u32[]{:S(2)}) collective-permute-start(s32[16]{0:T(128)S(1)} %add_add_fusion.1), channel_id=1, source_target_pairs={{0,16},{2,18},{4,20},{6,22},{8,24},{10,26},{12,28},{14,30},{16,0},... | collective-permute-start | bytes 200 | tf_op jit(solution)/shard_map/ppermute | solution.py:804
  30.7 3.8 %pack.9 = (bf16[8,240,256]{2,1,0:T(8,128)(2,1)}, bf16[8,240,256]{2,1,0:T(8,128)(2,1)}) custom-call(s32[8]{0:T(128)S(1)} %get-tuple-element.807.who, s32[16]{0:T(128)S(1)} %copy-done.15, bf16[4096,256]{1,0:T(8,128)(2,1)S(1)} %copy-done, bf16[3,4096,256]{2,1,0:T(8,128)(2,1)} %refs_2_.5, bf16[4096,256]{1,0:T(8,128)(2,1)} %refs_3_.5, bf16[3,4096,256]{2,1,0:T(8,128)(2,1)} %refs_4_.1), custom_call_target="tpu_custom_call" | custom-call | bytes 1024 | tf_op jit(solution)/shard_map/pack/pallas_call | solution.py:272
  36.6 4.0 %export.1 = (bf16[8,448,256]{2,1,0:T(8,128)(2,1)}, bf16[8,448,256]{2,1,0:T(8,128)(2,1)}) custom-call(s32[8]{0:T(128)S(1)} %get-tuple-element.807.who, s32[16]{0:T(128)S(1)} %copy-done.15, s32[8]{0:T(128)} %plan.1.refs_0_.rest_0_, bf16[4096,256]{1,0:T(8,128)(2,1)S(1)} %copy-done, bf16[3,4096,256]{2,1,0:T(8,128)(2,1)} %refs_2_.5, bf16[4096,256]{1,0:T(8,128)(2,1)} %refs_3_.5, ...), custom_call_target="tpu_custom_call" | custom-call | bytes 1024 | tf_op jit(solution)/shard_map/export/pallas_call | solution.py:313
  42.6 3.9 %collective-permute-start.14 = (bf16[8,448,256]{2,1,0:T(8,128)(2,1)}, bf16[8,448,256]{2,1,0:T(8,128)(2,1)}, u32[]{:S(2)}, u32[]{:S(2)}) collective-permute-start(bf16[8,448,256]{2,1,0:T(8,128)(2,1)} %get-tuple-element.485), channel_id=1, source_target_pairs={{2,0},{6,2},{4,6},{12,4},{14,12},{10,14},{8,10},{16,8},{18,16},{22... | collective-permute-start | bytes 5505032 | tf_op jit(solution)/shard_map/ppermute | solution.py:698
  47.1 4.6 %assemble.1 = (bf16[2,512,512]{2,1,0:T(8,128)(2,1)S(1)}, bf16[2,512,512]{2,1,0:T(8,128)(2,1)}, bf16[2,512,512]{2,1,0:T(8,128)(2,1)}, bf16[2,512,512]{2,1,0:T(8,128)(2,1)}, f32[2,2,512]{2,1,0:T(2,128)S(1)}) custom-call(s32[8]{0:T(128)S(1)} %get-tuple-element.807.who, bf16[2,512,256]{2,1,0:T(8,128)(2,1)} %w_in.3, bf16[2,256,512]{2,1,0:T(8,128)(2,1)} %w_out.3, ...), custom_call_target="tpu_custom_call" | custom-call | bytes 1024 | tf_op jit(solution)/shard_map/assemble/pallas_call | solution.py:791
  51.7 3.2 %blank.1 = (bf16[4096,256]{1,0:T(8,128)(2,1)}, bf16[3,4096,256]{2,1,0:T(8,128)(2,1)}, bf16[4096,256]{1,0:T(8,128)(2,1)}, bf16[3,4096,256]{2,1,0:T(8,128)(2,1)}) custom-call(s32[16]{0:T(128)S(1)} %copy-done.15), custom_call_target="tpu_custom_call" | custom-call | bytes 1024 | tf_op jit(solution)/shard_map/blank/pallas_call | solution.py:475
  54.9 11.1 %collective-permute-done.13.refs_5_ = bf16[8,448,256]{2,1,0:T(8,128)(2,1)} collective-permute-done((bf16[8,448,256]{2,1,0:T(8,128)(2,1)}, bf16[8,448,256]{2,1,0:T(8,128)(2,1)}, u32[]{:S(2)}, u32[]{:S(2)}) %collective-permute-start.13) | collective-permute-done | bytes 1835040 | tf_op jit(solution)/shard_map/ppermute | solution.py:698
  67.5 5.1 %pack.10 = (bf16[8,448,256]{2,1,0:T(8,128)(2,1)}, bf16[8,448,256]{2,1,0:T(8,128)(2,1)}) custom-call(s32[8]{0:T(128)S(1)} %get-tuple-element.807.who, s32[16]{0:T(128)S(1)} %copy-done.15, s32[8]{0:T(128)} %plan.1.refs_0_.rest_0_, bf16[4096,256]{1,0:T(8,128)(2,1)S(1)} %copy-done, bf16[3,4096,256]{2,1,0:T(8,128)(2,1)} %refs_2_.5, bf16[4096,256]{1,0:T(8,128)(2,1)} %refs_3_.5, ...), custom_call_target="tpu_custom_call" | custom-call | bytes 1024 | tf_op jit(solution)/shard_map/pack/pallas_call | solution.py:272
  72.6 13.2 %collective-permute-done.15.got = bf16[8,240,256]{2,1,0:T(8,128)(2,1)} collective-permute-done((bf16[8,240,256]{2,1,0:T(8,128)(2,1)}, bf16[8,240,256]{2,1,0:T(8,128)(2,1)}, u32[]{:S(2)}, u32[]{:S(2)}) %collective-permute-start.15) | collective-permute-done | bytes 983072 | tf_op jit(solution)/shard_map/ppermute | solution.py:693
  87.3 24.5 %blocks.8 = (bf16[4,576,256]{2,1,0:T(8,128)(2,1)}, bf16[4,576,256]{2,1,0:T(8,128)(2,1)}, bf16[8,576,256]{2,1,0:T(8,128)(2,1)}, f32[2,2176,256]{2,1,0:T(8,128)}, f32[4,8,512]{2,1,0:T(8,128)S(1)}) custom-call(s32[8]{0:T(128)S(1)} %get-tuple-element.807.who, bf16[8,576,256]{2,1,0:T(8,128)(2,1)} %get-tuple-element.525.own, ...), custom_call_target="tpu_custom_call" | custom-call | flops 40320000000 | bytes 1024 | tf_op jit(solution)/shard_map/blocks/pallas_call | solution.py:666
  112.7 16.9 %blocks.9 = (bf16[4,240,256]{2,1,0:T(8,128)(2,1)}, bf16[4,240,256]{2,1,0:T(8,128)(2,1)}, bf16[8,240,256]{2,1,0:T(8,128)(2,1)}, f32[2,2176,256]{2,1,0:T(8,128)}, f32[4,8,512]{2,1,0:T(8,128)S(1)}) custom-call(s32[8]{0:T(128)S(1)} %get-tuple-element.878, bf16[8,240,256]{2,1,0:T(8,128)(2,1)} %get-tuple-element.523.own, ...), custom_call_target="tpu_custom_call", output_to_operand_aliasing={{3}: (9, {}), {4}: (10, {})} | custom-call | bytes 1024 | tf_op jit(solution)/shard_map/blocks/pallas_call | solution.py:666
  130.1 22.0 %blocks.10 = (bf16[4,448,256]{2,1,0:T(8,128)(2,1)}, bf16[4,448,256]{2,1,0:T(8,128)(2,1)}, bf16[4,448,256]{2,1,0:T(8,128)(2,1)}, bf16[4,448,256]{2,1,0:T(8,128)(2...) custom-call(s32[8]{0:T(128)S(1)} %get-tuple-element.878, ...), custom_call_target="tpu_custom_call" | custom-call | bytes 1024 | tf_op jit(solution)/shard_map/blocks/pallas_call | solution.py:666
  155.1 2.0 convert_add_fusion
  160.6 3.5 %unpack.10 = (bf16[4096,256]{1,0:T(8,128)(2,1)S(1)}, bf16[3,4096,256]{2,1,0:T(8,128)(2,1)}, bf16[4096,256]{1,0:T(8,128)(2,1)}, bf16[3,4096,256]{2,1,0:T(8,128)(2,1)}) custom-call(s32[8]{0:T(128)S(1)} %get-tuple-element.878, s32[16]{0:T(128)S(1)} %get-tuple-element.888, ...), custom_call_target="tpu_custom_call", output_to_operand_aliasing={{0}: (6, {}), {1}: (7, {}), {2}: (8, {}), {3}: (9, {})} | custom-call | bytes 1024 | tf_op jit(solution)/shard_map/unpack/pallas_call | solution.py:425
  164.1 9.3 %collective-permute-done.21 = bf16[2,544,256]{2,1,0:T(8,128)(2,1)} collective-permute-done((bf16[2,544,256]{2,1,0:T(8,128)(2,1)S(1)}, bf16[2,544,256]{2,1,0:T(8,128)(2,1)}, u32[]{:S(2)}, u32[]{:S(2)}) %collective-permute-start.21) | collective-permute-done | bytes 557088 | tf_op jit(solution)/shard_map/ppermute | solution.py:804
  181.0 3.5 %unpack.11 = (bf16[4096,256]{1,0:T(8,128)(2,1)S(1)}, bf16[3,4096,256]{2,1,0:T(8,128)(2,1)}) custom-call(s32[8]{0:T(128)S(1)} %get-tuple-element.878, s32[16]{0:T(128)S(1)} %get-tuple-element.888, s32[8]{0:T(128)} %plan.1.refs_0_.rest_0_, bf16[4,448,256]{2,1,0:T(8,128)(2,1)} %get-tuple-element.564.refs_0_, ...), custom_call_target="tpu_custom_call", output_to_operand_aliasing={{0}: (5, {}), {1}: (6, {})} | custom-call | bytes 1024 | tf_op jit(solution)/shard_map/unpack/pallas_call | solution.py:425
  184.5 3.6 %collective-permute-done.25 = bf16[2,136,256]{2,1,0:T(8,128)(2,1)S(1)} collective-permute-done((bf16[2,136,256]{2,1,0:T(8,128)(2,1)}, bf16[2,136,256]{2,1,0:T(8,128)(2,1)S(1)}, u32[]{:S(2)}, u32[]{:S(2)}) %collective-permute-start.25) | collective-permute-done | bytes 139296 | tf_op jit(solution)/shard_map/ppermute | solution.py:804
  191.1 3.9 %collective-permute-done.26.refs_3_.refs_1_ = bf16[4,448,256]{2,1,0:T(8,128)(2,1)} collective-permute-done((bf16[4,448,256]{2,1,0:T(8,128)(2,1)}, bf16[4,448,256]{2,1,0:T(8,128)(2,1)}, u32[]{:S(2)}, u32[]{:S(2)}) %collective-permute-start.26) | collective-permute-done | bytes 917536 | tf_op jit(solution)/shard_map/ppermute | solution.py:693
  196.6 2.8 %collective-permute-done.27 = bf16[136,256]{1,0:T(8,128)(2,1)S(1)} collective-permute-done((bf16[136,256]{1,0:T(8,128)(2,1)S(1)}, bf16[136,256]{1,0:T(8,128)(2,1)S(1)}, u32[]{:S(2)}, u32[]{:S(2)}) %collective-permute-start.27) | collective-permute-done | bytes 69664 | tf_op jit(solution)/shard_map/ppermute | solution.py:693
  201.0 3.6 %handback.1 = (bf16[8,448,256]{2,1,0:T(8,128)(2,1)}, bf16[8,448,256]{2,1,0:T(8,128)(2,1)}) custom-call(s32[8]{0:T(128)S(1)} %get-tuple-element.878, s32[8]{0:T(128)} %plan.1.refs_0_.rest_0_, bf16[4,448,256]{2,1,0:T(8,128)(2,1)} %get-tuple-element.564.refs_0_, bf16[4,448,256]{2,1,0:T(8,128)(2,1)} %get-tuple-element.579.refs_1_.refs_0_, ...), custom_call_target="tpu_custom_call" | custom-call | flops 10000000000 | bytes 1024 | tf_op jit(solution)/shard_map/handback/pallas_call | solution.py:361
  204.6 2.2 collective-permute-start.31
  206.8 2.2 collective-permute-start.32
  210.8 23.6 %collective-permute-done.28.refs_1_ = bf16[136,256]{1,0:T(8,128)(2,1)S(1)} collective-permute-done((bf16[136,256]{1,0:T(8,128)(2,1)S(1)}, bf16[136,256]{1,0:T(8,128)(2,1)S(1)}, u32[]{:S(2)}, u32[]{:S(2)}) %collective-permute-start.28) | collective-permute-done | bytes 69664 | tf_op jit(solution)/shard_map/ppermute | solution.py:804
  236.6 3.0 %collective-permute-start.29 = (bf16[272,256]{1,0:T(8,128)(2,1)}, bf16[272,256]{1,0:T(8,128)(2,1)S(1)}, u32[]{:S(2)}, u32[]{:S(2)}) collective-permute-start(bf16[272,256]{1,0:T(8,128)(2,1)} %join.3.refs_0_), channel_id=1, source_target_pairs={{0,16},{2,18},{4,20},{6,22},{8,24},{10,26},{12,28},{14,30},{16,0},... | collective-permute-start | bytes 417800 | tf_op jit(solution)/shard_map/ppermute | solution.py:804
  239.6 3.3 %unpack.12 = (bf16[4096,256]{1,0:T(8,128)(2,1)}, bf16[3,4096,256]{2,1,0:T(8,128)(2,1)}) custom-call(s32[8]{0:T(128)S(1)} %get-tuple-element.878, s32[16]{0:T(128)S(1)} %get-tuple-element.888, s32[8]{0:T(128)} %plan.1.refs_0_.rest_0_, bf16[4,448,256]{2,1,0:T(8,128)(2,1)} %get-tuple-element.579.refs_1_.refs_0_, ...), custom_call_target="tpu_custom_call", output_to_operand_aliasing={{0}: (5, {}), {1}: (6, {})} | custom-call | bytes 1024 | tf_op jit(solution)/shard_map/unpack/pallas_call | solution.py:425
  245.4 6.7 %collective-permute-done.30.refs_1_ = bf16[544,256]{1,0:T(8,128)(2,1)S(1)} collective-permute-done((bf16[544,256]{1,0:T(8,128)(2,1)}, bf16[544,256]{1,0:T(8,128)(2,1)S(1)}, u32[]{:S(2)}, u32[]{:S(2)}) %collective-permute-start.30) | collective-permute-done | bytes 278560 | tf_op jit(solution)/shard_map/ppermute | solution.py:804
  254.8 3.6 %unpack.13 = (bf16[4096,256]{1,0:T(8,128)(2,1)S(1)}, bf16[3,4096,256]{2,1,0:T(8,128)(2,1)}, bf16[4096,256]{1,0:T(8,128)(2,1)}, bf16[3,4096,256]{2,1,0:T(8,128)(2,1)}) custom-call(s32[8]{0:T(128)S(1)} %get-tuple-element.878, s32[16]{0:T(128)S(1)} %get-tuple-element.888, ...), custom_call_target="tpu_custom_call", output_to_operand_aliasing={{0}: (5, {}), {1}: (6, {}), {2}: (7, {}), {3}: (8, {})} | custom-call | bytes 1024 | tf_op jit(solution)/shard_map/unpack/pallas_call | solution.py:425
  258.5 5.9 %unpack.14 = (bf16[4096,256]{1,0:T(8,128)(2,1)S(1)}, bf16[3,4096,256]{2,1,0:T(8,128)(2,1)}, bf16[4096,256]{1,0:T(8,128)(2,1)}, bf16[3,4096,256]{2,1,0:T(8,128)(2,1)}) custom-call(s32[8]{0:T(128)S(1)} %get-tuple-element.878, s32[16]{0:T(128)S(1)} %get-tuple-element.888, ...), custom_call_target="tpu_custom_call", output_to_operand_aliasing={{0}: (6, {}), {1}: (7, {}), {2}: (8, {}), {3}: (9, {})} | custom-call | bytes 1024 | tf_op jit(solution)/shard_map/unpack/pallas_call | solution.py:425
  265.3 2.6 finish.1
  (108 shorter events, 55.1 us)
Async XLA Ops:
  2.8 9.1 %collective-permute-start.5 = (bf16[512,256]{1,0:T(8,128)(2,1)}, bf16[512,256]{1,0:T(8,128)(2,1)S(1)}, u32[]{:S(2)}, u32[]{:S(2)}) collective-permute-start(bf16[512,256]{1,0:T(8,128)(2,1)} %get-tuple-element.474), channel_id=1, source_target_pairs={{0,1},{1,0},{2,3},{3,2},{4,5},{5,4},{6,7},{7,6},{8,9},{9,8},{10,11... | collective-permute-start | bytes 786440 | tf_op jit(solution)/shard_map/ppermute | solution.py:693
  5.1 6.8 %collective-permute-start.6 = (f32[2,2,256]{2,1,0:T(2,128)S(1)}, f32[2,2,256]{2,1,0:T(2,128)S(1)}, u32[]{:S(2)}, u32[]{:S(2)}) collective-permute-start(f32[2,2,256]{2,1,0:T(2,128)S(1)} %pad_maximum_fusion), channel_id=1, source_target_pairs={{0,1},{1,0},{2,3},{3,2},{4,5},{5,4},{6,7},{7,6},{8,9},{9,8},{10,11... | collective-permute-start | bytes 12296 | tf_op jit(solution)/shard_map/ppermute | solution.py:693
  11.9 75.4 %collective-permute-start.17 = (bf16[8,576,256]{2,1,0:T(8,128)(2,1)}, bf16[8,576,256]{2,1,0:T(8,128)(2,1)}, u32[]{:S(2)}, u32[]{:S(2)}) collective-permute-start(bf16[8,576,256]{2,1,0:T(8,128)(2,1)} %get-tuple-element.526), channel_id=1, source_target_pairs={{0,1},{1,0},{2,3},{3,2},{4,5},{5,4},{6,7},{7,6},{8,9},{9,8},{10,11... | collective-permute-start | bytes 7077896 | tf_op jit(solution)/shard_map/ppermute | solution.py:693
  14.2 3.0 %collective-permute-start.4 = (s32[16]{0:T(128)S(1)}, s32[16]{0:T(128)S(1)}, u32[]{:S(2)}, u32[]{:S(2)}) collective-permute-start(s32[16]{0:T(128)S(1)} %compare_select_fusion), channel_id=1, source_target_pairs={{0,6},{2,4},{4,2},{6,0},{8,14},{10,12},{12,10},{14,8},{16,22},{18,... | collective-permute-start | bytes 200 | tf_op jit(solution)/shard_map/ppermute | solution.py:804
  14.2 3.0 %collective-permute-start.2 = (s32[16]{0:T(128)S(1)}, s32[16]{0:T(128)S(1)}, u32[]{:S(2)}, u32[]{:S(2)}) collective-permute-start(s32[16]{0:T(128)S(1)} %compare_select_fusion), channel_id=1, source_target_pairs={{0,2},{2,0},{4,6},{6,4},{8,10},{10,8},{12,14},{14,12},{16,18},{18,... | collective-permute-start | bytes 200 | tf_op jit(solution)/shard_map/ppermute | solution.py:804
  14.8 3.7 %collective-permute-start.3 = (s32[16]{0:T(128)S(1)}, s32[16]{0:T(128)S(1)}, u32[]{:S(2)}, u32[]{:S(2)}) collective-permute-start(s32[16]{0:T(128)S(1)} %compare_select_fusion), channel_id=1, source_target_pairs={{0,4},{2,6},{4,0},{6,2},{8,12},{10,14},{12,8},{14,10},{16,20},{18,... | collective-permute-start | bytes 200 | tf_op jit(solution)/shard_map/ppermute | solution.py:804
  16.4 20.2 %collective-permute-start.10 = (bf16[512,256]{1,0:T(8,128)(2,1)S(1)}, bf16[512,256]{1,0:T(8,128)(2,1)S(1)}, u32[]{:S(2)}, u32[]{:S(2)}) collective-permute-start(bf16[512,256]{1,0:T(8,128)(2,1)S(1)} %collective-permute-done.5.refs_0_), channel_id=1, source_target_pairs={{0,4},{2,6},{4,0},{6,2},{8,12},{10,14},{12,8},{14,10},{16,20},{18,... | collective-permute-start | bytes 786440 | tf_op jit(solution)/shard_map/ppermute | solution.py:804
  17.2 19.4 %collective-permute-start.11 = (bf16[512,256]{1,0:T(8,128)(2,1)S(1)}, bf16[512,256]{1,0:T(8,128)(2,1)S(1)}, u32[]{:S(2)}, u32[]{:S(2)}) collective-permute-start(bf16[512,256]{1,0:T(8,128)(2,1)S(1)} %collective-permute-done.5.refs_0_), channel_id=1, source_target_pairs={{0,2},{2,0},{4,6},{6,4},{8,10},{10,8},{12,14},{14,12},{16,18},{18,... | collective-permute-start | bytes 786440 | tf_op jit(solution)/shard_map/ppermute | solution.py:804
  17.2 19.4 %collective-permute-start.12 = (bf16[512,256]{1,0:T(8,128)(2,1)S(1)}, bf16[512,256]{1,0:T(8,128)(2,1)S(1)}, u32[]{:S(2)}, u32[]{:S(2)}) collective-permute-start(bf16[512,256]{1,0:T(8,128)(2,1)S(1)} %collective-permute-done.5.refs_0_), channel_id=1, source_target_pairs={{0,6},{2,4},{4,2},{6,0},{8,14},{10,12},{12,10},{14,8},{16,22},{18,... | collective-permute-start | bytes 786440 | tf_op jit(solution)/shard_map/ppermute | solution.py:804
  19.2 3.6 %collective-permute-start.9 = (s32[16]{0:T(128)S(1)}, s32[16]{0:T(128)S(1)}, u32[]{:S(2)}, u32[]{:S(2)}) collective-permute-start(s32[16]{0:T(128)S(1)} %add_add_fusion.1), channel_id=1, source_target_pairs={{0,24},{2,26},{4,28},{6,30},{8,16},{10,18},{12,20},{14,22},{16,8},... | collective-permute-start | bytes 200 | tf_op jit(solution)/shard_map/ppermute | solution.py:804
  22.8 3.8 %collective-permute-start.7 = (s32[16]{0:T(128)S(1)}, s32[16]{0:T(128)S(1)}, u32[]{:S(2)}, u32[]{:S(2)}) collective-permute-start(s32[16]{0:T(128)S(1)} %add_add_fusion.1), channel_id=1, source_target_pairs={{0,8},{2,10},{4,12},{6,14},{8,0},{10,2},{12,4},{14,6},{16,24},{18,... | collective-permute-start | bytes 200 | tf_op jit(solution)/shard_map/ppermute | solution.py:804
  26.5 8.0 %collective-permute-start.8 = (s32[16]{0:T(128)S(1)}, s32[16]{0:T(128)S(1)}, u32[]{:S(2)}, u32[]{:S(2)}) collective-permute-start(s32[16]{0:T(128)S(1)} %add_add_fusion.1), channel_id=1, source_target_pairs={{0,16},{2,18},{4,20},{6,22},{8,24},{10,26},{12,28},{14,30},{16,0},... | collective-permute-start | bytes 200 | tf_op jit(solution)/shard_map/ppermute | solution.py:804
  40.6 25.4 %collective-permute-start.13 = (bf16[8,448,256]{2,1,0:T(8,128)(2,1)}, bf16[8,448,256]{2,1,0:T(8,128)(2,1)}, u32[]{:S(2)}, u32[]{:S(2)}) collective-permute-start(bf16[8,448,256]{2,1,0:T(8,128)(2,1)} %get-tuple-element.500), channel_id=1, source_target_pairs={{0,2},{2,6},{6,4},{4,12},{12,14},{14,10},{10,8},{8,16},{16,18},{18... | collective-permute-start | bytes 5505032 | tf_op jit(solution)/shard_map/ppermute | solution.py:698
  42.6 25.0 %collective-permute-start.14 = (bf16[8,448,256]{2,1,0:T(8,128)(2,1)}, bf16[8,448,256]{2,1,0:T(8,128)(2,1)}, u32[]{:S(2)}, u32[]{:S(2)}) collective-permute-start(bf16[8,448,256]{2,1,0:T(8,128)(2,1)} %get-tuple-element.485), channel_id=1, source_target_pairs={{2,0},{6,2},{4,6},{12,4},{14,12},{10,14},{8,10},{16,8},{18,16},{22... | collective-permute-start | bytes 5505032 | tf_op jit(solution)/shard_map/ppermute | solution.py:698
  46.5 39.3 %collective-permute-start.15 = (bf16[8,240,256]{2,1,0:T(8,128)(2,1)}, bf16[8,240,256]{2,1,0:T(8,128)(2,1)}, u32[]{:S(2)}, u32[]{:S(2)}) collective-permute-start(bf16[8,240,256]{2,1,0:T(8,128)(2,1)} %get-tuple-element.515), channel_id=1, source_target_pairs={{0,1},{1,0},{2,3},{3,2},{4,5},{5,4},{6,7},{7,6},{8,9},{9,8},{10,11... | collective-permute-start | bytes 2949128 | tf_op jit(solution)/shard_map/ppermute | solution.py:693
  85.8 44.3 %collective-permute-start.16 = (bf16[8,448,256]{2,1,0:T(8,128)(2,1)}, bf16[8,448,256]{2,1,0:T(8,128)(2,1)}, u32[]{:S(2)}, u32[]{:S(2)}) collective-permute-start(bf16[8,448,256]{2,1,0:T(8,128)(2,1)} %get-tuple-element.517), channel_id=1, source_target_pairs={{0,1},{1,0},{2,3},{3,2},{4,5},{5,4},{6,7},{7,6},{8,9},{9,8},{10,11... | collective-permute-start | bytes 5505032 | tf_op jit(solution)/shard_map/ppermute | solution.py:693
  129.5 22.5 %collective-permute-start.18 = (bf16[8,240,256]{2,1,0:T(8,128)(2,1)}, bf16[8,240,256]{2,1,0:T(8,128)(2,1)}, u32[]{:S(2)}, u32[]{:S(2)}) collective-permute-start(bf16[8,240,256]{2,1,0:T(8,128)(2,1)} %get-tuple-element.546), channel_id=1, source_target_pairs={{0,1},{1,0},{2,3},{3,2},{4,5},{5,4},{6,7},{7,6},{8,9},{9,8},{10,11... | collective-permute-start | bytes 2949128 | tf_op jit(solution)/shard_map/ppermute | solution.py:693
  152.2 3.0 %collective-permute-start.19 = (bf16[1088,256]{1,0:T(8,128)(2,1)}, bf16[1088,256]{1,0:T(8,128)(2,1)S(1)}, u32[]{:S(2)}, u32[]{:S(2)}) collective-permute-start(bf16[1088,256]{1,0:T(8,128)(2,1)} %get-tuple-element.548), channel_id=1, source_target_pairs={{0,2},{2,0},{4,6},{6,4},{8,10},{10,8},{12,14},{14,12},{16,18},{18,... | collective-permute-start | bytes 1671176 | tf_op jit(solution)/shard_map/ppermute | solution.py:804
  152.7 23.5 %collective-permute-start.22 = (bf16[4,448,256]{2,1,0:T(8,128)(2,1)}, bf16[4,448,256]{2,1,0:T(8,128)(2,1)}, u32[]{:S(2)}, u32[]{:S(2)}) collective-permute-start(bf16[4,448,256]{2,1,0:T(8,128)(2,1)} %get-tuple-element.550), channel_id=1, source_target_pairs={{0,1},{1,0},{2,3},{3,2},{4,5},{5,4},{6,7},{7,6},{8,9},{9,8},{10,11... | collective-permute-start | bytes 2752520 | tf_op jit(solution)/shard_map/ppermute | solution.py:693
  158.5 14.8 %collective-permute-start.21 = (bf16[2,544,256]{2,1,0:T(8,128)(2,1)S(1)}, bf16[2,544,256]{2,1,0:T(8,128)(2,1)}, u32[]{:S(2)}, u32[]{:S(2)}) collective-permute-start(bf16[2,544,256]{2,1,0:T(8,128)(2,1)S(1)} %dynamic-slice_convert_fusion), channel_id=1, source_target_pairs={{0,4},{2,6},{4,0},{6,2},{8,12},{10,14},{12,8},{14,10},{16,20},{18,... | collective-permute-start | bytes 1671176 | tf_op jit(solution)/shard_map/ppermute | solution.py:804
  159.1 35.9 %collective-permute-start.26 = (bf16[4,448,256]{2,1,0:T(8,128)(2,1)}, bf16[4,448,256]{2,1,0:T(8,128)(2,1)}, u32[]{:S(2)}, u32[]{:S(2)}) collective-permute-start(bf16[4,448,256]{2,1,0:T(8,128)(2,1)} %get-tuple-element.563), channel_id=1, source_target_pairs={{0,1},{1,0},{2,3},{3,2},{4,5},{5,4},{6,7},{7,6},{8,9},{9,8},{10,11... | collective-permute-start | bytes 2752520 | tf_op jit(solution)/shard_map/ppermute | solution.py:693
  177.0 11.1 %collective-permute-start.25 = (bf16[2,136,256]{2,1,0:T(8,128)(2,1)}, bf16[2,136,256]{2,1,0:T(8,128)(2,1)S(1)}, u32[]{:S(2)}, u32[]{:S(2)}) collective-permute-start(bf16[2,136,256]{2,1,0:T(8,128)(2,1)} %get-tuple-element.659), channel_id=1, source_target_pairs={{0,24},{2,26},{4,28},{6,30},{8,16},{10,18},{12,20},{14,22},{16,8},... | collective-permute-start | bytes 417800 | tf_op jit(solution)/shard_map/ppermute | solution.py:804
  178.5 10.7 %collective-permute-start.24 = (bf16[2,136,256]{2,1,0:T(8,128)(2,1)}, bf16[2,136,256]{2,1,0:T(8,128)(2,1)S(1)}, u32[]{:S(2)}, u32[]{:S(2)}) collective-permute-start(bf16[2,136,256]{2,1,0:T(8,128)(2,1)} %get-tuple-element.660), channel_id=1, source_target_pairs={{0,16},{2,18},{4,20},{6,22},{8,24},{10,26},{12,28},{14,30},{16,0},... | collective-permute-start | bytes 417800 | tf_op jit(solution)/shard_map/ppermute | solution.py:804
  179.8 10.2 %collective-permute-start.23 = (bf16[2,136,256]{2,1,0:T(8,128)(2,1)}, bf16[2,136,256]{2,1,0:T(8,128)(2,1)}, u32[]{:S(2)}, u32[]{:S(2)}) collective-permute-start(bf16[2,136,256]{2,1,0:T(8,128)(2,1)} %get-tuple-element.658), channel_id=1, source_target_pairs={{0,8},{2,10},{4,12},{6,14},{8,0},{10,2},{12,4},{14,6},{16,24},{18,... | collective-permute-start | bytes 417800 | tf_op jit(solution)/shard_map/ppermute | solution.py:804
  195.0 4.4 %collective-permute-start.27 = (bf16[136,256]{1,0:T(8,128)(2,1)S(1)}, bf16[136,256]{1,0:T(8,128)(2,1)S(1)}, u32[]{:S(2)}, u32[]{:S(2)}) collective-permute-start(bf16[136,256]{1,0:T(8,128)(2,1)S(1)} %fusion.1), channel_id=1, source_target_pairs={{0,1},{1,0},{2,3},{3,2},{4,5},{5,4},{6,7},{7,6},{8,9},{9,8},{10,11... | collective-permute-start | bytes 208904 | tf_op jit(solution)/shard_map/ppermute | solution.py:693
  199.4 59.0 %collective-permute-start.33 = (bf16[8,576,256]{2,1,0:T(8,128)(2,1)}, bf16[8,576,256]{2,1,0:T(8,128)(2,1)}, u32[]{:S(2)}, u32[]{:S(2)}) collective-permute-start(bf16[8,576,256]{2,1,0:T(8,128)(2,1)} %get-tuple-element.600), channel_id=1, source_target_pairs={{0,1},{1,0},{2,3},{3,2},{4,5},{5,4},{6,7},{7,6},{8,9},{9,8},{10,11... | collective-permute-start | bytes 7077896 | tf_op jit(solution)/shard_map/ppermute | solution.py:693
  204.6 50.2 %collective-permute-start.31 = (bf16[8,448,256]{2,1,0:T(8,128)(2,1)}, bf16[8,448,256]{2,1,0:T(8,128)(2,1)}, u32[]{:S(2)}, u32[]{:S(2)}) collective-permute-start(bf16[8,448,256]{2,1,0:T(8,128)(2,1)} %get-tuple-element.590), channel_id=1, source_target_pairs={{2,0},{6,2},{4,6},{12,4},{14,12},{10,14},{8,10},{16,8},{18,16},{22... | collective-permute-start | bytes 5505032 | tf_op jit(solution)/shard_map/ppermute | solution.py:698
  206.8 48.0 %collective-permute-start.32 = (bf16[8,448,256]{2,1,0:T(8,128)(2,1)}, bf16[8,448,256]{2,1,0:T(8,128)(2,1)}, u32[]{:S(2)}, u32[]{:S(2)}) collective-permute-start(bf16[8,448,256]{2,1,0:T(8,128)(2,1)} %get-tuple-element.591), channel_id=1, source_target_pairs={{0,2},{2,6},{6,4},{4,12},{12,14},{14,10},{10,8},{8,16},{16,18},{18... | collective-permute-start | bytes 5505032 | tf_op jit(solution)/shard_map/ppermute | solution.py:698
  209.0 25.4 %collective-permute-start.28 = (bf16[136,256]{1,0:T(8,128)(2,1)S(1)}, bf16[136,256]{1,0:T(8,128)(2,1)S(1)}, u32[]{:S(2)}, u32[]{:S(2)}) collective-permute-start(bf16[136,256]{1,0:T(8,128)(2,1)S(1)} %fusion.refs_0_), channel_id=1, source_target_pairs={{0,8},{2,10},{4,12},{6,14},{8,0},{10,2},{12,4},{14,6},{16,24},{18,... | collective-permute-start | bytes 208904 | tf_op jit(solution)/shard_map/ppermute | solution.py:804
  236.6 6.4 %collective-permute-start.29 = (bf16[272,256]{1,0:T(8,128)(2,1)}, bf16[272,256]{1,0:T(8,128)(2,1)S(1)}, u32[]{:S(2)}, u32[]{:S(2)}) collective-permute-start(bf16[272,256]{1,0:T(8,128)(2,1)} %join.3.refs_0_), channel_id=1, source_target_pairs={{0,16},{2,18},{4,20},{6,22},{8,24},{10,26},{12,28},{14,30},{16,0},... | collective-permute-start | bytes 417800 | tf_op jit(solution)/shard_map/ppermute | solution.py:804
  245.4 6.8 %collective-permute-start.30 = (bf16[544,256]{1,0:T(8,128)(2,1)}, bf16[544,256]{1,0:T(8,128)(2,1)S(1)}, u32[]{:S(2)}, u32[]{:S(2)}) collective-permute-start(bf16[544,256]{1,0:T(8,128)(2,1)} %join.4.refs_0_), channel_id=1, source_target_pairs={{0,4},{2,6},{4,0},{6,2},{8,12},{10,14},{12,8},{14,10},{16,20},{18,... | collective-permute-start | bytes 835592 | tf_op jit(solution)/shard_map/ppermute | solution.py:804
  258.4 6.0 %collective-permute-start.34 = (bf16[1088,256]{1,0:T(8,128)(2,1)S(1)}, bf16[1088,256]{1,0:T(8,128)(2,1)S(1)}, u32[]{:S(2)}, u32[]{:S(2)}) collective-permute-start(bf16[1088,256]{1,0:T(8,128)(2,1)S(1)} %copy-done.7), channel_id=1, source_target_pairs={{0,2},{2,0},{4,6},{6,4},{8,10},{10,8},{12,14},{14,12},{16,18},{18,... | collective-permute-start | bytes 1671176 | tf_op jit(solution)/shard_map/ppermute | solution.py:804
  (21 other events, 171.8 us)

commit v4 on v3

--- a/solution.py
+++ b/solution.py
@@ -33,6 +33,7 @@
 
 NO_COST = pl.CostEstimate(flops=0, bytes_accessed=1024, transcendentals=0)
 SOME_COST = pl.CostEstimate(flops=10**10, bytes_accessed=1024, transcendentals=0)
+LAST_COST = pl.CostEstimate(flops=2 * 10**10, bytes_accessed=1024, transcendentals=0)
 COST_PER_ROW = 7 * 10**7
 
 
@@ -433,7 +434,7 @@
             pltpu.SemaphoreType.DMA((5,)),
         ]
         + tails,
-        cost_estimate=NO_COST,
+        cost_estimate=LAST_COST if base == 0 else NO_COST,
         compiler_params=PARAMS,
         name="unpack",
     )(who, counts, plan, *mine, theirs, *outs)
@@ -1008,24 +1009,20 @@
     total = (mine + swap_tensor(other).astype(F32)).astype(BF16)
     total, yd1_send = together(total, result1[2])
     yd1_got = swap_tensor(yd1_send)
+    for bit, many in reversed(others):
+        for step in range(bit, bit + many):
+            total = gather_step(total, (step, 1), place, dp_size)
     plan, total = together(plan, total)
     to_left, to_right = handback(
         dims, who, plan, result3[:2], (y3_got, d3_got), *last, moved
     )
-    total, to_left = together(total, to_left)
     back = (shift(to_left, order, -1), shift(to_right, order, 1))
-    for bit, many in reversed(others):
-        for step in range(bit, bit + many):
-            total = gather_step(total, (step, 1), place, dp_size)
+    total = gather_step(total, across, place, dp_size)
+    total_got = flipped(total, 1, dp_size)
     outs = place_grads(outs, *last, result3[1], d3_got)
-    total, outs = together(total, outs)
-    total = gather_step(total, across, place, dp_size)
+    outs = place_all(outs, 0, first, plan, result1, yd1_got)
+    sums = finish((place & 1).astype(jnp.int32)[None], total, total_got)
     outs = unpack(dims, who, counts, plan, back[:1], back[1], outs, None, moved)
-    total, outs, yd1_got = together(total, outs, yd1_got)
-    total_got = flipped(total, 1, dp_size)
-    outs = place_all(outs, 0, first, plan, result1, yd1_got)
-    outs, total_got = together(outs, total_got)
-    sums = finish((place & 1).astype(jnp.int32)[None], total, total_got)
     grad_in, grad_out, bias_in_grad, bias_out_grad = sums
     return (*outs, grad_in, bias_in_grad, grad_out, bias_out_grad)
 

time: 271 us -> 265 us (0.978)
  starting transfers between devices: 45 us -> 40.6 us
    ppermute x19, waiting for transfers between devices: 49.2 us -> 37.1 us  [flipped(): return lax.ppermute(value, 'dp', [(i, i ^ flip) for i in range(size)])]
    ppermute x10, waiting for transfers between devices: 21.2 us -> 30.1 us  [swap_tensor(): return lax.ppermute(value, 'tensor', [(0, 1), (1, 0)])]
    ppermute x19, starting transfers between devices: 22.2 us -> 16.2 us  [flipped(): return lax.ppermute(value, 'dp', [(i, i ^ flip) for i in range(size)])]
    unnamed x40 -> x38, local copies, waits for them, and re-layouts: 4.95 us -> 6.28 us
  transfers between devices with their start and end apart: 33 -> 33, of which waited for: 17 -> 19; matrix products, arithmetic and copies ran while one was open for 3% -> 3% of each run, Pallas kernels for 45% -> 45%
where the time goes in v4:
time: 265 us; the launch traced here: 263 us
  Pallas kernels  124 us (47%)
  waiting for transfers between devices  81.6 us (31%)
  starting transfers between devices  40.6 us (15%)
  local copies, waits for them, and re-layouts  7.7 us (3%)
  other arithmetic  7.18 us (3%)
    pallas_call x3, Pallas kernels, run_blocks(): pl.pallas_call(functools.partial(blocks_kernel, dims, base, rows, tile, f...  63.3 us
    ppermute x19, waiting for transfers between devices, flipped(): return lax.ppermute(value, 'dp', [(i, i ^ flip) for i in range(size)])  37.1 us
    ppermute x10, waiting for transfers between devices, swap_tensor(): return lax.ppermute(value, 'tensor', [(0, 1), (1, 0)])  30.1 us
    pallas_call x5, Pallas kernels, unpack(): pl.pallas_call(functools.partial(unpack_kernel, dims, base, rows, streams...  19.9 us
    ppermute x19, starting transfers between devices, flipped(): return lax.ppermute(value, 'dp', [(i, i ^ flip) for i in range(size)])  16.2 us
    pallas_call x3, Pallas kernels, pack(): pl.pallas_call(functools.partial(pack_kernel, dims, base, rows, len(neigh...  14.5 us
    ppermute x4, waiting for transfers between devices, shift(): lax.ppermute(value, 'dp', pairs if step == 1 else [(b, a) for a, b in pai...  14.4 us
    ppermute x10, starting transfers between devices, swap_tensor(): return lax.ppermute(value, 'tensor', [(0, 1), (1, 0)])  12.5 us
  transfers between devices with their start and end apart: 33, of which 19 were waited for; matrix products, arithmetic and copies ran while one was open for 3% of the time, Pallas kernels for 45%

profile of v4, /device:TPU:10, one launch (start us, length us, event | category | flops | bytes accessed | tf_op | source)
XLA Modules:
  0.0 263.5 jit_solution(6978663523642396248)
XLA Ops:
  6.2 5.7 %pack.8 = (bf16[8,576,256]{2,1,0:T(8,128)(2,1)}, bf16[8,576,256]{2,1,0:T(8,128)(2,1)}) custom-call(s32[8]{0:T(128)S(1)} %get-tuple-element.771.who, s32[16]{0:T(128)} %counts.20, bf16[4096,256]{1,0:T(8,128)(2,1)} %refs_1_.5, bf16[3,4096,256]{2,1,0:T(8,128)(2,1)} %refs_2_.5, bf16[4096,256]{1,0:T(8,128)(2,1)} %refs_3_.5, bf16[3,4096,256]{2,1,0:T(8,128)(2,1)} %refs_4_.1), custom_call_target="tpu_custom_call" | custom-call | bytes 1024 | tf_op jit(solution)/shard_map/pack/pallas_call | solution.py:273
  19.4 3.1 %collective-permute-done.7 = s32[16]{0:T(128)S(1)} collective-permute-done((s32[16]{0:T(128)S(1)}, s32[16]{0:T(128)S(1)}, u32[]{:S(2)}, u32[]{:S(2)}) %collective-permute-start.7) | collective-permute-done | bytes 96 | tf_op jit(solution)/shard_map/ppermute | solution.py:805
  22.5 2.6 collective-permute-start.8
  28.6 3.7 %pack.9 = (bf16[8,240,256]{2,1,0:T(8,128)(2,1)}, bf16[8,240,256]{2,1,0:T(8,128)(2,1)}) custom-call(s32[8]{0:T(128)S(1)} %get-tuple-element.771.who, s32[16]{0:T(128)S(1)} %copy-done.14, bf16[4096,256]{1,0:T(8,128)(2,1)S(1)} %copy-done, bf16[3,4096,256]{2,1,0:T(8,128)(2,1)} %refs_2_.5, bf16[4096,256]{1,0:T(8,128)(2,1)} %refs_3_.5, bf16[3,4096,256]{2,1,0:T(8,128)(2,1)} %refs_4_.1), custom_call_target="tpu_custom_call" | custom-call | bytes 1024 | tf_op jit(solution)/shard_map/pack/pallas_call | solution.py:273
  34.4 4.1 %export.1 = (bf16[8,448,256]{2,1,0:T(8,128)(2,1)}, bf16[8,448,256]{2,1,0:T(8,128)(2,1)}) custom-call(s32[8]{0:T(128)S(1)} %get-tuple-element.771.who, s32[16]{0:T(128)S(1)} %copy-done.14, s32[8]{0:T(128)} %plan.1.refs_0_.rest_0_, bf16[4096,256]{1,0:T(8,128)(2,1)S(1)} %copy-done, bf16[3,4096,256]{2,1,0:T(8,128)(2,1)} %refs_2_.5, bf16[4096,256]{1,0:T(8,128)(2,1)} %refs_3_.5, ...), custom_call_target="tpu_custom_call" | custom-call | bytes 1024 | tf_op jit(solution)/shard_map/export/pallas_call | solution.py:314
  40.5 4.7 %collective-permute-start.14 = (bf16[8,448,256]{2,1,0:T(8,128)(2,1)}, bf16[8,448,256]{2,1,0:T(8,128)(2,1)}, u32[]{:S(2)}, u32[]{:S(2)}) collective-permute-start(bf16[8,448,256]{2,1,0:T(8,128)(2,1)} %get-tuple-element.467), channel_id=1, source_target_pairs={{2,0},{6,2},{4,6},{12,4},{14,12},{10,14},{8,10},{16,8},{18,16},{22... | collective-permute-start | bytes 5505032 | tf_op jit(solution)/shard_map/ppermute | solution.py:699
  45.8 4.6 %assemble.1 = (bf16[2,512,512]{2,1,0:T(8,128)(2,1)S(1)}, bf16[2,512,512]{2,1,0:T(8,128)(2,1)}, bf16[2,512,512]{2,1,0:T(8,128)(2,1)}, bf16[2,512,512]{2,1,0:T(8,128)(2,1)}, f32[2,2,512]{2,1,0:T(2,128)S(1)}) custom-call(s32[8]{0:T(128)S(1)} %get-tuple-element.771.who, bf16[2,512,256]{2,1,0:T(8,128)(2,1)} %w_in.3, bf16[2,256,512]{2,1,0:T(8,128)(2,1)} %w_out.3, ...), custom_call_target="tpu_custom_call" | custom-call | bytes 1024 | tf_op jit(solution)/shard_map/assemble/pallas_call | solution.py:792
  50.4 3.0 %blank.1 = (bf16[4096,256]{1,0:T(8,128)(2,1)}, bf16[3,4096,256]{2,1,0:T(8,128)(2,1)}, bf16[4096,256]{1,0:T(8,128)(2,1)}, bf16[3,4096,256]{2,1,0:T(8,128)(2,1)}) custom-call(s32[16]{0:T(128)S(1)} %copy-done.14), custom_call_target="tpu_custom_call" | custom-call | bytes 1024 | tf_op jit(solution)/shard_map/blank/pallas_call | solution.py:476
  53.4 11.4 %collective-permute-done.13.refs_5_ = bf16[8,448,256]{2,1,0:T(8,128)(2,1)} collective-permute-done((bf16[8,448,256]{2,1,0:T(8,128)(2,1)}, bf16[8,448,256]{2,1,0:T(8,128)(2,1)}, u32[]{:S(2)}, u32[]{:S(2)}) %collective-permute-start.13) | collective-permute-done | bytes 1835040 | tf_op jit(solution)/shard_map/ppermute | solution.py:699
  66.2 5.1 %pack.10 = (bf16[8,448,256]{2,1,0:T(8,128)(2,1)}, bf16[8,448,256]{2,1,0:T(8,128)(2,1)}) custom-call(s32[8]{0:T(128)S(1)} %get-tuple-element.771.who, s32[16]{0:T(128)S(1)} %copy-done.14, s32[8]{0:T(128)} %plan.1.refs_0_.rest_0_, bf16[4096,256]{1,0:T(8,128)(2,1)S(1)} %copy-done, bf16[3,4096,256]{2,1,0:T(8,128)(2,1)} %refs_2_.5, bf16[4096,256]{1,0:T(8,128)(2,1)} %refs_3_.5, ...), custom_call_target="tpu_custom_call" | custom-call | bytes 1024 | tf_op jit(solution)/shard_map/pack/pallas_call | solution.py:273
  71.3 14.4 %collective-permute-done.15.got = bf16[8,240,256]{2,1,0:T(8,128)(2,1)} collective-permute-done((bf16[8,240,256]{2,1,0:T(8,128)(2,1)}, bf16[8,240,256]{2,1,0:T(8,128)(2,1)}, u32[]{:S(2)}, u32[]{:S(2)}) %collective-permute-start.15) | collective-permute-done | bytes 983072 | tf_op jit(solution)/shard_map/ppermute | solution.py:694
  87.3 24.5 %blocks.8 = (bf16[4,576,256]{2,1,0:T(8,128)(2,1)}, bf16[4,576,256]{2,1,0:T(8,128)(2,1)}, bf16[8,576,256]{2,1,0:T(8,128)(2,1)}, f32[2,2176,256]{2,1,0:T(8,128)}, f32[4,8,512]{2,1,0:T(8,128)S(1)}) custom-call(s32[8]{0:T(128)S(1)} %get-tuple-element.771.who, bf16[8,576,256]{2,1,0:T(8,128)(2,1)} %get-tuple-element.507.own, ...), custom_call_target="tpu_custom_call" | custom-call | flops 40320000000 | bytes 1024 | tf_op jit(solution)/shard_map/blocks/pallas_call | solution.py:667
  112.7 16.8 %blocks.9 = (bf16[4,240,256]{2,1,0:T(8,128)(2,1)}, bf16[4,240,256]{2,1,0:T(8,128)(2,1)}, bf16[8,240,256]{2,1,0:T(8,128)(2,1)}, f32[2,2176,256]{2,1,0:T(8,128)}, f32[4,8,512]{2,1,0:T(8,128)S(1)}) custom-call(s32[8]{0:T(128)S(1)} %get-tuple-element.842, bf16[8,240,256]{2,1,0:T(8,128)(2,1)} %get-tuple-element.505.own, ...), custom_call_target="tpu_custom_call", output_to_operand_aliasing={{3}: (9, {}), {4}: (10, {})} | custom-call | bytes 1024 | tf_op jit(solution)/shard_map/blocks/pallas_call | solution.py:667
  130.1 22.0 %blocks.10 = (bf16[4,448,256]{2,1,0:T(8,128)(2,1)}, bf16[4,448,256]{2,1,0:T(8,128)(2,1)}, bf16[4,448,256]{2,1,0:T(8,128)(2,1)}, bf16[4,448,256]{2,1,0:T(8,128)(2...) custom-call(s32[8]{0:T(128)S(1)} %get-tuple-element.842, ...), custom_call_target="tpu_custom_call" | custom-call | bytes 1024 | tf_op jit(solution)/shard_map/blocks/pallas_call | solution.py:667
  160.7 3.5 %unpack.10 = (bf16[4096,256]{1,0:T(8,128)(2,1)S(1)}, bf16[3,4096,256]{2,1,0:T(8,128)(2,1)}, bf16[4096,256]{1,0:T(8,128)(2,1)}, bf16[3,4096,256]{2,1,0:T(8,128)(2,1)}) custom-call(s32[8]{0:T(128)S(1)} %get-tuple-element.842, s32[16]{0:T(128)S(1)} %get-tuple-element.852, ...), custom_call_target="tpu_custom_call", output_to_operand_aliasing={{0}: (6, {}), {1}: (7, {}), {2}: (8, {}), {3}: (9, {})} | custom-call | bytes 1024 | tf_op jit(solution)/shard_map/unpack/pallas_call | solution.py:426
  164.2 9.2 %collective-permute-done.21 = bf16[2,544,256]{2,1,0:T(8,128)(2,1)} collective-permute-done((bf16[2,544,256]{2,1,0:T(8,128)(2,1)S(1)}, bf16[2,544,256]{2,1,0:T(8,128)(2,1)}, u32[]{:S(2)}, u32[]{:S(2)}) %collective-permute-start.21) | collective-permute-done | bytes 557088 | tf_op jit(solution)/shard_map/ppermute | solution.py:805
  177.5 2.5 collective-permute-start.24
  180.4 3.6 %unpack.11 = (bf16[4096,256]{1,0:T(8,128)(2,1)S(1)}, bf16[3,4096,256]{2,1,0:T(8,128)(2,1)}) custom-call(s32[8]{0:T(128)S(1)} %get-tuple-element.842, s32[16]{0:T(128)S(1)} %get-tuple-element.852, s32[8]{0:T(128)} %plan.1.refs_0_.rest_0_, bf16[4,448,256]{2,1,0:T(8,128)(2,1)} %get-tuple-element.546.refs_0_, ...), custom_call_target="tpu_custom_call", output_to_operand_aliasing={{0}: (5, {}), {1}: (6, {})} | custom-call | bytes 1024 | tf_op jit(solution)/shard_map/unpack/pallas_call | solution.py:426
  184.1 4.9 %collective-permute-done.24 = bf16[2,136,256]{2,1,0:T(8,128)(2,1)S(1)} collective-permute-done((bf16[2,136,256]{2,1,0:T(8,128)(2,1)}, bf16[2,136,256]{2,1,0:T(8,128)(2,1)S(1)}, u32[]{:S(2)}, u32[]{:S(2)}) %collective-permute-start.24) | collective-permute-done | bytes 139296 | tf_op jit(solution)/shard_map/ppermute | solution.py:805
  192.5 2.5 collective-permute-done.26.refs_3_.refs_1_
  196.6 2.8 %collective-permute-done.27 = bf16[136,256]{1,0:T(8,128)(2,1)S(1)} collective-permute-done((bf16[136,256]{1,0:T(8,128)(2,1)S(1)}, bf16[136,256]{1,0:T(8,128)(2,1)S(1)}, u32[]{:S(2)}, u32[]{:S(2)}) %collective-permute-start.27) | collective-permute-done | bytes 69664 | tf_op jit(solution)/shard_map/ppermute | solution.py:694
  201.5 3.8 %collective-permute-done.28.refs_1_ = bf16[136,256]{1,0:T(8,128)(2,1)S(1)} collective-permute-done((bf16[136,256]{1,0:T(8,128)(2,1)S(1)}, bf16[136,256]{1,0:T(8,128)(2,1)S(1)}, u32[]{:S(2)}, u32[]{:S(2)}) %collective-permute-start.28) | collective-permute-done | bytes 69664 | tf_op jit(solution)/shard_map/ppermute | solution.py:805
  207.5 2.7 %collective-permute-start.29 = (bf16[272,256]{1,0:T(8,128)(2,1)}, bf16[272,256]{1,0:T(8,128)(2,1)S(1)}, u32[]{:S(2)}, u32[]{:S(2)}) collective-permute-start(bf16[272,256]{1,0:T(8,128)(2,1)} %join.3.refs_0_), channel_id=1, source_target_pairs={{0,16},{2,18},{4,20},{6,22},{8,24},{10,26},{12,28},{14,30},{16,0},... | collective-permute-start | bytes 417800 | tf_op jit(solution)/shard_map/ppermute | solution.py:805
  210.2 4.2 %collective-permute-done.29.refs_1_ = bf16[272,256]{1,0:T(8,128)(2,1)S(1)} collective-permute-done((bf16[272,256]{1,0:T(8,128)(2,1)}, bf16[272,256]{1,0:T(8,128)(2,1)S(1)}, u32[]{:S(2)}, u32[]{:S(2)}) %collective-permute-start.29) | collective-permute-done | bytes 139296 | tf_op jit(solution)/shard_map/ppermute | solution.py:805
  217.4 6.2 %collective-permute-done.33.refs_1_ = bf16[544,256]{1,0:T(8,128)(2,1)S(1)} collective-permute-done((bf16[544,256]{1,0:T(8,128)(2,1)}, bf16[544,256]{1,0:T(8,128)(2,1)S(1)}, u32[]{:S(2)}, u32[]{:S(2)}) %collective-permute-start.33) | collective-permute-done | bytes 278560 | tf_op jit(solution)/shard_map/ppermute | solution.py:805
  226.3 3.5 %handback.1 = (bf16[8,448,256]{2,1,0:T(8,128)(2,1)}, bf16[8,448,256]{2,1,0:T(8,128)(2,1)}) custom-call(s32[8]{0:T(128)S(1)} %get-tuple-element.842, s32[8]{0:T(128)} %plan.1.refs_0_.rest_0_, bf16[4,448,256]{2,1,0:T(8,128)(2,1)} %get-tuple-element.546.refs_0_, bf16[4,448,256]{2,1,0:T(8,128)(2,1)} %get-tuple-element.558.refs_1_.refs_0_, ...), custom_call_target="tpu_custom_call" | custom-call | flops 10000000000 | bytes 1024 | tf_op jit(solution)/shard_map/handback/pallas_call | solution.py:362
  229.8 3.3 %collective-permute-start.30 = (bf16[8,448,256]{2,1,0:T(8,128)(2,1)}, bf16[8,448,256]{2,1,0:T(8,128)(2,1)}, u32[]{:S(2)}, u32[]{:S(2)}) collective-permute-start(bf16[8,448,256]{2,1,0:T(8,128)(2,1)} %get-tuple-element.560), channel_id=1, source_target_pairs={{2,0},{6,2},{4,6},{12,4},{14,12},{10,14},{8,10},{16,8},{18,16},{22... | collective-permute-start | bytes 5505032 | tf_op jit(solution)/shard_map/ppermute | solution.py:699
  235.0 3.3 %unpack.12 = (bf16[4096,256]{1,0:T(8,128)(2,1)}, bf16[3,4096,256]{2,1,0:T(8,128)(2,1)}) custom-call(s32[8]{0:T(128)S(1)} %get-tuple-element.842, s32[16]{0:T(128)S(1)} %get-tuple-element.852, s32[8]{0:T(128)} %plan.1.refs_0_.rest_0_, bf16[4,448,256]{2,1,0:T(8,128)(2,1)} %get-tuple-element.558.refs_1_.refs_0_, ...), custom_call_target="tpu_custom_call", output_to_operand_aliasing={{0}: (5, {}), {1}: (6, {})} | custom-call | bytes 1024 | tf_op jit(solution)/shard_map/unpack/pallas_call | solution.py:426
  239.2 2.6 finish.1
  241.8 9.2 %collective-permute-done.32.refs_2_ = bf16[8,576,256]{2,1,0:T(8,128)(2,1)} collective-permute-done((bf16[8,576,256]{2,1,0:T(8,128)(2,1)}, bf16[8,576,256]{2,1,0:T(8,128)(2,1)}, u32[]{:S(2)}, u32[]{:S(2)}) %collective-permute-start.32) | collective-permute-done | bytes 2359328 | tf_op jit(solution)/shard_map/ppermute | solution.py:694
  251.0 5.9 %unpack.13 = (bf16[4096,256]{1,0:T(8,128)(2,1)S(1)}, bf16[3,4096,256]{2,1,0:T(8,128)(2,1)}, bf16[4096,256]{1,0:T(8,128)(2,1)}, bf16[3,4096,256]{2,1,0:T(8,128)(2,1)}) custom-call(s32[8]{0:T(128)S(1)} %get-tuple-element.842, s32[16]{0:T(128)S(1)} %get-tuple-element.852, ...), custom_call_target="tpu_custom_call", output_to_operand_aliasing={{0}: (6, {}), {1}: (7, {}), {2}: (8, {}), {3}: (9, {})} | custom-call | flops 20000000000 | bytes 1024 | tf_op jit(solution)/shard_map/unpack/pallas_call | solution.py:426
  258.5 3.6 %unpack.14 = (bf16[4096,256]{1,0:T(8,128)(2,1)S(1)}, bf16[3,4096,256]{2,1,0:T(8,128)(2,1)}, bf16[4096,256]{1,0:T(8,128)(2,1)}, bf16[3,4096,256]{2,1,0:T(8,128)(2,1)}) custom-call(s32[8]{0:T(128)S(1)} %get-tuple-element.842, s32[16]{0:T(128)S(1)} %get-tuple-element.852, ...), custom_call_target="tpu_custom_call", output_to_operand_aliasing={{0}: (5, {}), {1}: (6, {}), {2}: (7, {}), {3}: (8, {})} | custom-call | bytes 1024 | tf_op jit(solution)/shard_map/unpack/pallas_call | solution.py:426
  (106 shorter events, 59.3 us)
Async XLA Ops:
  2.8 9.1 %collective-permute-start.5 = (bf16[512,256]{1,0:T(8,128)(2,1)}, bf16[512,256]{1,0:T(8,128)(2,1)S(1)}, u32[]{:S(2)}, u32[]{:S(2)}) collective-permute-start(bf16[512,256]{1,0:T(8,128)(2,1)} %get-tuple-element.456), channel_id=1, source_target_pairs={{0,1},{1,0},{2,3},{3,2},{4,5},{5,4},{6,7},{7,6},{8,9},{9,8},{10,11... | collective-permute-start | bytes 786440 | tf_op jit(solution)/shard_map/ppermute | solution.py:694
  5.1 6.8 %collective-permute-start.6 = (f32[2,2,256]{2,1,0:T(2,128)S(1)}, f32[2,2,256]{2,1,0:T(2,128)S(1)}, u32[]{:S(2)}, u32[]{:S(2)}) collective-permute-start(f32[2,2,256]{2,1,0:T(2,128)S(1)} %pad_maximum_fusion), channel_id=1, source_target_pairs={{0,1},{1,0},{2,3},{3,2},{4,5},{5,4},{6,7},{7,6},{8,9},{9,8},{10,11... | collective-permute-start | bytes 12296 | tf_op jit(solution)/shard_map/ppermute | solution.py:694
  11.9 75.4 %collective-permute-start.17 = (bf16[8,576,256]{2,1,0:T(8,128)(2,1)}, bf16[8,576,256]{2,1,0:T(8,128)(2,1)}, u32[]{:S(2)}, u32[]{:S(2)}) collective-permute-start(bf16[8,576,256]{2,1,0:T(8,128)(2,1)} %get-tuple-element.508), channel_id=1, source_target_pairs={{0,1},{1,0},{2,3},{3,2},{4,5},{5,4},{6,7},{7,6},{8,9},{9,8},{10,11... | collective-permute-start | bytes 7077896 | tf_op jit(solution)/shard_map/ppermute | solution.py:694
  14.1 2.5 collective-permute-start.2
  14.2 3.6 %collective-permute-start.3 = (s32[16]{0:T(128)S(1)}, s32[16]{0:T(128)S(1)}, u32[]{:S(2)}, u32[]{:S(2)}) collective-permute-start(s32[16]{0:T(128)S(1)} %compare_select_fusion), channel_id=1, source_target_pairs={{0,4},{2,6},{4,0},{6,2},{8,12},{10,14},{12,8},{14,10},{16,20},{18,... | collective-permute-start | bytes 200 | tf_op jit(solution)/shard_map/ppermute | solution.py:805
  14.8 3.4 %collective-permute-start.4 = (s32[16]{0:T(128)S(1)}, s32[16]{0:T(128)S(1)}, u32[]{:S(2)}, u32[]{:S(2)}) collective-permute-start(s32[16]{0:T(128)S(1)} %compare_select_fusion), channel_id=1, source_target_pairs={{0,6},{2,4},{4,2},{6,0},{8,14},{10,12},{12,10},{14,8},{16,22},{18,... | collective-permute-start | bytes 200 | tf_op jit(solution)/shard_map/ppermute | solution.py:805
  16.1 18.3 %collective-permute-start.10 = (bf16[512,256]{1,0:T(8,128)(2,1)S(1)}, bf16[512,256]{1,0:T(8,128)(2,1)S(1)}, u32[]{:S(2)}, u32[]{:S(2)}) collective-permute-start(bf16[512,256]{1,0:T(8,128)(2,1)S(1)} %collective-permute-done.5.refs_0_), channel_id=1, source_target_pairs={{0,4},{2,6},{4,0},{6,2},{8,12},{10,14},{12,8},{14,10},{16,20},{18,... | collective-permute-start | bytes 786440 | tf_op jit(solution)/shard_map/ppermute | solution.py:805
  16.6 17.8 %collective-permute-start.11 = (bf16[512,256]{1,0:T(8,128)(2,1)S(1)}, bf16[512,256]{1,0:T(8,128)(2,1)S(1)}, u32[]{:S(2)}, u32[]{:S(2)}) collective-permute-start(bf16[512,256]{1,0:T(8,128)(2,1)S(1)} %collective-permute-done.5.refs_0_), channel_id=1, source_target_pairs={{0,2},{2,0},{4,6},{6,4},{8,10},{10,8},{12,14},{14,12},{16,18},{18,... | collective-permute-start | bytes 786440 | tf_op jit(solution)/shard_map/ppermute | solution.py:805
  17.8 16.6 %collective-permute-start.12 = (bf16[512,256]{1,0:T(8,128)(2,1)S(1)}, bf16[512,256]{1,0:T(8,128)(2,1)S(1)}, u32[]{:S(2)}, u32[]{:S(2)}) collective-permute-start(bf16[512,256]{1,0:T(8,128)(2,1)S(1)} %collective-permute-done.5.refs_0_), channel_id=1, source_target_pairs={{0,6},{2,4},{4,2},{6,0},{8,14},{10,12},{12,10},{14,8},{16,22},{18,... | collective-permute-start | bytes 786440 | tf_op jit(solution)/shard_map/ppermute | solution.py:805
  18.9 3.6 %collective-permute-start.7 = (s32[16]{0:T(128)S(1)}, s32[16]{0:T(128)S(1)}, u32[]{:S(2)}, u32[]{:S(2)}) collective-permute-start(s32[16]{0:T(128)S(1)} %add_add_fusion.1), channel_id=1, source_target_pairs={{0,8},{2,10},{4,12},{6,14},{8,0},{10,2},{12,4},{14,6},{16,24},{18,... | collective-permute-start | bytes 200 | tf_op jit(solution)/shard_map/ppermute | solution.py:805
  22.5 4.4 %collective-permute-start.8 = (s32[16]{0:T(128)S(1)}, s32[16]{0:T(128)S(1)}, u32[]{:S(2)}, u32[]{:S(2)}) collective-permute-start(s32[16]{0:T(128)S(1)} %add_add_fusion.1), channel_id=1, source_target_pairs={{0,16},{2,18},{4,20},{6,22},{8,24},{10,26},{12,28},{14,30},{16,0},... | collective-permute-start | bytes 200 | tf_op jit(solution)/shard_map/ppermute | solution.py:805
  26.9 5.4 %collective-permute-start.9 = (s32[16]{0:T(128)S(1)}, s32[16]{0:T(128)S(1)}, u32[]{:S(2)}, u32[]{:S(2)}) collective-permute-start(s32[16]{0:T(128)S(1)} %add_add_fusion.1), channel_id=1, source_target_pairs={{0,24},{2,26},{4,28},{6,30},{8,16},{10,18},{12,20},{14,22},{16,8},... | collective-permute-start | bytes 200 | tf_op jit(solution)/shard_map/ppermute | solution.py:805
  38.6 26.2 %collective-permute-start.13 = (bf16[8,448,256]{2,1,0:T(8,128)(2,1)}, bf16[8,448,256]{2,1,0:T(8,128)(2,1)}, u32[]{:S(2)}, u32[]{:S(2)}) collective-permute-start(bf16[8,448,256]{2,1,0:T(8,128)(2,1)} %get-tuple-element.482), channel_id=1, source_target_pairs={{0,2},{2,6},{6,4},{4,12},{12,14},{14,10},{10,8},{8,16},{16,18},{18... | collective-permute-start | bytes 5505032 | tf_op jit(solution)/shard_map/ppermute | solution.py:699
  40.5 25.8 %collective-permute-start.14 = (bf16[8,448,256]{2,1,0:T(8,128)(2,1)}, bf16[8,448,256]{2,1,0:T(8,128)(2,1)}, u32[]{:S(2)}, u32[]{:S(2)}) collective-permute-start(bf16[8,448,256]{2,1,0:T(8,128)(2,1)} %get-tuple-element.467), channel_id=1, source_target_pairs={{2,0},{6,2},{4,6},{12,4},{14,12},{10,14},{8,10},{16,8},{18,16},{22... | collective-permute-start | bytes 5505032 | tf_op jit(solution)/shard_map/ppermute | solution.py:699
  45.2 40.6 %collective-permute-start.15 = (bf16[8,240,256]{2,1,0:T(8,128)(2,1)}, bf16[8,240,256]{2,1,0:T(8,128)(2,1)}, u32[]{:S(2)}, u32[]{:S(2)}) collective-permute-start(bf16[8,240,256]{2,1,0:T(8,128)(2,1)} %get-tuple-element.497), channel_id=1, source_target_pairs={{0,1},{1,0},{2,3},{3,2},{4,5},{5,4},{6,7},{7,6},{8,9},{9,8},{10,11... | collective-permute-start | bytes 2949128 | tf_op jit(solution)/shard_map/ppermute | solution.py:694
  85.8 44.3 %collective-permute-start.16 = (bf16[8,448,256]{2,1,0:T(8,128)(2,1)}, bf16[8,448,256]{2,1,0:T(8,128)(2,1)}, u32[]{:S(2)}, u32[]{:S(2)}) collective-permute-start(bf16[8,448,256]{2,1,0:T(8,128)(2,1)} %get-tuple-element.499), channel_id=1, source_target_pairs={{0,1},{1,0},{2,3},{3,2},{4,5},{5,4},{6,7},{7,6},{8,9},{9,8},{10,11... | collective-permute-start | bytes 5505032 | tf_op jit(solution)/shard_map/ppermute | solution.py:694
  129.5 22.6 %collective-permute-start.18 = (bf16[8,240,256]{2,1,0:T(8,128)(2,1)}, bf16[8,240,256]{2,1,0:T(8,128)(2,1)}, u32[]{:S(2)}, u32[]{:S(2)}) collective-permute-start(bf16[8,240,256]{2,1,0:T(8,128)(2,1)} %get-tuple-element.528), channel_id=1, source_target_pairs={{0,1},{1,0},{2,3},{3,2},{4,5},{5,4},{6,7},{7,6},{8,9},{9,8},{10,11... | collective-permute-start | bytes 2949128 | tf_op jit(solution)/shard_map/ppermute | solution.py:694
  152.2 3.0 %collective-permute-start.20 = (bf16[1088,256]{1,0:T(8,128)(2,1)}, bf16[1088,256]{1,0:T(8,128)(2,1)S(1)}, u32[]{:S(2)}, u32[]{:S(2)}) collective-permute-start(bf16[1088,256]{1,0:T(8,128)(2,1)} %get-tuple-element.531), channel_id=1, source_target_pairs={{0,2},{2,0},{4,6},{6,4},{8,10},{10,8},{12,14},{14,12},{16,18},{18,... | collective-permute-start | bytes 1671176 | tf_op jit(solution)/shard_map/ppermute | solution.py:805
  152.7 23.5 %collective-permute-start.22 = (bf16[4,448,256]{2,1,0:T(8,128)(2,1)}, bf16[4,448,256]{2,1,0:T(8,128)(2,1)}, u32[]{:S(2)}, u32[]{:S(2)}) collective-permute-start(bf16[4,448,256]{2,1,0:T(8,128)(2,1)} %get-tuple-element.532), channel_id=1, source_target_pairs={{0,1},{1,0},{2,3},{3,2},{4,5},{5,4},{6,7},{7,6},{8,9},{9,8},{10,11... | collective-permute-start | bytes 2752520 | tf_op jit(solution)/shard_map/ppermute | solution.py:694
  158.6 14.8 %collective-permute-start.21 = (bf16[2,544,256]{2,1,0:T(8,128)(2,1)S(1)}, bf16[2,544,256]{2,1,0:T(8,128)(2,1)}, u32[]{:S(2)}, u32[]{:S(2)}) collective-permute-start(bf16[2,544,256]{2,1,0:T(8,128)(2,1)S(1)} %dynamic-slice_convert_fusion), channel_id=1, source_target_pairs={{0,4},{2,6},{4,0},{6,2},{8,12},{10,14},{12,8},{14,10},{16,20},{18,... | collective-permute-start | bytes 1671176 | tf_op jit(solution)/shard_map/ppermute | solution.py:805
  159.2 35.7 %collective-permute-start.26 = (bf16[4,448,256]{2,1,0:T(8,128)(2,1)}, bf16[4,448,256]{2,1,0:T(8,128)(2,1)}, u32[]{:S(2)}, u32[]{:S(2)}) collective-permute-start(bf16[4,448,256]{2,1,0:T(8,128)(2,1)} %get-tuple-element.545), channel_id=1, source_target_pairs={{0,1},{1,0},{2,3},{3,2},{4,5},{5,4},{6,7},{7,6},{8,9},{9,8},{10,11... | collective-permute-start | bytes 2752520 | tf_op jit(solution)/shard_map/ppermute | solution.py:694
  177.0 7.1 %collective-permute-start.23 = (bf16[2,136,256]{2,1,0:T(8,128)(2,1)}, bf16[2,136,256]{2,1,0:T(8,128)(2,1)S(1)}, u32[]{:S(2)}, u32[]{:S(2)}) collective-permute-start(bf16[2,136,256]{2,1,0:T(8,128)(2,1)} %get-tuple-element.622), channel_id=1, source_target_pairs={{0,8},{2,10},{4,12},{6,14},{8,0},{10,2},{12,4},{14,6},{16,24},{18,... | collective-permute-start | bytes 417800 | tf_op jit(solution)/shard_map/ppermute | solution.py:805
  177.5 11.5 %collective-permute-start.24 = (bf16[2,136,256]{2,1,0:T(8,128)(2,1)}, bf16[2,136,256]{2,1,0:T(8,128)(2,1)S(1)}, u32[]{:S(2)}, u32[]{:S(2)}) collective-permute-start(bf16[2,136,256]{2,1,0:T(8,128)(2,1)} %get-tuple-element.624), channel_id=1, source_target_pairs={{0,16},{2,18},{4,20},{6,22},{8,24},{10,26},{12,28},{14,30},{16,0},... | collective-permute-start | bytes 417800 | tf_op jit(solution)/shard_map/ppermute | solution.py:805
  180.0 11.4 %collective-permute-start.25 = (bf16[2,136,256]{2,1,0:T(8,128)(2,1)}, bf16[2,136,256]{2,1,0:T(8,128)(2,1)}, u32[]{:S(2)}, u32[]{:S(2)}) collective-permute-start(bf16[2,136,256]{2,1,0:T(8,128)(2,1)} %get-tuple-element.623), channel_id=1, source_target_pairs={{0,24},{2,26},{4,28},{6,30},{8,16},{10,18},{12,20},{14,22},{16,8},... | collective-permute-start | bytes 417800 | tf_op jit(solution)/shard_map/ppermute | solution.py:805
  195.0 4.4 %collective-permute-start.27 = (bf16[136,256]{1,0:T(8,128)(2,1)S(1)}, bf16[136,256]{1,0:T(8,128)(2,1)S(1)}, u32[]{:S(2)}, u32[]{:S(2)}) collective-permute-start(bf16[136,256]{1,0:T(8,128)(2,1)S(1)} %fusion.1), channel_id=1, source_target_pairs={{0,1},{1,0},{2,3},{3,2},{4,5},{5,4},{6,7},{7,6},{8,9},{9,8},{10,11... | collective-permute-start | bytes 208904 | tf_op jit(solution)/shard_map/ppermute | solution.py:694
  199.4 51.6 %collective-permute-start.32 = (bf16[8,576,256]{2,1,0:T(8,128)(2,1)}, bf16[8,576,256]{2,1,0:T(8,128)(2,1)}, u32[]{:S(2)}, u32[]{:S(2)}) collective-permute-start(bf16[8,576,256]{2,1,0:T(8,128)(2,1)} %get-tuple-element.564), channel_id=1, source_target_pairs={{0,1},{1,0},{2,3},{3,2},{4,5},{5,4},{6,7},{7,6},{8,9},{9,8},{10,11... | collective-permute-start | bytes 7077896 | tf_op jit(solution)/shard_map/ppermute | solution.py:694
  201.0 4.3 %collective-permute-start.28 = (bf16[136,256]{1,0:T(8,128)(2,1)S(1)}, bf16[136,256]{1,0:T(8,128)(2,1)S(1)}, u32[]{:S(2)}, u32[]{:S(2)}) collective-permute-start(bf16[136,256]{1,0:T(8,128)(2,1)S(1)} %fusion.refs_0_), channel_id=1, source_target_pairs={{0,8},{2,10},{4,12},{6,14},{8,0},{10,2},{12,4},{14,6},{16,24},{18,... | collective-permute-start | bytes 208904 | tf_op jit(solution)/shard_map/ppermute | solution.py:805
  207.5 6.9 %collective-permute-start.29 = (bf16[272,256]{1,0:T(8,128)(2,1)}, bf16[272,256]{1,0:T(8,128)(2,1)S(1)}, u32[]{:S(2)}, u32[]{:S(2)}) collective-permute-start(bf16[272,256]{1,0:T(8,128)(2,1)} %join.3.refs_0_), channel_id=1, source_target_pairs={{0,16},{2,18},{4,20},{6,22},{8,24},{10,26},{12,28},{14,30},{16,0},... | collective-permute-start | bytes 417800 | tf_op jit(solution)/shard_map/ppermute | solution.py:805
  216.8 6.8 %collective-permute-start.33 = (bf16[544,256]{1,0:T(8,128)(2,1)}, bf16[544,256]{1,0:T(8,128)(2,1)S(1)}, u32[]{:S(2)}, u32[]{:S(2)}) collective-permute-start(bf16[544,256]{1,0:T(8,128)(2,1)} %join.4.refs_0_), channel_id=1, source_target_pairs={{0,4},{2,6},{4,0},{6,2},{8,12},{10,14},{12,8},{14,10},{16,20},{18,... | collective-permute-start | bytes 835592 | tf_op jit(solution)/shard_map/ppermute | solution.py:805
  226.2 12.1 %collective-permute-start.34 = (bf16[1088,256]{1,0:T(8,128)(2,1)}, bf16[1088,256]{1,0:T(8,128)(2,1)S(1)}, u32[]{:S(2)}, u32[]{:S(2)}) collective-permute-start(bf16[1088,256]{1,0:T(8,128)(2,1)} %join.5.mine), channel_id=1, source_target_pairs={{0,2},{2,0},{4,6},{6,4},{8,10},{10,8},{12,14},{14,12},{16,18},{18,... | collective-permute-start | bytes 1671176 | tf_op jit(solution)/shard_map/ppermute | solution.py:805
  229.8 27.1 %collective-permute-start.30 = (bf16[8,448,256]{2,1,0:T(8,128)(2,1)}, bf16[8,448,256]{2,1,0:T(8,128)(2,1)}, u32[]{:S(2)}, u32[]{:S(2)}) collective-permute-start(bf16[8,448,256]{2,1,0:T(8,128)(2,1)} %get-tuple-element.560), channel_id=1, source_target_pairs={{2,0},{6,2},{4,6},{12,4},{14,12},{10,14},{8,10},{16,8},{18,16},{22... | collective-permute-start | bytes 5505032 | tf_op jit(solution)/shard_map/ppermute | solution.py:699
  233.1 25.4 %collective-permute-start.31 = (bf16[8,448,256]{2,1,0:T(8,128)(2,1)}, bf16[8,448,256]{2,1,0:T(8,128)(2,1)}, u32[]{:S(2)}, u32[]{:S(2)}) collective-permute-start(bf16[8,448,256]{2,1,0:T(8,128)(2,1)} %get-tuple-element.561), channel_id=1, source_target_pairs={{0,2},{2,6},{6,4},{4,12},{12,14},{14,10},{10,8},{8,16},{16,18},{18... | collective-permute-start | bytes 5505032 | tf_op jit(solution)/shard_map/ppermute | solution.py:699
  (20 other events, 157.8 us)

commit v5 on v4

--- a/solution.py
+++ b/solution.py
@@ -106,7 +106,9 @@
 def moved_pieces(dims, plan, base, rows):
     top = 2 * dims[2] - base
     left, right = plan[IN_LEFT], plan[IN_RIGHT]
-    return (aligned(top - left - right), aligned(left)), (aligned(top - right), aligned(right))
+    at_left = jnp.where(left > 0, top - left - right, 0)
+    at_right = jnp.where(right > 0, top - right, 0)
+    return (aligned(at_left), aligned(left)), (aligned(at_right), aligned(right))
 
 
 def sent_pieces(who, plan):

time: 265 us -> 265 us (level)
  transfers between devices with their start and end apart: 33 -> 33, of which waited for: 19 -> 20; matrix products, arithmetic and copies ran while one was open for 3% -> 3% of each run, Pallas kernels for 45% -> 44%
where the time goes in v5:
time: 265 us; the launch traced here: 264 us
  Pallas kernels  123 us (46%)
  waiting for transfers between devices  84 us (32%)
  starting transfers between devices  39.9 us (15%)
  local copies, waits for them, and re-layouts  7.7 us (3%)
  other arithmetic  7.18 us (3%)
    pallas_call x3, Pallas kernels, run_blocks(): pl.pallas_call(functools.partial(blocks_kernel, dims, base, rows, tile, f...  63.3 us
    ppermute x19, waiting for transfers between devices, flipped(): return lax.ppermute(value, 'dp', [(i, i ^ flip) for i in range(size)])  38.7 us
    ppermute x10, waiting for transfers between devices, swap_tensor(): return lax.ppermute(value, 'tensor', [(0, 1), (1, 0)])  31.6 us
    pallas_call x5, Pallas kernels, unpack(): pl.pallas_call(functools.partial(unpack_kernel, dims, base, rows, streams...  17.4 us
    ppermute x19, starting transfers between devices, flipped(): return lax.ppermute(value, 'dp', [(i, i ^ flip) for i in range(size)])  16.1 us
    pallas_call x3, Pallas kernels, pack(): pl.pallas_call(functools.partial(pack_kernel, dims, base, rows, len(neigh...  14.1 us
    ppermute x4, waiting for transfers between devices, shift(): lax.ppermute(value, 'dp', pairs if step == 1 else [(b, a) for a, b in pai...  13.7 us
    ppermute x10, starting transfers between devices, swap_tensor(): return lax.ppermute(value, 'tensor', [(0, 1), (1, 0)])  12.5 us
  transfers between devices with their start and end apart: 33, of which 20 were waited for; matrix products, arithmetic and copies ran while one was open for 3% of the time, Pallas kernels for 44%

profile of v5, /device:TPU:10, one launch (start us, length us, event | category | flops | bytes accessed | tf_op | source)
XLA Modules:
  0.0 263.9 jit_solution(14464430734396149645)
XLA Ops:
  6.2 5.7 %pack.8 = (bf16[8,576,256]{2,1,0:T(8,128)(2,1)}, bf16[8,576,256]{2,1,0:T(8,128)(2,1)}) custom-call(s32[8]{0:T(128)S(1)} %get-tuple-element.771.who, s32[16]{0:T(128)} %counts.20, bf16[4096,256]{1,0:T(8,128)(2,1)} %refs_1_.5, bf16[3,4096,256]{2,1,0:T(8,128)(2,1)} %refs_2_.5, bf16[4096,256]{1,0:T(8,128)(2,1)} %refs_3_.5, bf16[3,4096,256]{2,1,0:T(8,128)(2,1)} %refs_4_.1), custom_call_target="tpu_custom_call" | custom-call | bytes 1024 | tf_op jit(solution)/shard_map/pack/pallas_call | solution.py:275
  19.4 3.1 %collective-permute-done.7 = s32[16]{0:T(128)S(1)} collective-permute-done((s32[16]{0:T(128)S(1)}, s32[16]{0:T(128)S(1)}, u32[]{:S(2)}, u32[]{:S(2)}) %collective-permute-start.7) | collective-permute-done | bytes 96 | tf_op jit(solution)/shard_map/ppermute | solution.py:807
  22.5 2.6 collective-permute-start.8
  28.5 3.9 %pack.9 = (bf16[8,240,256]{2,1,0:T(8,128)(2,1)}, bf16[8,240,256]{2,1,0:T(8,128)(2,1)}) custom-call(s32[8]{0:T(128)S(1)} %get-tuple-element.771.who, s32[16]{0:T(128)S(1)} %copy-done.14, bf16[4096,256]{1,0:T(8,128)(2,1)S(1)} %copy-done, bf16[3,4096,256]{2,1,0:T(8,128)(2,1)} %refs_2_.5, bf16[4096,256]{1,0:T(8,128)(2,1)} %refs_3_.5, bf16[3,4096,256]{2,1,0:T(8,128)(2,1)} %refs_4_.1), custom_call_target="tpu_custom_call" | custom-call | bytes 1024 | tf_op jit(solution)/shard_map/pack/pallas_call | solution.py:275
  34.6 4.4 %export.1 = (bf16[8,448,256]{2,1,0:T(8,128)(2,1)}, bf16[8,448,256]{2,1,0:T(8,128)(2,1)}) custom-call(s32[8]{0:T(128)S(1)} %get-tuple-element.771.who, s32[16]{0:T(128)S(1)} %copy-done.14, s32[8]{0:T(128)} %plan.1.refs_0_.rest_0_, bf16[4096,256]{1,0:T(8,128)(2,1)S(1)} %copy-done, bf16[3,4096,256]{2,1,0:T(8,128)(2,1)} %refs_2_.5, bf16[4096,256]{1,0:T(8,128)(2,1)} %refs_3_.5, ...), custom_call_target="tpu_custom_call" | custom-call | bytes 1024 | tf_op jit(solution)/shard_map/export/pallas_call | solution.py:316
  40.9 4.3 %collective-permute-start.14 = (bf16[8,448,256]{2,1,0:T(8,128)(2,1)}, bf16[8,448,256]{2,1,0:T(8,128)(2,1)}, u32[]{:S(2)}, u32[]{:S(2)}) collective-permute-start(bf16[8,448,256]{2,1,0:T(8,128)(2,1)} %get-tuple-element.467), channel_id=1, source_target_pairs={{2,0},{6,2},{4,6},{12,4},{14,12},{10,14},{8,10},{16,8},{18,16},{22... | collective-permute-start | bytes 5505032 | tf_op jit(solution)/shard_map/ppermute | solution.py:701
  45.8 4.6 %assemble.1 = (bf16[2,512,512]{2,1,0:T(8,128)(2,1)S(1)}, bf16[2,512,512]{2,1,0:T(8,128)(2,1)}, bf16[2,512,512]{2,1,0:T(8,128)(2,1)}, bf16[2,512,512]{2,1,0:T(8,128)(2,1)}, f32[2,2,512]{2,1,0:T(2,128)S(1)}) custom-call(s32[8]{0:T(128)S(1)} %get-tuple-element.771.who, bf16[2,512,256]{2,1,0:T(8,128)(2,1)} %w_in.3, bf16[2,256,512]{2,1,0:T(8,128)(2,1)} %w_out.3, ...), custom_call_target="tpu_custom_call" | custom-call | bytes 1024 | tf_op jit(solution)/shard_map/assemble/pallas_call | solution.py:794
  50.4 4.0 %blank.1 = (bf16[4096,256]{1,0:T(8,128)(2,1)}, bf16[3,4096,256]{2,1,0:T(8,128)(2,1)}, bf16[4096,256]{1,0:T(8,128)(2,1)}, bf16[3,4096,256]{2,1,0:T(8,128)(2,1)}) custom-call(s32[16]{0:T(128)S(1)} %copy-done.14), custom_call_target="tpu_custom_call" | custom-call | bytes 1024 | tf_op jit(solution)/shard_map/blank/pallas_call | solution.py:478
  54.4 10.4 %collective-permute-done.13.refs_5_ = bf16[8,448,256]{2,1,0:T(8,128)(2,1)} collective-permute-done((bf16[8,448,256]{2,1,0:T(8,128)(2,1)}, bf16[8,448,256]{2,1,0:T(8,128)(2,1)}, u32[]{:S(2)}, u32[]{:S(2)}) %collective-permute-start.13) | collective-permute-done | bytes 1835040 | tf_op jit(solution)/shard_map/ppermute | solution.py:701
  66.3 4.5 %pack.10 = (bf16[8,448,256]{2,1,0:T(8,128)(2,1)}, bf16[8,448,256]{2,1,0:T(8,128)(2,1)}) custom-call(s32[8]{0:T(128)S(1)} %get-tuple-element.771.who, s32[16]{0:T(128)S(1)} %copy-done.14, s32[8]{0:T(128)} %plan.1.refs_0_.rest_0_, bf16[4096,256]{1,0:T(8,128)(2,1)S(1)} %copy-done, bf16[3,4096,256]{2,1,0:T(8,128)(2,1)} %refs_2_.5, bf16[4096,256]{1,0:T(8,128)(2,1)} %refs_3_.5, ...), custom_call_target="tpu_custom_call" | custom-call | bytes 1024 | tf_op jit(solution)/shard_map/pack/pallas_call | solution.py:275
  70.8 15.0 %collective-permute-done.15.got = bf16[8,240,256]{2,1,0:T(8,128)(2,1)} collective-permute-done((bf16[8,240,256]{2,1,0:T(8,128)(2,1)}, bf16[8,240,256]{2,1,0:T(8,128)(2,1)}, u32[]{:S(2)}, u32[]{:S(2)}) %collective-permute-start.15) | collective-permute-done | bytes 983072 | tf_op jit(solution)/shard_map/ppermute | solution.py:696
  87.3 24.5 %blocks.8 = (bf16[4,576,256]{2,1,0:T(8,128)(2,1)}, bf16[4,576,256]{2,1,0:T(8,128)(2,1)}, bf16[8,576,256]{2,1,0:T(8,128)(2,1)}, f32[2,2176,256]{2,1,0:T(8,128)}, f32[4,8,512]{2,1,0:T(8,128)S(1)}) custom-call(s32[8]{0:T(128)S(1)} %get-tuple-element.771.who, bf16[8,576,256]{2,1,0:T(8,128)(2,1)} %get-tuple-element.507.own, ...), custom_call_target="tpu_custom_call" | custom-call | flops 40320000000 | bytes 1024 | tf_op jit(solution)/shard_map/blocks/pallas_call | solution.py:669
  112.7 16.8 %blocks.9 = (bf16[4,240,256]{2,1,0:T(8,128)(2,1)}, bf16[4,240,256]{2,1,0:T(8,128)(2,1)}, bf16[8,240,256]{2,1,0:T(8,128)(2,1)}, f32[2,2176,256]{2,1,0:T(8,128)}, f32[4,8,512]{2,1,0:T(8,128)S(1)}) custom-call(s32[8]{0:T(128)S(1)} %get-tuple-element.842, bf16[8,240,256]{2,1,0:T(8,128)(2,1)} %get-tuple-element.505.own, ...), custom_call_target="tpu_custom_call", output_to_operand_aliasing={{3}: (9, {}), {4}: (10, {})} | custom-call | bytes 1024 | tf_op jit(solution)/shard_map/blocks/pallas_call | solution.py:669
  130.1 22.0 %blocks.10 = (bf16[4,448,256]{2,1,0:T(8,128)(2,1)}, bf16[4,448,256]{2,1,0:T(8,128)(2,1)}, bf16[4,448,256]{2,1,0:T(8,128)(2,1)}, bf16[4,448,256]{2,1,0:T(8,128)(2...) custom-call(s32[8]{0:T(128)S(1)} %get-tuple-element.842, ...), custom_call_target="tpu_custom_call" | custom-call | bytes 1024 | tf_op jit(solution)/shard_map/blocks/pallas_call | solution.py:669
  160.8 3.3 %unpack.10 = (bf16[4096,256]{1,0:T(8,128)(2,1)S(1)}, bf16[3,4096,256]{2,1,0:T(8,128)(2,1)}, bf16[4096,256]{1,0:T(8,128)(2,1)}, bf16[3,4096,256]{2,1,0:T(8,128)(2,1)}) custom-call(s32[8]{0:T(128)S(1)} %get-tuple-element.842, s32[16]{0:T(128)S(1)} %get-tuple-element.852, ...), custom_call_target="tpu_custom_call", output_to_operand_aliasing={{0}: (6, {}), {1}: (7, {}), {2}: (8, {}), {3}: (9, {})} | custom-call | bytes 1024 | tf_op jit(solution)/shard_map/unpack/pallas_call | solution.py:428
  164.1 9.4 %collective-permute-done.21 = bf16[2,544,256]{2,1,0:T(8,128)(2,1)} collective-permute-done((bf16[2,544,256]{2,1,0:T(8,128)(2,1)S(1)}, bf16[2,544,256]{2,1,0:T(8,128)(2,1)}, u32[]{:S(2)}, u32[]{:S(2)}) %collective-permute-start.21) | collective-permute-done | bytes 557088 | tf_op jit(solution)/shard_map/ppermute | solution.py:807
  177.4 2.5 collective-permute-start.24
  180.4 2.2 unpack.11
  183.7 5.2 %collective-permute-done.24 = bf16[2,136,256]{2,1,0:T(8,128)(2,1)S(1)} collective-permute-done((bf16[2,136,256]{2,1,0:T(8,128)(2,1)}, bf16[2,136,256]{2,1,0:T(8,128)(2,1)S(1)}, u32[]{:S(2)}, u32[]{:S(2)}) %collective-permute-start.24) | collective-permute-done | bytes 139296 | tf_op jit(solution)/shard_map/ppermute | solution.py:807
  192.5 2.5 collective-permute-done.26.refs_3_.refs_1_
  196.6 2.8 %collective-permute-done.27 = bf16[136,256]{1,0:T(8,128)(2,1)S(1)} collective-permute-done((bf16[136,256]{1,0:T(8,128)(2,1)S(1)}, bf16[136,256]{1,0:T(8,128)(2,1)S(1)}, u32[]{:S(2)}, u32[]{:S(2)}) %collective-permute-start.27) | collective-permute-done | bytes 69664 | tf_op jit(solution)/shard_map/ppermute | solution.py:696
  201.4 3.9 %collective-permute-done.28.refs_1_ = bf16[136,256]{1,0:T(8,128)(2,1)S(1)} collective-permute-done((bf16[136,256]{1,0:T(8,128)(2,1)S(1)}, bf16[136,256]{1,0:T(8,128)(2,1)S(1)}, u32[]{:S(2)}, u32[]{:S(2)}) %collective-permute-start.28) | collective-permute-done | bytes 69664 | tf_op jit(solution)/shard_map/ppermute | solution.py:807
  207.5 2.7 %collective-permute-start.29 = (bf16[272,256]{1,0:T(8,128)(2,1)}, bf16[272,256]{1,0:T(8,128)(2,1)S(1)}, u32[]{:S(2)}, u32[]{:S(2)}) collective-permute-start(bf16[272,256]{1,0:T(8,128)(2,1)} %join.3.refs_0_), channel_id=1, source_target_pairs={{0,16},{2,18},{4,20},{6,22},{8,24},{10,26},{12,28},{14,30},{16,0},... | collective-permute-start | bytes 417800 | tf_op jit(solution)/shard_map/ppermute | solution.py:807
  210.2 4.2 %collective-permute-done.29.refs_1_ = bf16[272,256]{1,0:T(8,128)(2,1)S(1)} collective-permute-done((bf16[272,256]{1,0:T(8,128)(2,1)}, bf16[272,256]{1,0:T(8,128)(2,1)S(1)}, u32[]{:S(2)}, u32[]{:S(2)}) %collective-permute-start.29) | collective-permute-done | bytes 139296 | tf_op jit(solution)/shard_map/ppermute | solution.py:807
  217.4 6.2 %collective-permute-done.33.refs_1_ = bf16[544,256]{1,0:T(8,128)(2,1)S(1)} collective-permute-done((bf16[544,256]{1,0:T(8,128)(2,1)}, bf16[544,256]{1,0:T(8,128)(2,1)S(1)}, u32[]{:S(2)}, u32[]{:S(2)}) %collective-permute-start.33) | collective-permute-done | bytes 278560 | tf_op jit(solution)/shard_map/ppermute | solution.py:807
  226.2 4.0 %handback.1 = (bf16[8,448,256]{2,1,0:T(8,128)(2,1)}, bf16[8,448,256]{2,1,0:T(8,128)(2,1)}) custom-call(s32[8]{0:T(128)S(1)} %get-tuple-element.842, s32[8]{0:T(128)} %plan.1.refs_0_.rest_0_, bf16[4,448,256]{2,1,0:T(8,128)(2,1)} %get-tuple-element.546.refs_0_, bf16[4,448,256]{2,1,0:T(8,128)(2,1)} %get-tuple-element.558.refs_1_.refs_0_, ...), custom_call_target="tpu_custom_call" | custom-call | flops 10000000000 | bytes 1024 | tf_op jit(solution)/shard_map/handback/pallas_call | solution.py:364
  230.2 3.1 %collective-permute-start.30 = (bf16[8,448,256]{2,1,0:T(8,128)(2,1)}, bf16[8,448,256]{2,1,0:T(8,128)(2,1)}, u32[]{:S(2)}, u32[]{:S(2)}) collective-permute-start(bf16[8,448,256]{2,1,0:T(8,128)(2,1)} %get-tuple-element.560), channel_id=1, source_target_pairs={{2,0},{6,2},{4,6},{12,4},{14,12},{10,14},{8,10},{16,8},{18,16},{22... | collective-permute-start | bytes 5505032 | tf_op jit(solution)/shard_map/ppermute | solution.py:701
  235.2 2.2 unpack.12
  238.3 2.6 finish.1
  240.9 10.1 %collective-permute-done.32.refs_2_ = bf16[8,576,256]{2,1,0:T(8,128)(2,1)} collective-permute-done((bf16[8,576,256]{2,1,0:T(8,128)(2,1)}, bf16[8,576,256]{2,1,0:T(8,128)(2,1)}, u32[]{:S(2)}, u32[]{:S(2)}) %collective-permute-start.32) | collective-permute-done | bytes 2359328 | tf_op jit(solution)/shard_map/ppermute | solution.py:696
  251.0 5.9 %unpack.13 = (bf16[4096,256]{1,0:T(8,128)(2,1)S(1)}, bf16[3,4096,256]{2,1,0:T(8,128)(2,1)}, bf16[4096,256]{1,0:T(8,128)(2,1)}, bf16[3,4096,256]{2,1,0:T(8,128)(2,1)}) custom-call(s32[8]{0:T(128)S(1)} %get-tuple-element.842, s32[16]{0:T(128)S(1)} %get-tuple-element.852, ...), custom_call_target="tpu_custom_call", output_to_operand_aliasing={{0}: (6, {}), {1}: (7, {}), {2}: (8, {}), {3}: (9, {})} | custom-call | flops 20000000000 | bytes 1024 | tf_op jit(solution)/shard_map/unpack/pallas_call | solution.py:428
  258.7 3.8 %unpack.14 = (bf16[4096,256]{1,0:T(8,128)(2,1)S(1)}, bf16[3,4096,256]{2,1,0:T(8,128)(2,1)}, bf16[4096,256]{1,0:T(8,128)(2,1)}, bf16[3,4096,256]{2,1,0:T(8,128)(2,1)}) custom-call(s32[8]{0:T(128)S(1)} %get-tuple-element.842, s32[16]{0:T(128)S(1)} %get-tuple-element.852, ...), custom_call_target="tpu_custom_call", output_to_operand_aliasing={{0}: (5, {}), {1}: (6, {}), {2}: (7, {}), {3}: (8, {})} | custom-call | bytes 1024 | tf_op jit(solution)/shard_map/unpack/pallas_call | solution.py:428
  (106 shorter events, 60.5 us)
Async XLA Ops:
  2.8 9.1 %collective-permute-start.5 = (bf16[512,256]{1,0:T(8,128)(2,1)}, bf16[512,256]{1,0:T(8,128)(2,1)S(1)}, u32[]{:S(2)}, u32[]{:S(2)}) collective-permute-start(bf16[512,256]{1,0:T(8,128)(2,1)} %get-tuple-element.456), channel_id=1, source_target_pairs={{0,1},{1,0},{2,3},{3,2},{4,5},{5,4},{6,7},{7,6},{8,9},{9,8},{10,11... | collective-permute-start | bytes 786440 | tf_op jit(solution)/shard_map/ppermute | solution.py:696
  5.1 6.8 %collective-permute-start.6 = (f32[2,2,256]{2,1,0:T(2,128)S(1)}, f32[2,2,256]{2,1,0:T(2,128)S(1)}, u32[]{:S(2)}, u32[]{:S(2)}) collective-permute-start(f32[2,2,256]{2,1,0:T(2,128)S(1)} %pad_maximum_fusion), channel_id=1, source_target_pairs={{0,1},{1,0},{2,3},{3,2},{4,5},{5,4},{6,7},{7,6},{8,9},{9,8},{10,11... | collective-permute-start | bytes 12296 | tf_op jit(solution)/shard_map/ppermute | solution.py:696
  11.9 75.4 %collective-permute-start.17 = (bf16[8,576,256]{2,1,0:T(8,128)(2,1)}, bf16[8,576,256]{2,1,0:T(8,128)(2,1)}, u32[]{:S(2)}, u32[]{:S(2)}) collective-permute-start(bf16[8,576,256]{2,1,0:T(8,128)(2,1)} %get-tuple-element.508), channel_id=1, source_target_pairs={{0,1},{1,0},{2,3},{3,2},{4,5},{5,4},{6,7},{7,6},{8,9},{9,8},{10,11... | collective-permute-start | bytes 7077896 | tf_op jit(solution)/shard_map/ppermute | solution.py:696
  14.2 2.5 collective-permute-start.2
  14.3 3.6 %collective-permute-start.3 = (s32[16]{0:T(128)S(1)}, s32[16]{0:T(128)S(1)}, u32[]{:S(2)}, u32[]{:S(2)}) collective-permute-start(s32[16]{0:T(128)S(1)} %compare_select_fusion), channel_id=1, source_target_pairs={{0,4},{2,6},{4,0},{6,2},{8,12},{10,14},{12,8},{14,10},{16,20},{18,... | collective-permute-start | bytes 200 | tf_op jit(solution)/shard_map/ppermute | solution.py:807
  14.8 3.4 %collective-permute-start.4 = (s32[16]{0:T(128)S(1)}, s32[16]{0:T(128)S(1)}, u32[]{:S(2)}, u32[]{:S(2)}) collective-permute-start(s32[16]{0:T(128)S(1)} %compare_select_fusion), channel_id=1, source_target_pairs={{0,6},{2,4},{4,2},{6,0},{8,14},{10,12},{12,10},{14,8},{16,22},{18,... | collective-permute-start | bytes 200 | tf_op jit(solution)/shard_map/ppermute | solution.py:807
  16.1 18.4 %collective-permute-start.10 = (bf16[512,256]{1,0:T(8,128)(2,1)S(1)}, bf16[512,256]{1,0:T(8,128)(2,1)S(1)}, u32[]{:S(2)}, u32[]{:S(2)}) collective-permute-start(bf16[512,256]{1,0:T(8,128)(2,1)S(1)} %collective-permute-done.5.refs_0_), channel_id=1, source_target_pairs={{0,4},{2,6},{4,0},{6,2},{8,12},{10,14},{12,8},{14,10},{16,20},{18,... | collective-permute-start | bytes 786440 | tf_op jit(solution)/shard_map/ppermute | solution.py:807
  16.6 17.9 %collective-permute-start.11 = (bf16[512,256]{1,0:T(8,128)(2,1)S(1)}, bf16[512,256]{1,0:T(8,128)(2,1)S(1)}, u32[]{:S(2)}, u32[]{:S(2)}) collective-permute-start(bf16[512,256]{1,0:T(8,128)(2,1)S(1)} %collective-permute-done.5.refs_0_), channel_id=1, source_target_pairs={{0,2},{2,0},{4,6},{6,4},{8,10},{10,8},{12,14},{14,12},{16,18},{18,... | collective-permute-start | bytes 786440 | tf_op jit(solution)/shard_map/ppermute | solution.py:807
  17.9 16.7 %collective-permute-start.12 = (bf16[512,256]{1,0:T(8,128)(2,1)S(1)}, bf16[512,256]{1,0:T(8,128)(2,1)S(1)}, u32[]{:S(2)}, u32[]{:S(2)}) collective-permute-start(bf16[512,256]{1,0:T(8,128)(2,1)S(1)} %collective-permute-done.5.refs_0_), channel_id=1, source_target_pairs={{0,6},{2,4},{4,2},{6,0},{8,14},{10,12},{12,10},{14,8},{16,22},{18,... | collective-permute-start | bytes 786440 | tf_op jit(solution)/shard_map/ppermute | solution.py:807
  18.9 3.6 %collective-permute-start.7 = (s32[16]{0:T(128)S(1)}, s32[16]{0:T(128)S(1)}, u32[]{:S(2)}, u32[]{:S(2)}) collective-permute-start(s32[16]{0:T(128)S(1)} %add_add_fusion.1), channel_id=1, source_target_pairs={{0,8},{2,10},{4,12},{6,14},{8,0},{10,2},{12,4},{14,6},{16,24},{18,... | collective-permute-start | bytes 200 | tf_op jit(solution)/shard_map/ppermute | solution.py:807
  22.5 4.4 %collective-permute-start.8 = (s32[16]{0:T(128)S(1)}, s32[16]{0:T(128)S(1)}, u32[]{:S(2)}, u32[]{:S(2)}) collective-permute-start(s32[16]{0:T(128)S(1)} %add_add_fusion.1), channel_id=1, source_target_pairs={{0,16},{2,18},{4,20},{6,22},{8,24},{10,26},{12,28},{14,30},{16,0},... | collective-permute-start | bytes 200 | tf_op jit(solution)/shard_map/ppermute | solution.py:807
  27.0 5.5 %collective-permute-start.9 = (s32[16]{0:T(128)S(1)}, s32[16]{0:T(128)S(1)}, u32[]{:S(2)}, u32[]{:S(2)}) collective-permute-start(s32[16]{0:T(128)S(1)} %add_add_fusion.1), channel_id=1, source_target_pairs={{0,24},{2,26},{4,28},{6,30},{8,16},{10,18},{12,20},{14,22},{16,8},... | collective-permute-start | bytes 200 | tf_op jit(solution)/shard_map/ppermute | solution.py:807
  39.0 25.8 %collective-permute-start.13 = (bf16[8,448,256]{2,1,0:T(8,128)(2,1)}, bf16[8,448,256]{2,1,0:T(8,128)(2,1)}, u32[]{:S(2)}, u32[]{:S(2)}) collective-permute-start(bf16[8,448,256]{2,1,0:T(8,128)(2,1)} %get-tuple-element.482), channel_id=1, source_target_pairs={{0,2},{2,6},{6,4},{4,12},{12,14},{14,10},{10,8},{8,16},{16,18},{18... | collective-permute-start | bytes 5505032 | tf_op jit(solution)/shard_map/ppermute | solution.py:701
  40.9 25.4 %collective-permute-start.14 = (bf16[8,448,256]{2,1,0:T(8,128)(2,1)}, bf16[8,448,256]{2,1,0:T(8,128)(2,1)}, u32[]{:S(2)}, u32[]{:S(2)}) collective-permute-start(bf16[8,448,256]{2,1,0:T(8,128)(2,1)} %get-tuple-element.467), channel_id=1, source_target_pairs={{2,0},{6,2},{4,6},{12,4},{14,12},{10,14},{8,10},{16,8},{18,16},{22... | collective-permute-start | bytes 5505032 | tf_op jit(solution)/shard_map/ppermute | solution.py:701
  45.2 40.5 %collective-permute-start.15 = (bf16[8,240,256]{2,1,0:T(8,128)(2,1)}, bf16[8,240,256]{2,1,0:T(8,128)(2,1)}, u32[]{:S(2)}, u32[]{:S(2)}) collective-permute-start(bf16[8,240,256]{2,1,0:T(8,128)(2,1)} %get-tuple-element.497), channel_id=1, source_target_pairs={{0,1},{1,0},{2,3},{3,2},{4,5},{5,4},{6,7},{7,6},{8,9},{9,8},{10,11... | collective-permute-start | bytes 2949128 | tf_op jit(solution)/shard_map/ppermute | solution.py:696
  85.8 44.3 %collective-permute-start.16 = (bf16[8,448,256]{2,1,0:T(8,128)(2,1)}, bf16[8,448,256]{2,1,0:T(8,128)(2,1)}, u32[]{:S(2)}, u32[]{:S(2)}) collective-permute-start(bf16[8,448,256]{2,1,0:T(8,128)(2,1)} %get-tuple-element.499), channel_id=1, source_target_pairs={{0,1},{1,0},{2,3},{3,2},{4,5},{5,4},{6,7},{7,6},{8,9},{9,8},{10,11... | collective-permute-start | bytes 5505032 | tf_op jit(solution)/shard_map/ppermute | solution.py:696
  129.5 22.6 %collective-permute-start.18 = (bf16[8,240,256]{2,1,0:T(8,128)(2,1)}, bf16[8,240,256]{2,1,0:T(8,128)(2,1)}, u32[]{:S(2)}, u32[]{:S(2)}) collective-permute-start(bf16[8,240,256]{2,1,0:T(8,128)(2,1)} %get-tuple-element.528), channel_id=1, source_target_pairs={{0,1},{1,0},{2,3},{3,2},{4,5},{5,4},{6,7},{7,6},{8,9},{9,8},{10,11... | collective-permute-start | bytes 2949128 | tf_op jit(solution)/shard_map/ppermute | solution.py:696
  152.2 3.0 %collective-permute-start.20 = (bf16[1088,256]{1,0:T(8,128)(2,1)}, bf16[1088,256]{1,0:T(8,128)(2,1)S(1)}, u32[]{:S(2)}, u32[]{:S(2)}) collective-permute-start(bf16[1088,256]{1,0:T(8,128)(2,1)} %get-tuple-element.531), channel_id=1, source_target_pairs={{0,2},{2,0},{4,6},{6,4},{8,10},{10,8},{12,14},{14,12},{16,18},{18,... | collective-permute-start | bytes 1671176 | tf_op jit(solution)/shard_map/ppermute | solution.py:807
  152.7 23.5 %collective-permute-start.22 = (bf16[4,448,256]{2,1,0:T(8,128)(2,1)}, bf16[4,448,256]{2,1,0:T(8,128)(2,1)}, u32[]{:S(2)}, u32[]{:S(2)}) collective-permute-start(bf16[4,448,256]{2,1,0:T(8,128)(2,1)} %get-tuple-element.532), channel_id=1, source_target_pairs={{0,1},{1,0},{2,3},{3,2},{4,5},{5,4},{6,7},{7,6},{8,9},{9,8},{10,11... | collective-permute-start | bytes 2752520 | tf_op jit(solution)/shard_map/ppermute | solution.py:696
  158.6 14.8 %collective-permute-start.21 = (bf16[2,544,256]{2,1,0:T(8,128)(2,1)S(1)}, bf16[2,544,256]{2,1,0:T(8,128)(2,1)}, u32[]{:S(2)}, u32[]{:S(2)}) collective-permute-start(bf16[2,544,256]{2,1,0:T(8,128)(2,1)S(1)} %dynamic-slice_convert_fusion), channel_id=1, source_target_pairs={{0,4},{2,6},{4,0},{6,2},{8,12},{10,14},{12,8},{14,10},{16,20},{18,... | collective-permute-start | bytes 1671176 | tf_op jit(solution)/shard_map/ppermute | solution.py:807
  159.3 35.7 %collective-permute-start.26 = (bf16[4,448,256]{2,1,0:T(8,128)(2,1)}, bf16[4,448,256]{2,1,0:T(8,128)(2,1)}, u32[]{:S(2)}, u32[]{:S(2)}) collective-permute-start(bf16[4,448,256]{2,1,0:T(8,128)(2,1)} %get-tuple-element.545), channel_id=1, source_target_pairs={{0,1},{1,0},{2,3},{3,2},{4,5},{5,4},{6,7},{7,6},{8,9},{9,8},{10,11... | collective-permute-start | bytes 2752520 | tf_op jit(solution)/shard_map/ppermute | solution.py:696
  177.0 6.8 %collective-permute-start.23 = (bf16[2,136,256]{2,1,0:T(8,128)(2,1)}, bf16[2,136,256]{2,1,0:T(8,128)(2,1)S(1)}, u32[]{:S(2)}, u32[]{:S(2)}) collective-permute-start(bf16[2,136,256]{2,1,0:T(8,128)(2,1)} %get-tuple-element.622), channel_id=1, source_target_pairs={{0,8},{2,10},{4,12},{6,14},{8,0},{10,2},{12,4},{14,6},{16,24},{18,... | collective-permute-start | bytes 417800 | tf_op jit(solution)/shard_map/ppermute | solution.py:807
  177.4 11.5 %collective-permute-start.24 = (bf16[2,136,256]{2,1,0:T(8,128)(2,1)}, bf16[2,136,256]{2,1,0:T(8,128)(2,1)S(1)}, u32[]{:S(2)}, u32[]{:S(2)}) collective-permute-start(bf16[2,136,256]{2,1,0:T(8,128)(2,1)} %get-tuple-element.624), channel_id=1, source_target_pairs={{0,16},{2,18},{4,20},{6,22},{8,24},{10,26},{12,28},{14,30},{16,0},... | collective-permute-start | bytes 417800 | tf_op jit(solution)/shard_map/ppermute | solution.py:807
  180.0 11.4 %collective-permute-start.25 = (bf16[2,136,256]{2,1,0:T(8,128)(2,1)}, bf16[2,136,256]{2,1,0:T(8,128)(2,1)}, u32[]{:S(2)}, u32[]{:S(2)}) collective-permute-start(bf16[2,136,256]{2,1,0:T(8,128)(2,1)} %get-tuple-element.623), channel_id=1, source_target_pairs={{0,24},{2,26},{4,28},{6,30},{8,16},{10,18},{12,20},{14,22},{16,8},... | collective-permute-start | bytes 417800 | tf_op jit(solution)/shard_map/ppermute | solution.py:807
  195.0 4.4 %collective-permute-start.27 = (bf16[136,256]{1,0:T(8,128)(2,1)S(1)}, bf16[136,256]{1,0:T(8,128)(2,1)S(1)}, u32[]{:S(2)}, u32[]{:S(2)}) collective-permute-start(bf16[136,256]{1,0:T(8,128)(2,1)S(1)} %fusion.1), channel_id=1, source_target_pairs={{0,1},{1,0},{2,3},{3,2},{4,5},{5,4},{6,7},{7,6},{8,9},{9,8},{10,11... | collective-permute-start | bytes 208904 | tf_op jit(solution)/shard_map/ppermute | solution.py:696
  199.4 51.6 %collective-permute-start.32 = (bf16[8,576,256]{2,1,0:T(8,128)(2,1)}, bf16[8,576,256]{2,1,0:T(8,128)(2,1)}, u32[]{:S(2)}, u32[]{:S(2)}) collective-permute-start(bf16[8,576,256]{2,1,0:T(8,128)(2,1)} %get-tuple-element.564), channel_id=1, source_target_pairs={{0,1},{1,0},{2,3},{3,2},{4,5},{5,4},{6,7},{7,6},{8,9},{9,8},{10,11... | collective-permute-start | bytes 7077896 | tf_op jit(solution)/shard_map/ppermute | solution.py:696
  201.0 4.3 %collective-permute-start.28 = (bf16[136,256]{1,0:T(8,128)(2,1)S(1)}, bf16[136,256]{1,0:T(8,128)(2,1)S(1)}, u32[]{:S(2)}, u32[]{:S(2)}) collective-permute-start(bf16[136,256]{1,0:T(8,128)(2,1)S(1)} %fusion.refs_0_), channel_id=1, source_target_pairs={{0,8},{2,10},{4,12},{6,14},{8,0},{10,2},{12,4},{14,6},{16,24},{18,... | collective-permute-start | bytes 208904 | tf_op jit(solution)/shard_map/ppermute | solution.py:807
  207.5 6.9 %collective-permute-start.29 = (bf16[272,256]{1,0:T(8,128)(2,1)}, bf16[272,256]{1,0:T(8,128)(2,1)S(1)}, u32[]{:S(2)}, u32[]{:S(2)}) collective-permute-start(bf16[272,256]{1,0:T(8,128)(2,1)} %join.3.refs_0_), channel_id=1, source_target_pairs={{0,16},{2,18},{4,20},{6,22},{8,24},{10,26},{12,28},{14,30},{16,0},... | collective-permute-start | bytes 417800 | tf_op jit(solution)/shard_map/ppermute | solution.py:807
  216.7 6.8 %collective-permute-start.33 = (bf16[544,256]{1,0:T(8,128)(2,1)}, bf16[544,256]{1,0:T(8,128)(2,1)S(1)}, u32[]{:S(2)}, u32[]{:S(2)}) collective-permute-start(bf16[544,256]{1,0:T(8,128)(2,1)} %join.4.refs_0_), channel_id=1, source_target_pairs={{0,4},{2,6},{4,0},{6,2},{8,12},{10,14},{12,8},{14,10},{16,20},{18,... | collective-permute-start | bytes 835592 | tf_op jit(solution)/shard_map/ppermute | solution.py:807
  226.2 11.3 %collective-permute-start.34 = (bf16[1088,256]{1,0:T(8,128)(2,1)}, bf16[1088,256]{1,0:T(8,128)(2,1)S(1)}, u32[]{:S(2)}, u32[]{:S(2)}) collective-permute-start(bf16[1088,256]{1,0:T(8,128)(2,1)} %join.5.mine), channel_id=1, source_target_pairs={{0,2},{2,0},{4,6},{6,4},{8,10},{10,8},{12,14},{14,12},{16,18},{18,... | collective-permute-start | bytes 1671176 | tf_op jit(solution)/shard_map/ppermute | solution.py:807
  230.2 26.7 %collective-permute-start.30 = (bf16[8,448,256]{2,1,0:T(8,128)(2,1)}, bf16[8,448,256]{2,1,0:T(8,128)(2,1)}, u32[]{:S(2)}, u32[]{:S(2)}) collective-permute-start(bf16[8,448,256]{2,1,0:T(8,128)(2,1)} %get-tuple-element.560), channel_id=1, source_target_pairs={{2,0},{6,2},{4,6},{12,4},{14,12},{10,14},{8,10},{16,8},{18,16},{22... | collective-permute-start | bytes 5505032 | tf_op jit(solution)/shard_map/ppermute | solution.py:701
  233.3 25.4 %collective-permute-start.31 = (bf16[8,448,256]{2,1,0:T(8,128)(2,1)}, bf16[8,448,256]{2,1,0:T(8,128)(2,1)}, u32[]{:S(2)}, u32[]{:S(2)}) collective-permute-start(bf16[8,448,256]{2,1,0:T(8,128)(2,1)} %get-tuple-element.561), channel_id=1, source_target_pairs={{0,2},{2,6},{6,4},{4,12},{12,14},{14,10},{10,8},{8,16},{16,18},{18... | collective-permute-start | bytes 5505032 | tf_op jit(solution)/shard_map/ppermute | solution.py:701
  (20 other events, 159.2 us)

commit v6 on v5

--- a/solution.py
+++ b/solution.py
@@ -440,6 +440,72 @@
         compiler_params=PARAMS,
         name="unpack",
     )(who, counts, plan, *mine, theirs, *outs)
+
+
+def unpack_part_kernel(dims, base, rows, parts, own, who, counts, plan, *refs):
+    arrays, refs = refs[:parts], refs[parts:]
+    outs, (held, ends, sems) = refs[4:8], refs[8:]
+    part = who[SIDE] if own else 1 - who[SIDE]
+    loads = [
+        pltpu.make_async_copy(array, held.at[pl.ds(4 * number, array.shape[0])], sems.at[number])
+        for number, array in enumerate(arrays)
+    ]
+    for load in loads:
+        load.start()
+    for load in loads:
+        load.wait()
+    first = base + part * rows
+    size = jnp.clip(plan[KEPT] - first, 0, rows)
+
+    def start_out(origin, place, row, size, sem):
+        for number in range(2):
+            copies = copies_between(
+                origin, 4 * number, place, outs[2 * number], outs[2 * number + 1], row, size
+            )
+            for there, here in copies:
+                pltpu.make_async_copy(here, there, sem).start()
+
+    def start(row, place, size):
+        start_out(held, place, row, size, sems.at[2])
+
+    each_run(dims, who, counts, (first, first + size, size), start)
+
+    @pl.when(part == 0)
+    def _():
+        matrix = tail_matrix(dims, counts)
+        for stream in range(8):
+            packed = held[stream, : dims[0] * GROUP, :]
+            ends[stream] = dot(matrix, packed, TN).astype(BF16)
+
+        def start_tail(source, row, left):
+            @pl.when(left > 0)
+            def _():
+                start_out(ends, aligned(source * GROUP), row, GROUP, sems.at[3])
+
+        found = each_tail(dims, counts, start_tail)
+        wait_for(ends, slice(0, 8), found * GROUP, sems.at[3])
+
+    wait_for(held, slice(0, 8), size - jnp.where(part == 0, who[TAILS], 0), sems.at[2])
+
+
+def unpack_part(dims, who, counts, plan, arrays, outs, base, rows, own):
+    half = outs[0].shape[1]
+    first = 3 + len(arrays)
+    return pl.pallas_call(
+        functools.partial(unpack_part_kernel, dims, base, rows, len(arrays), own),
+        out_shape=[jax.ShapeDtypeStruct(out.shape, BF16) for out in outs],
+        in_specs=[SCALARS] * 3 + [HBM] * (len(arrays) + len(outs)),
+        out_specs=[HBM] * len(outs),
+        input_output_aliases={first + number: number for number in range(len(outs))},
+        scratch_shapes=[
+            pltpu.VMEM((8, rows, half), BF16),
+            pltpu.VMEM((8, dims[0] * GROUP, half), BF16),
+            pltpu.SemaphoreType.DMA((4,)),
+        ],
+        cost_estimate=NO_COST if own else LAST_COST,
+        compiler_params=PARAMS,
+        name="unpack_part",
+    )(who, counts, plan, *arrays, *outs)
 
 
 def blank_kernel(sources, slot, counts, values, tangents, other_values, other_tangents, zeros, sem):
@@ -1020,9 +1086,11 @@
     )
     back = (shift(to_left, order, -1), shift(to_right, order, 1))
     total = gather_step(total, across, place, dp_size)
+    outs = place_grads(outs, *last, result3[1], d3_got)
+    outs = unpack_part(dims, who, counts, plan, result1[:2], outs, 0, first, True)
+    total, outs = together(total, outs)
     total_got = flipped(total, 1, dp_size)
-    outs = place_grads(outs, *last, result3[1], d3_got)
-    outs = place_all(outs, 0, first, plan, result1, yd1_got)
+    outs = unpack_part(dims, who, counts, plan, [yd1_got], outs, 0, first, False)
     sums = finish((place & 1).astype(jnp.int32)[None], total, total_got)
     outs = unpack(dims, who, counts, plan, back[:1], back[1], outs, None, moved)
     grad_in, grad_out, bias_in_grad, bias_out_grad = sums

time: 265 us -> 267 us (level)
  Pallas kernels: 123 us -> 128 us
  waiting for transfers between devices: 84 us -> 81.3 us
    pallas_call x0 -> x2, Pallas kernels: none -> 8.42 us  [unpack_part(): pl.pallas_call(functools.partial(unpack_part_kernel, dims, base, rows, le...]
    ppermute x19, waiting for transfers between devices: 38.7 us -> 31.4 us  [flipped(): return lax.ppermute(value, 'dp', [(i, i ^ flip) for i in range(size)])]
    ppermute x4, waiting for transfers between devices: 13.7 us -> 18.4 us  [shift(): lax.ppermute(value, 'dp', pairs if step == 1 else [(b, a) for a, b in pai...]
    pallas_call x5 -> x4, Pallas kernels: 17.4 us -> 13.8 us  [unpack(): pl.pallas_call(functools.partial(unpack_kernel, dims, base, rows, streams...]
  transfers between devices with their start and end apart: 33 -> 33, of which waited for: 20 -> 19; matrix products, arithmetic and copies ran while one was open for 3% -> 3% of each run, Pallas kernels for 44% -> 46%
where the time goes in v6:
time: 267 us; the launch traced here: 266 us
  Pallas kernels  128 us (48%)
  waiting for transfers between devices  81.3 us (30%)
  starting transfers between devices  40 us (15%)
  local copies, waits for them, and re-layouts  7.66 us (3%)
  other arithmetic  7.18 us (3%)
    pallas_call x3, Pallas kernels, run_blocks(): pl.pallas_call(functools.partial(blocks_kernel, dims, base, rows, tile, f...  63.2 us
    ppermute x10, waiting for transfers between devices, swap_tensor(): return lax.ppermute(value, 'tensor', [(0, 1), (1, 0)])  31.5 us
    ppermute x19, waiting for transfers between devices, flipped(): return lax.ppermute(value, 'dp', [(i, i ^ flip) for i in range(size)])  31.4 us
    ppermute x4, waiting for transfers between devices, shift(): lax.ppermute(value, 'dp', pairs if step == 1 else [(b, a) for a, b in pai...  18.4 us
    ppermute x19, starting transfers between devices, flipped(): return lax.ppermute(value, 'dp', [(i, i ^ flip) for i in range(size)])  16 us
    pallas_call x3, Pallas kernels, pack(): pl.pallas_call(functools.partial(pack_kernel, dims, base, rows, len(neigh...  14.6 us
    pallas_call x4, Pallas kernels, unpack(): pl.pallas_call(functools.partial(unpack_kernel, dims, base, rows, streams...  13.8 us
    ppermute x10, starting transfers between devices, swap_tensor(): return lax.ppermute(value, 'tensor', [(0, 1), (1, 0)])  12.5 us
  transfers between devices with their start and end apart: 33, of which 19 were waited for; matrix products, arithmetic and copies ran while one was open for 3% of the time, Pallas kernels for 46%

profile of v6, /device:TPU:10, one launch (start us, length us, event | category | flops | bytes accessed | tf_op | source)
XLA Modules:
  0.0 265.6 jit_solution(17125725895705876888)
XLA Ops:
  6.2 5.6 %pack.8 = (bf16[8,576,256]{2,1,0:T(8,128)(2,1)}, bf16[8,576,256]{2,1,0:T(8,128)(2,1)}) custom-call(s32[8]{0:T(128)S(1)} %get-tuple-element.789.who, s32[16]{0:T(128)} %counts.22, bf16[4096,256]{1,0:T(8,128)(2,1)} %refs_1_.5, bf16[3,4096,256]{2,1,0:T(8,128)(2,1)} %refs_2_.5, bf16[4096,256]{1,0:T(8,128)(2,1)} %refs_3_.5, bf16[3,4096,256]{2,1,0:T(8,128)(2,1)} %refs_4_.1), custom_call_target="tpu_custom_call" | custom-call | bytes 1024 | tf_op jit(solution)/shard_map/pack/pallas_call | solution.py:275
  19.4 3.1 %collective-permute-done.7 = s32[16]{0:T(128)S(1)} collective-permute-done((s32[16]{0:T(128)S(1)}, s32[16]{0:T(128)S(1)}, u32[]{:S(2)}, u32[]{:S(2)}) %collective-permute-start.7) | collective-permute-done | bytes 96 | tf_op jit(solution)/shard_map/ppermute | solution.py:873
  22.5 2.6 collective-permute-start.8
  28.5 3.8 %pack.9 = (bf16[8,240,256]{2,1,0:T(8,128)(2,1)}, bf16[8,240,256]{2,1,0:T(8,128)(2,1)}) custom-call(s32[8]{0:T(128)S(1)} %get-tuple-element.789.who, s32[16]{0:T(128)S(1)} %copy-done.14, bf16[4096,256]{1,0:T(8,128)(2,1)S(1)} %copy-done, bf16[3,4096,256]{2,1,0:T(8,128)(2,1)} %refs_2_.5, bf16[4096,256]{1,0:T(8,128)(2,1)} %refs_3_.5, bf16[3,4096,256]{2,1,0:T(8,128)(2,1)} %refs_4_.1), custom_call_target="tpu_custom_call" | custom-call | bytes 1024 | tf_op jit(solution)/shard_map/pack/pallas_call | solution.py:275
  34.4 4.5 %export.1 = (bf16[8,448,256]{2,1,0:T(8,128)(2,1)}, bf16[8,448,256]{2,1,0:T(8,128)(2,1)}) custom-call(s32[8]{0:T(128)S(1)} %get-tuple-element.789.who, s32[16]{0:T(128)S(1)} %copy-done.14, s32[8]{0:T(128)} %plan.1.refs_0_.rest_0_, bf16[4096,256]{1,0:T(8,128)(2,1)S(1)} %copy-done, bf16[3,4096,256]{2,1,0:T(8,128)(2,1)} %refs_2_.5, bf16[4096,256]{1,0:T(8,128)(2,1)} %refs_3_.5, ...), custom_call_target="tpu_custom_call" | custom-call | bytes 1024 | tf_op jit(solution)/shard_map/export/pallas_call | solution.py:316
  40.9 4.4 %collective-permute-start.14 = (bf16[8,448,256]{2,1,0:T(8,128)(2,1)}, bf16[8,448,256]{2,1,0:T(8,128)(2,1)}, u32[]{:S(2)}, u32[]{:S(2)}) collective-permute-start(bf16[8,448,256]{2,1,0:T(8,128)(2,1)} %get-tuple-element.476), channel_id=1, source_target_pairs={{2,0},{6,2},{4,6},{12,4},{14,12},{10,14},{8,10},{16,8},{18,16},{22... | collective-permute-start | bytes 5505032 | tf_op jit(solution)/shard_map/ppermute | solution.py:767
  45.8 4.6 %assemble.1 = (bf16[2,512,512]{2,1,0:T(8,128)(2,1)S(1)}, bf16[2,512,512]{2,1,0:T(8,128)(2,1)}, bf16[2,512,512]{2,1,0:T(8,128)(2,1)}, bf16[2,512,512]{2,1,0:T(8,128)(2,1)}, f32[2,2,512]{2,1,0:T(2,128)S(1)}) custom-call(s32[8]{0:T(128)S(1)} %get-tuple-element.789.who, bf16[2,512,256]{2,1,0:T(8,128)(2,1)} %w_in.3, bf16[2,256,512]{2,1,0:T(8,128)(2,1)} %w_out.3, ...), custom_call_target="tpu_custom_call" | custom-call | bytes 1024 | tf_op jit(solution)/shard_map/assemble/pallas_call | solution.py:860
  50.4 3.1 %blank.1 = (bf16[4096,256]{1,0:T(8,128)(2,1)}, bf16[3,4096,256]{2,1,0:T(8,128)(2,1)}, bf16[4096,256]{1,0:T(8,128)(2,1)}, bf16[3,4096,256]{2,1,0:T(8,128)(2,1)}) custom-call(s32[16]{0:T(128)S(1)} %copy-done.14), custom_call_target="tpu_custom_call" | custom-call | bytes 1024 | tf_op jit(solution)/shard_map/blank/pallas_call | solution.py:544
  53.5 11.3 %collective-permute-done.13.refs_5_ = bf16[8,448,256]{2,1,0:T(8,128)(2,1)} collective-permute-done((bf16[8,448,256]{2,1,0:T(8,128)(2,1)}, bf16[8,448,256]{2,1,0:T(8,128)(2,1)}, u32[]{:S(2)}, u32[]{:S(2)}) %collective-permute-start.13) | collective-permute-done | bytes 1835040 | tf_op jit(solution)/shard_map/ppermute | solution.py:767
  66.3 5.2 %pack.10 = (bf16[8,448,256]{2,1,0:T(8,128)(2,1)}, bf16[8,448,256]{2,1,0:T(8,128)(2,1)}) custom-call(s32[8]{0:T(128)S(1)} %get-tuple-element.789.who, s32[16]{0:T(128)S(1)} %copy-done.14, s32[8]{0:T(128)} %plan.1.refs_0_.rest_0_, bf16[4096,256]{1,0:T(8,128)(2,1)S(1)} %copy-done, bf16[3,4096,256]{2,1,0:T(8,128)(2,1)} %refs_2_.5, bf16[4096,256]{1,0:T(8,128)(2,1)} %refs_3_.5, ...), custom_call_target="tpu_custom_call" | custom-call | bytes 1024 | tf_op jit(solution)/shard_map/pack/pallas_call | solution.py:275
  71.5 14.3 %collective-permute-done.15.got = bf16[8,240,256]{2,1,0:T(8,128)(2,1)} collective-permute-done((bf16[8,240,256]{2,1,0:T(8,128)(2,1)}, bf16[8,240,256]{2,1,0:T(8,128)(2,1)}, u32[]{:S(2)}, u32[]{:S(2)}) %collective-permute-start.15) | collective-permute-done | bytes 983072 | tf_op jit(solution)/shard_map/ppermute | solution.py:762
  87.3 24.5 %blocks.8 = (bf16[4,576,256]{2,1,0:T(8,128)(2,1)}, bf16[4,576,256]{2,1,0:T(8,128)(2,1)}, bf16[8,576,256]{2,1,0:T(8,128)(2,1)}, f32[2,2176,256]{2,1,0:T(8,128)}, f32[4,8,512]{2,1,0:T(8,128)S(1)}) custom-call(s32[8]{0:T(128)S(1)} %get-tuple-element.789.who, bf16[8,576,256]{2,1,0:T(8,128)(2,1)} %get-tuple-element.516.own, ...), custom_call_target="tpu_custom_call" | custom-call | flops 40320000000 | bytes 1024 | tf_op jit(solution)/shard_map/blocks/pallas_call | solution.py:735
  112.6 16.8 %blocks.9 = (bf16[4,240,256]{2,1,0:T(8,128)(2,1)}, bf16[4,240,256]{2,1,0:T(8,128)(2,1)}, bf16[8,240,256]{2,1,0:T(8,128)(2,1)}, f32[2,2176,256]{2,1,0:T(8,128)}, f32[4,8,512]{2,1,0:T(8,128)S(1)}) custom-call(s32[8]{0:T(128)S(1)} %get-tuple-element.860, bf16[8,240,256]{2,1,0:T(8,128)(2,1)} %get-tuple-element.514.own, ...), custom_call_target="tpu_custom_call", output_to_operand_aliasing={{3}: (9, {}), {4}: (10, {})} | custom-call | bytes 1024 | tf_op jit(solution)/shard_map/blocks/pallas_call | solution.py:735
  130.0 22.0 %blocks.10 = (bf16[4,448,256]{2,1,0:T(8,128)(2,1)}, bf16[4,448,256]{2,1,0:T(8,128)(2,1)}, bf16[4,448,256]{2,1,0:T(8,128)(2,1)}, bf16[4,448,256]{2,1,0:T(8,128)(2...) custom-call(s32[8]{0:T(128)S(1)} %get-tuple-element.860, ...), custom_call_target="tpu_custom_call" | custom-call | bytes 1024 | tf_op jit(solution)/shard_map/blocks/pallas_call | solution.py:735
  160.6 3.4 %unpack.9 = (bf16[4096,256]{1,0:T(8,128)(2,1)S(1)}, bf16[3,4096,256]{2,1,0:T(8,128)(2,1)}, bf16[4096,256]{1,0:T(8,128)(2,1)}, bf16[3,4096,256]{2,1,0:T(8,128)(2,1)}) custom-call(s32[8]{0:T(128)S(1)} %get-tuple-element.860, s32[16]{0:T(128)S(1)} %get-tuple-element.870, ...), custom_call_target="tpu_custom_call", output_to_operand_aliasing={{0}: (6, {}), {1}: (7, {}), {2}: (8, {}), {3}: (9, {})} | custom-call | bytes 1024 | tf_op jit(solution)/shard_map/unpack/pallas_call | solution.py:428
  164.0 9.3 %collective-permute-done.21 = bf16[2,544,256]{2,1,0:T(8,128)(2,1)} collective-permute-done((bf16[2,544,256]{2,1,0:T(8,128)(2,1)S(1)}, bf16[2,544,256]{2,1,0:T(8,128)(2,1)}, u32[]{:S(2)}, u32[]{:S(2)}) %collective-permute-start.21) | collective-permute-done | bytes 557088 | tf_op jit(solution)/shard_map/ppermute | solution.py:873
  177.2 2.6 collective-permute-start.24
  180.3 3.3 %unpack.10 = (bf16[4096,256]{1,0:T(8,128)(2,1)S(1)}, bf16[3,4096,256]{2,1,0:T(8,128)(2,1)}) custom-call(s32[8]{0:T(128)S(1)} %get-tuple-element.860, s32[16]{0:T(128)S(1)} %get-tuple-element.870, s32[8]{0:T(128)} %plan.1.refs_0_.rest_0_, bf16[4,448,256]{2,1,0:T(8,128)(2,1)} %get-tuple-element.555.refs_0_, ...), custom_call_target="tpu_custom_call", output_to_operand_aliasing={{0}: (5, {}), {1}: (6, {})} | custom-call | bytes 1024 | tf_op jit(solution)/shard_map/unpack/pallas_call | solution.py:428
  183.6 5.2 %collective-permute-done.24 = bf16[2,136,256]{2,1,0:T(8,128)(2,1)S(1)} collective-permute-done((bf16[2,136,256]{2,1,0:T(8,128)(2,1)}, bf16[2,136,256]{2,1,0:T(8,128)(2,1)S(1)}, u32[]{:S(2)}, u32[]{:S(2)}) %collective-permute-start.24) | collective-permute-done | bytes 139296 | tf_op jit(solution)/shard_map/ppermute | solution.py:873
  196.5 2.8 %collective-permute-done.27 = bf16[136,256]{1,0:T(8,128)(2,1)S(1)} collective-permute-done((bf16[136,256]{1,0:T(8,128)(2,1)S(1)}, bf16[136,256]{1,0:T(8,128)(2,1)S(1)}, u32[]{:S(2)}, u32[]{:S(2)}) %collective-permute-start.27) | collective-permute-done | bytes 69664 | tf_op jit(solution)/shard_map/ppermute | solution.py:762
  201.2 3.9 %collective-permute-done.28.refs_1_ = bf16[136,256]{1,0:T(8,128)(2,1)S(1)} collective-permute-done((bf16[136,256]{1,0:T(8,128)(2,1)S(1)}, bf16[136,256]{1,0:T(8,128)(2,1)S(1)}, u32[]{:S(2)}, u32[]{:S(2)}) %collective-permute-start.28) | collective-permute-done | bytes 69664 | tf_op jit(solution)/shard_map/ppermute | solution.py:873
  207.4 2.6 collective-permute-start.29
  210.0 4.2 %collective-permute-done.29.refs_1_ = bf16[272,256]{1,0:T(8,128)(2,1)S(1)} collective-permute-done((bf16[272,256]{1,0:T(8,128)(2,1)}, bf16[272,256]{1,0:T(8,128)(2,1)S(1)}, u32[]{:S(2)}, u32[]{:S(2)}) %collective-permute-start.29) | collective-permute-done | bytes 139296 | tf_op jit(solution)/shard_map/ppermute | solution.py:873
  217.2 3.1 %unpack.11 = (bf16[4096,256]{1,0:T(8,128)(2,1)}, bf16[3,4096,256]{2,1,0:T(8,128)(2,1)}) custom-call(s32[8]{0:T(128)S(1)} %get-tuple-element.860, s32[16]{0:T(128)S(1)} %get-tuple-element.870, s32[8]{0:T(128)} %plan.1.refs_0_.rest_0_, bf16[4,448,256]{2,1,0:T(8,128)(2,1)} %get-tuple-element.567.refs_1_.refs_0_, ...), custom_call_target="tpu_custom_call", output_to_operand_aliasing={{0}: (5, {}), {1}: (6, {})} | custom-call | bytes 1024 | tf_op jit(solution)/shard_map/unpack/pallas_call | solution.py:428
  220.4 4.7 %unpack_part.2 = (bf16[4096,256]{1,0:T(8,128)(2,1)S(1)}, bf16[3,4096,256]{2,1,0:T(8,128)(2,1)}, bf16[4096,256]{1,0:T(8,128)(2,1)}, bf16[3,4096,256]{2,1,0:T(8,128)(2,1)}) custom-call(s32[8]{0:T(128)S(1)} %get-tuple-element.860, s32[16]{0:T(128)S(1)} %get-tuple-element.870, ...), custom_call_target="tpu_custom_call", output_to_operand_aliasing={{0}: (5, {}), {1}: (6, {}), {2}: (7, {}), {3}: (8, {})} | custom-call | bytes 1024 | tf_op jit(solution)/shard_map/unpack_part/pallas_call | solution.py:494
  227.7 4.0 %handback.1 = (bf16[8,448,256]{2,1,0:T(8,128)(2,1)}, bf16[8,448,256]{2,1,0:T(8,128)(2,1)}) custom-call(s32[8]{0:T(128)S(1)} %get-tuple-element.860, s32[8]{0:T(128)} %plan.1.refs_0_.rest_0_, bf16[4,448,256]{2,1,0:T(8,128)(2,1)} %get-tuple-element.555.refs_0_, bf16[4,448,256]{2,1,0:T(8,128)(2,1)} %get-tuple-element.567.refs_1_.refs_0_, ...), custom_call_target="tpu_custom_call" | custom-call | flops 10000000000 | bytes 1024 | tf_op jit(solution)/shard_map/handback/pallas_call | solution.py:364
  231.7 3.2 %collective-permute-start.30 = (bf16[8,448,256]{2,1,0:T(8,128)(2,1)}, bf16[8,448,256]{2,1,0:T(8,128)(2,1)}, u32[]{:S(2)}, u32[]{:S(2)}) collective-permute-start(bf16[8,448,256]{2,1,0:T(8,128)(2,1)} %get-tuple-element.569), channel_id=1, source_target_pairs={{2,0},{6,2},{4,6},{12,4},{14,12},{10,14},{8,10},{16,8},{18,16},{22... | collective-permute-start | bytes 5505032 | tf_op jit(solution)/shard_map/ppermute | solution.py:767
  237.6 2.6 finish.1
  240.3 10.6 %collective-permute-done.32.refs_0_ = bf16[8,576,256]{2,1,0:T(8,128)(2,1)} collective-permute-done((bf16[8,576,256]{2,1,0:T(8,128)(2,1)}, bf16[8,576,256]{2,1,0:T(8,128)(2,1)}, u32[]{:S(2)}, u32[]{:S(2)}) %collective-permute-start.32) | collective-permute-done | bytes 2359328 | tf_op jit(solution)/shard_map/ppermute | solution.py:762
  250.9 3.8 %unpack_part.3 = (bf16[4096,256]{1,0:T(8,128)(2,1)S(1)}, bf16[3,4096,256]{2,1,0:T(8,128)(2,1)}, bf16[4096,256]{1,0:T(8,128)(2,1)}, bf16[3,4096,256]{2,1,0:T(8,128)(2,1)}) custom-call(s32[8]{0:T(128)S(1)} %get-tuple-element.860, s32[16]{0:T(128)S(1)} %get-tuple-element.870, ...), custom_call_target="tpu_custom_call", output_to_operand_aliasing={{0}: (4, {}), {1}: (5, {}), {2}: (6, {}), {3}: (7, {})} | custom-call | flops 20000000000 | bytes 1024 | tf_op jit(solution)/shard_map/unpack_part/pallas_call | solution.py:494
  255.9 4.4 %collective-permute-done.31.refs_1_ = bf16[8,448,256]{2,1,0:T(8,128)(2,1)} collective-permute-done((bf16[8,448,256]{2,1,0:T(8,128)(2,1)}, bf16[8,448,256]{2,1,0:T(8,128)(2,1)}, u32[]{:S(2)}, u32[]{:S(2)}) %collective-permute-start.31) | collective-permute-done | bytes 1835040 | tf_op jit(solution)/shard_map/ppermute | solution.py:767
  260.3 4.0 %unpack.12 = (bf16[4096,256]{1,0:T(8,128)(2,1)S(1)}, bf16[3,4096,256]{2,1,0:T(8,128)(2,1)}, bf16[4096,256]{1,0:T(8,128)(2,1)}, bf16[3,4096,256]{2,1,0:T(8,128)(2,1)}) custom-call(s32[8]{0:T(128)S(1)} %get-tuple-element.860, s32[16]{0:T(128)S(1)} %get-tuple-element.870, ...), custom_call_target="tpu_custom_call", output_to_operand_aliasing={{0}: (5, {}), {1}: (6, {}), {2}: (7, {}), {3}: (8, {})} | custom-call | bytes 1024 | tf_op jit(solution)/shard_map/unpack/pallas_call | solution.py:428
  (107 shorter events, 61.0 us)
Async XLA Ops:
  2.8 9.1 %collective-permute-start.5 = (bf16[512,256]{1,0:T(8,128)(2,1)}, bf16[512,256]{1,0:T(8,128)(2,1)S(1)}, u32[]{:S(2)}, u32[]{:S(2)}) collective-permute-start(bf16[512,256]{1,0:T(8,128)(2,1)} %get-tuple-element.465), channel_id=1, source_target_pairs={{0,1},{1,0},{2,3},{3,2},{4,5},{5,4},{6,7},{7,6},{8,9},{9,8},{10,11... | collective-permute-start | bytes 786440 | tf_op jit(solution)/shard_map/ppermute | solution.py:762
  5.1 6.7 %collective-permute-start.6 = (f32[2,2,256]{2,1,0:T(2,128)S(1)}, f32[2,2,256]{2,1,0:T(2,128)S(1)}, u32[]{:S(2)}, u32[]{:S(2)}) collective-permute-start(f32[2,2,256]{2,1,0:T(2,128)S(1)} %pad_maximum_fusion), channel_id=1, source_target_pairs={{0,1},{1,0},{2,3},{3,2},{4,5},{5,4},{6,7},{7,6},{8,9},{9,8},{10,11... | collective-permute-start | bytes 12296 | tf_op jit(solution)/shard_map/ppermute | solution.py:762
  11.9 75.4 %collective-permute-start.17 = (bf16[8,576,256]{2,1,0:T(8,128)(2,1)}, bf16[8,576,256]{2,1,0:T(8,128)(2,1)}, u32[]{:S(2)}, u32[]{:S(2)}) collective-permute-start(bf16[8,576,256]{2,1,0:T(8,128)(2,1)} %get-tuple-element.517), channel_id=1, source_target_pairs={{0,1},{1,0},{2,3},{3,2},{4,5},{5,4},{6,7},{7,6},{8,9},{9,8},{10,11... | collective-permute-start | bytes 7077896 | tf_op jit(solution)/shard_map/ppermute | solution.py:762
  14.1 2.5 collective-permute-start.2
  14.2 3.6 %collective-permute-start.3 = (s32[16]{0:T(128)S(1)}, s32[16]{0:T(128)S(1)}, u32[]{:S(2)}, u32[]{:S(2)}) collective-permute-start(s32[16]{0:T(128)S(1)} %compare_select_fusion), channel_id=1, source_target_pairs={{0,4},{2,6},{4,0},{6,2},{8,12},{10,14},{12,8},{14,10},{16,20},{18,... | collective-permute-start | bytes 200 | tf_op jit(solution)/shard_map/ppermute | solution.py:873
  14.8 3.4 %collective-permute-start.4 = (s32[16]{0:T(128)S(1)}, s32[16]{0:T(128)S(1)}, u32[]{:S(2)}, u32[]{:S(2)}) collective-permute-start(s32[16]{0:T(128)S(1)} %compare_select_fusion), channel_id=1, source_target_pairs={{0,6},{2,4},{4,2},{6,0},{8,14},{10,12},{12,10},{14,8},{16,22},{18,... | collective-permute-start | bytes 200 | tf_op jit(solution)/shard_map/ppermute | solution.py:873
  16.1 18.3 %collective-permute-start.10 = (bf16[512,256]{1,0:T(8,128)(2,1)S(1)}, bf16[512,256]{1,0:T(8,128)(2,1)S(1)}, u32[]{:S(2)}, u32[]{:S(2)}) collective-permute-start(bf16[512,256]{1,0:T(8,128)(2,1)S(1)} %collective-permute-done.5.refs_0_), channel_id=1, source_target_pairs={{0,4},{2,6},{4,0},{6,2},{8,12},{10,14},{12,8},{14,10},{16,20},{18,... | collective-permute-start | bytes 786440 | tf_op jit(solution)/shard_map/ppermute | solution.py:873
  16.6 17.8 %collective-permute-start.11 = (bf16[512,256]{1,0:T(8,128)(2,1)S(1)}, bf16[512,256]{1,0:T(8,128)(2,1)S(1)}, u32[]{:S(2)}, u32[]{:S(2)}) collective-permute-start(bf16[512,256]{1,0:T(8,128)(2,1)S(1)} %collective-permute-done.5.refs_0_), channel_id=1, source_target_pairs={{0,2},{2,0},{4,6},{6,4},{8,10},{10,8},{12,14},{14,12},{16,18},{18,... | collective-permute-start | bytes 786440 | tf_op jit(solution)/shard_map/ppermute | solution.py:873
  17.8 16.6 %collective-permute-start.12 = (bf16[512,256]{1,0:T(8,128)(2,1)S(1)}, bf16[512,256]{1,0:T(8,128)(2,1)S(1)}, u32[]{:S(2)}, u32[]{:S(2)}) collective-permute-start(bf16[512,256]{1,0:T(8,128)(2,1)S(1)} %collective-permute-done.5.refs_0_), channel_id=1, source_target_pairs={{0,6},{2,4},{4,2},{6,0},{8,14},{10,12},{12,10},{14,8},{16,22},{18,... | collective-permute-start | bytes 786440 | tf_op jit(solution)/shard_map/ppermute | solution.py:873
  18.9 3.6 %collective-permute-start.7 = (s32[16]{0:T(128)S(1)}, s32[16]{0:T(128)S(1)}, u32[]{:S(2)}, u32[]{:S(2)}) collective-permute-start(s32[16]{0:T(128)S(1)} %add_add_fusion.1), channel_id=1, source_target_pairs={{0,8},{2,10},{4,12},{6,14},{8,0},{10,2},{12,4},{14,6},{16,24},{18,... | collective-permute-start | bytes 200 | tf_op jit(solution)/shard_map/ppermute | solution.py:873
  22.5 4.4 %collective-permute-start.8 = (s32[16]{0:T(128)S(1)}, s32[16]{0:T(128)S(1)}, u32[]{:S(2)}, u32[]{:S(2)}) collective-permute-start(s32[16]{0:T(128)S(1)} %add_add_fusion.1), channel_id=1, source_target_pairs={{0,16},{2,18},{4,20},{6,22},{8,24},{10,26},{12,28},{14,30},{16,0},... | collective-permute-start | bytes 200 | tf_op jit(solution)/shard_map/ppermute | solution.py:873
  26.9 5.4 %collective-permute-start.9 = (s32[16]{0:T(128)S(1)}, s32[16]{0:T(128)S(1)}, u32[]{:S(2)}, u32[]{:S(2)}) collective-permute-start(s32[16]{0:T(128)S(1)} %add_add_fusion.1), channel_id=1, source_target_pairs={{0,24},{2,26},{4,28},{6,30},{8,16},{10,18},{12,20},{14,22},{16,8},... | collective-permute-start | bytes 200 | tf_op jit(solution)/shard_map/ppermute | solution.py:873
  38.9 25.9 %collective-permute-start.13 = (bf16[8,448,256]{2,1,0:T(8,128)(2,1)}, bf16[8,448,256]{2,1,0:T(8,128)(2,1)}, u32[]{:S(2)}, u32[]{:S(2)}) collective-permute-start(bf16[8,448,256]{2,1,0:T(8,128)(2,1)} %get-tuple-element.491), channel_id=1, source_target_pairs={{0,2},{2,6},{6,4},{4,12},{12,14},{14,10},{10,8},{8,16},{16,18},{18... | collective-permute-start | bytes 5505032 | tf_op jit(solution)/shard_map/ppermute | solution.py:767
  40.9 25.4 %collective-permute-start.14 = (bf16[8,448,256]{2,1,0:T(8,128)(2,1)}, bf16[8,448,256]{2,1,0:T(8,128)(2,1)}, u32[]{:S(2)}, u32[]{:S(2)}) collective-permute-start(bf16[8,448,256]{2,1,0:T(8,128)(2,1)} %get-tuple-element.476), channel_id=1, source_target_pairs={{2,0},{6,2},{4,6},{12,4},{14,12},{10,14},{8,10},{16,8},{18,16},{22... | collective-permute-start | bytes 5505032 | tf_op jit(solution)/shard_map/ppermute | solution.py:767
  45.3 40.5 %collective-permute-start.15 = (bf16[8,240,256]{2,1,0:T(8,128)(2,1)}, bf16[8,240,256]{2,1,0:T(8,128)(2,1)}, u32[]{:S(2)}, u32[]{:S(2)}) collective-permute-start(bf16[8,240,256]{2,1,0:T(8,128)(2,1)} %get-tuple-element.506), channel_id=1, source_target_pairs={{0,1},{1,0},{2,3},{3,2},{4,5},{5,4},{6,7},{7,6},{8,9},{9,8},{10,11... | collective-permute-start | bytes 2949128 | tf_op jit(solution)/shard_map/ppermute | solution.py:762
  85.8 44.2 %collective-permute-start.16 = (bf16[8,448,256]{2,1,0:T(8,128)(2,1)}, bf16[8,448,256]{2,1,0:T(8,128)(2,1)}, u32[]{:S(2)}, u32[]{:S(2)}) collective-permute-start(bf16[8,448,256]{2,1,0:T(8,128)(2,1)} %get-tuple-element.508), channel_id=1, source_target_pairs={{0,1},{1,0},{2,3},{3,2},{4,5},{5,4},{6,7},{7,6},{8,9},{9,8},{10,11... | collective-permute-start | bytes 5505032 | tf_op jit(solution)/shard_map/ppermute | solution.py:762
  129.4 22.6 %collective-permute-start.18 = (bf16[8,240,256]{2,1,0:T(8,128)(2,1)}, bf16[8,240,256]{2,1,0:T(8,128)(2,1)}, u32[]{:S(2)}, u32[]{:S(2)}) collective-permute-start(bf16[8,240,256]{2,1,0:T(8,128)(2,1)} %get-tuple-element.537), channel_id=1, source_target_pairs={{0,1},{1,0},{2,3},{3,2},{4,5},{5,4},{6,7},{7,6},{8,9},{9,8},{10,11... | collective-permute-start | bytes 2949128 | tf_op jit(solution)/shard_map/ppermute | solution.py:762
  152.1 3.0 %collective-permute-start.20 = (bf16[1088,256]{1,0:T(8,128)(2,1)}, bf16[1088,256]{1,0:T(8,128)(2,1)S(1)}, u32[]{:S(2)}, u32[]{:S(2)}) collective-permute-start(bf16[1088,256]{1,0:T(8,128)(2,1)} %get-tuple-element.540), channel_id=1, source_target_pairs={{0,2},{2,0},{4,6},{6,4},{8,10},{10,8},{12,14},{14,12},{16,18},{18,... | collective-permute-start | bytes 1671176 | tf_op jit(solution)/shard_map/ppermute | solution.py:873
  152.5 23.5 %collective-permute-start.22 = (bf16[4,448,256]{2,1,0:T(8,128)(2,1)}, bf16[4,448,256]{2,1,0:T(8,128)(2,1)}, u32[]{:S(2)}, u32[]{:S(2)}) collective-permute-start(bf16[4,448,256]{2,1,0:T(8,128)(2,1)} %get-tuple-element.541), channel_id=1, source_target_pairs={{0,1},{1,0},{2,3},{3,2},{4,5},{5,4},{6,7},{7,6},{8,9},{9,8},{10,11... | collective-permute-start | bytes 2752520 | tf_op jit(solution)/shard_map/ppermute | solution.py:762
  158.5 14.8 %collective-permute-start.21 = (bf16[2,544,256]{2,1,0:T(8,128)(2,1)S(1)}, bf16[2,544,256]{2,1,0:T(8,128)(2,1)}, u32[]{:S(2)}, u32[]{:S(2)}) collective-permute-start(bf16[2,544,256]{2,1,0:T(8,128)(2,1)S(1)} %dynamic-slice_convert_fusion), channel_id=1, source_target_pairs={{0,4},{2,6},{4,0},{6,2},{8,12},{10,14},{12,8},{14,10},{16,20},{18,... | collective-permute-start | bytes 1671176 | tf_op jit(solution)/shard_map/ppermute | solution.py:873
  159.1 35.8 %collective-permute-start.26 = (bf16[4,448,256]{2,1,0:T(8,128)(2,1)}, bf16[4,448,256]{2,1,0:T(8,128)(2,1)}, u32[]{:S(2)}, u32[]{:S(2)}) collective-permute-start(bf16[4,448,256]{2,1,0:T(8,128)(2,1)} %get-tuple-element.554), channel_id=1, source_target_pairs={{0,1},{1,0},{2,3},{3,2},{4,5},{5,4},{6,7},{7,6},{8,9},{9,8},{10,11... | collective-permute-start | bytes 2752520 | tf_op jit(solution)/shard_map/ppermute | solution.py:762
  176.8 6.8 %collective-permute-start.23 = (bf16[2,136,256]{2,1,0:T(8,128)(2,1)}, bf16[2,136,256]{2,1,0:T(8,128)(2,1)S(1)}, u32[]{:S(2)}, u32[]{:S(2)}) collective-permute-start(bf16[2,136,256]{2,1,0:T(8,128)(2,1)} %get-tuple-element.640), channel_id=1, source_target_pairs={{0,8},{2,10},{4,12},{6,14},{8,0},{10,2},{12,4},{14,6},{16,24},{18,... | collective-permute-start | bytes 417800 | tf_op jit(solution)/shard_map/ppermute | solution.py:873
  177.2 11.6 %collective-permute-start.24 = (bf16[2,136,256]{2,1,0:T(8,128)(2,1)}, bf16[2,136,256]{2,1,0:T(8,128)(2,1)S(1)}, u32[]{:S(2)}, u32[]{:S(2)}) collective-permute-start(bf16[2,136,256]{2,1,0:T(8,128)(2,1)} %get-tuple-element.642), channel_id=1, source_target_pairs={{0,16},{2,18},{4,20},{6,22},{8,24},{10,26},{12,28},{14,30},{16,0},... | collective-permute-start | bytes 417800 | tf_op jit(solution)/shard_map/ppermute | solution.py:873
  179.8 11.4 %collective-permute-start.25 = (bf16[2,136,256]{2,1,0:T(8,128)(2,1)}, bf16[2,136,256]{2,1,0:T(8,128)(2,1)}, u32[]{:S(2)}, u32[]{:S(2)}) collective-permute-start(bf16[2,136,256]{2,1,0:T(8,128)(2,1)} %get-tuple-element.641), channel_id=1, source_target_pairs={{0,24},{2,26},{4,28},{6,30},{8,16},{10,18},{12,20},{14,22},{16,8},... | collective-permute-start | bytes 417800 | tf_op jit(solution)/shard_map/ppermute | solution.py:873
  194.9 4.4 %collective-permute-start.27 = (bf16[136,256]{1,0:T(8,128)(2,1)S(1)}, bf16[136,256]{1,0:T(8,128)(2,1)S(1)}, u32[]{:S(2)}, u32[]{:S(2)}) collective-permute-start(bf16[136,256]{1,0:T(8,128)(2,1)S(1)} %fusion.1), channel_id=1, source_target_pairs={{0,1},{1,0},{2,3},{3,2},{4,5},{5,4},{6,7},{7,6},{8,9},{9,8},{10,11... | collective-permute-start | bytes 208904 | tf_op jit(solution)/shard_map/ppermute | solution.py:762
  199.3 51.6 %collective-permute-start.32 = (bf16[8,576,256]{2,1,0:T(8,128)(2,1)}, bf16[8,576,256]{2,1,0:T(8,128)(2,1)}, u32[]{:S(2)}, u32[]{:S(2)}) collective-permute-start(bf16[8,576,256]{2,1,0:T(8,128)(2,1)} %get-tuple-element.571), channel_id=1, source_target_pairs={{0,1},{1,0},{2,3},{3,2},{4,5},{5,4},{6,7},{7,6},{8,9},{9,8},{10,11... | collective-permute-start | bytes 7077896 | tf_op jit(solution)/shard_map/ppermute | solution.py:762
  200.9 4.3 %collective-permute-start.28 = (bf16[136,256]{1,0:T(8,128)(2,1)S(1)}, bf16[136,256]{1,0:T(8,128)(2,1)S(1)}, u32[]{:S(2)}, u32[]{:S(2)}) collective-permute-start(bf16[136,256]{1,0:T(8,128)(2,1)S(1)} %fusion.refs_0_), channel_id=1, source_target_pairs={{0,8},{2,10},{4,12},{6,14},{8,0},{10,2},{12,4},{14,6},{16,24},{18,... | collective-permute-start | bytes 208904 | tf_op jit(solution)/shard_map/ppermute | solution.py:873
  207.4 6.9 %collective-permute-start.29 = (bf16[272,256]{1,0:T(8,128)(2,1)}, bf16[272,256]{1,0:T(8,128)(2,1)S(1)}, u32[]{:S(2)}, u32[]{:S(2)}) collective-permute-start(bf16[272,256]{1,0:T(8,128)(2,1)} %join.3.refs_0_), channel_id=1, source_target_pairs={{0,16},{2,18},{4,20},{6,22},{8,24},{10,26},{12,28},{14,30},{16,0},... | collective-permute-start | bytes 417800 | tf_op jit(solution)/shard_map/ppermute | solution.py:873
  216.6 8.4 %collective-permute-start.33 = (bf16[544,256]{1,0:T(8,128)(2,1)}, bf16[544,256]{1,0:T(8,128)(2,1)S(1)}, u32[]{:S(2)}, u32[]{:S(2)}) collective-permute-start(bf16[544,256]{1,0:T(8,128)(2,1)} %join.4.refs_0_), channel_id=1, source_target_pairs={{0,4},{2,6},{4,0},{6,2},{8,12},{10,14},{12,8},{14,10},{16,20},{18,... | collective-permute-start | bytes 835592 | tf_op jit(solution)/shard_map/ppermute | solution.py:873
  227.6 9.1 %collective-permute-start.34 = (bf16[1088,256]{1,0:T(8,128)(2,1)}, bf16[1088,256]{1,0:T(8,128)(2,1)S(1)}, u32[]{:S(2)}, u32[]{:S(2)}) collective-permute-start(bf16[1088,256]{1,0:T(8,128)(2,1)} %join.5.mine), channel_id=1, source_target_pairs={{0,2},{2,0},{4,6},{6,4},{8,10},{10,8},{12,14},{14,12},{16,18},{18,... | collective-permute-start | bytes 1671176 | tf_op jit(solution)/shard_map/ppermute | solution.py:873
  231.7 24.2 %collective-permute-start.30 = (bf16[8,448,256]{2,1,0:T(8,128)(2,1)}, bf16[8,448,256]{2,1,0:T(8,128)(2,1)}, u32[]{:S(2)}, u32[]{:S(2)}) collective-permute-start(bf16[8,448,256]{2,1,0:T(8,128)(2,1)} %get-tuple-element.569), channel_id=1, source_target_pairs={{2,0},{6,2},{4,6},{12,4},{14,12},{10,14},{8,10},{16,8},{18,16},{22... | collective-permute-start | bytes 5505032 | tf_op jit(solution)/shard_map/ppermute | solution.py:767
  234.8 25.4 %collective-permute-start.31 = (bf16[8,448,256]{2,1,0:T(8,128)(2,1)}, bf16[8,448,256]{2,1,0:T(8,128)(2,1)}, u32[]{:S(2)}, u32[]{:S(2)}) collective-permute-start(bf16[8,448,256]{2,1,0:T(8,128)(2,1)} %get-tuple-element.570), channel_id=1, source_target_pairs={{0,2},{2,6},{6,4},{4,12},{12,14},{14,10},{10,8},{8,16},{16,18},{18... | collective-permute-start | bytes 5505032 | tf_op jit(solution)/shard_map/ppermute | solution.py:767
  (20 other events, 159.1 us)
